TPU v7x, 512 devices: a whole 4x8x8 slice. The times are simulated.
512 devices in a mesh: rep: 8 (over x, y_lo), shard: 64 (over z, y_hi, core).
Axes of the slice: x: 4, y: 8 (y_hi: 4, y_lo: 2; y = y_hi * 2 + y_lo), z: 8, core: 2. Of those that a mesh axis runs over, the one named last changes fastest.
Arguments:
- activations: bfloat16 [393216, 1024], P(('rep', 'shard')), may hold values from -24 to 24
- cotangents: bfloat16 [393216, 1024], P(('rep', 'shard')), may hold values from -0.0012207031 to 0.0012207031
- statistics: float32 [8, 512, 512], P('rep', 'shard'), may hold values from -22 to 22, as said below
- owner: int32 [8], replicated, may hold values from 0 to 7, each once
Outputs:
- new_statistics: float32 [8, 512, 512], P('rep', 'shard')
- direction: float32 [1024, 1024], P('shard')
Inputs may be any that keep to these rules, and one draw needn't show every extreme that they name: `owner`: each root is held by exactly one slot. `statistics`: each slot is symmetric and positive semidefinite.
All inputs are finite; a program needn't handle non-finite values.
Results may differ from a plain program's by a relative error of at most 0.0052.
Values may be sent and summed in bfloat16 or wider, within the bound.
No kernel may reach another device: no remote copies, remote signals or barrier semaphores. Data moves between devices by JAX's collectives and lax.ppermute only.
A program may use at most 64 MiB of HBM per device.

v0:
```python
import jax
import jax.numpy as jnp
from jax import lax
from jax.sharding import PartitionSpec as P

ITERS = 3


ema_decay = 0.9
highest = lax.Precision.HIGHEST


def grad_term_maker(activations, cotangents):

    def grad_term(first_row, count):
        return lax.dot_general(
            activations, cotangents, (((0,), (0,)), ((), ())), preferred_element_type=jnp.float32
        )

    return grad_term


def slot_product(left, right):
    return jnp.einsum(
        "sik,skj->sij", left, right, precision=highest, preferred_element_type=jnp.float32
    )


def lookup(table, index):
    positions = jnp.arange(table.shape[0], dtype=jnp.int32)
    return jnp.sum(jnp.where(positions == index, table, 0))


def body(activations, cotangents, statistics, owner):
    shard_count = lax.axis_size("shard")
    position = lax.axis_index("shard")
    replica = lax.axis_index("rep")
    grad_rows = activations.shape[1]
    grad_cols = cotangents.shape[1]
    out_rows = grad_rows // shard_count
    grad_term = grad_term_maker(activations, cotangents)
    summed = lax.psum(grad_term(0, grad_rows), ("rep", "shard"))
    gradient = summed.astype(jnp.bfloat16)
    slots_here, slot_rows, block_size = statistics.shape
    root_count = owner.shape[0]
    block_count = root_count // 2
    col_blocks = grad_cols // block_size
    root_ids = jnp.arange(root_count, dtype=jnp.int32)
    slot_ids = replica * slots_here + jnp.arange(slots_here, dtype=jnp.int32)
    held_roots = jnp.sum(
        jnp.where(owner[None, :] == slot_ids[:, None], root_ids[None, :], 0), axis=1
    )

    def lead_block(root_id):
        block_id = root_id % block_count
        grad_tile = lax.dynamic_slice(
            gradient,
            (block_id // col_blocks * block_size, block_id % col_blocks * block_size),
            (block_size, block_size),
        )
        return jnp.where(root_id < block_count, grad_tile, grad_tile.T)

    lead_blocks = jax.vmap(lead_block)(held_roots)
    first_row = position * slot_rows
    own_rows = lax.dynamic_slice_in_dim(lead_blocks, first_row, slot_rows, 1)
    gram_rows = jnp.einsum(
        "sik,sjk->sij", own_rows, lead_blocks, preferred_element_type=jnp.float32
    )
    updated = ema_decay * statistics + (1.0 - ema_decay) * gram_rows
    updated_whole = lax.all_gather(updated, "shard", axis=1, tiled=True)
    norm_scale = jnp.sqrt(jnp.sum(updated_whole * updated_whole, axis=(1, 2)) + 1e-06)
    state_whole = updated_whole / norm_scale[:, None, None]
    identity = jnp.eye(block_size, dtype=jnp.float32)
    current = state_whole
    for iteration in range(ITERS):
        factor = (5.0 * identity - current) * 0.25
        if iteration + 1 < ITERS:
            square = slot_product(factor, factor)
            fourth = slot_product(square, square)
            current = slot_product(fourth, current)
        if iteration == 0:
            root_whole = factor
        else:
            root_whole = slot_product(root_whole, factor)
    all_roots = lax.all_gather(root_whole.astype(jnp.bfloat16), "rep", axis=0, tiled=True)
    start_out = position * out_rows
    block_row = start_out // block_size
    offset = start_out % block_size
    pieces = []
    for column in range(col_blocks):
        block_id = block_row * col_blocks + column
        left_slot = lookup(owner, block_id)
        right_slot = lookup(owner, block_count + block_id)
        left_rows = lax.dynamic_slice(all_roots, (left_slot, offset, 0), (1, out_rows, block_size))[
            0
        ]
        right_root = lax.dynamic_index_in_dim(all_roots, right_slot, 0, keepdims=False)
        grad_tile = lax.dynamic_slice(
            gradient, (block_row * block_size, column * block_size), (block_size, block_size)
        )
        mixed_rows = jnp.dot(left_rows, grad_tile, preferred_element_type=jnp.float32).astype(
            jnp.bfloat16
        )
        pieces.append(jnp.dot(mixed_rows, right_root, preferred_element_type=jnp.float32))
    return (updated, jnp.concatenate(pieces, axis=1))


def solution(mesh):
    placed = (P(("rep", "shard"), None), P(("rep", "shard"), None), P("rep", "shard", None), P())
    return jax.shard_map(
        body,
        mesh=mesh,
        in_specs=placed,
        out_specs=(P("rep", "shard", None), P("shard", None)),
        check_vma=False,
    )
```

profile of v0, /device:TPU:1, one launch (start us, length us, event | category | flops | bytes accessed | tf_op | source)
XLA Modules:
  0.0 342.5 jit_solution(6746923872731827019)
XLA Ops:
  7.2 0.0 copy-start
  7.2 0.0 all-gather.4.cloned.1.call-start
  7.2 1.5 fusion.52
  11.4 0.0 copy-done
  11.4 5.2 %fusion.67 = f32[1024,1024]{1,0:T(8,128)} fusion(bf16[768,1024]{1,0:T(8,128)(2,1)S(1)} %copy-done, bf16[768,1024]{1,0:T(8,128)(2,1)} %param.5), kind=kOutput, calls=%fused_computation.75 | convolution fusion | flops 1610612736 | bytes 7340032 | tf_op jit(solution)/shard_map/dot_general | solution.py:16
  16.6 122.8 %all-reduce.1 = bf16[1024,1024]{1,0:T(8,128)(2,1)} all-reduce(f32[1024,1024]{1,0:T(8,128)} %fusion.67), channel_id=1, replica_groups=mesh['rep'=8,'shard'=64] {'rep','shard'}, use_global_device_ids=true, to_apply=%region_1.2 | all-reduce | flops 1048576 | bytes 6291456 | tf_op jit(solution)/shard_map/psum | solution.py:42
  139.4 0.0 copy-start.2
  139.4 1.1 dynamic-slice_bitcast_fusion
  140.5 0.2 copy.7
  140.7 1.2 bitcast_select_fusion
  141.9 0.0 copy-done.2
  141.9 0.9 fusion.4
  142.8 0.0 all-gather.4.cloned.1.call-update
  142.8 0.2 all-gather.6.cloned.1.call-start
  143.1 76.7 %all-gather.4.cloned.1.call-done = f32[1,512,512]{2,1,0:T(8,128)} async-done(((f32[1,8,512]{2,1,0:T(8,128)}), f32[1,512,512]{2,1,0:T(8,128)}) %all-gather.4.cloned.1.call-update) | async-done | bytes 1048592 | tf_op jit(solution)/shard_map/all_gather | solution.py:70
  219.7 2.1 multiply_reduce_fusion
  222.5 3.6 %fusion.10 = f32[512,512]{1,0:T(8,128)S(1)} fusion(f32[1,512,512]{2,1,0:T(8,128)} %all-gather.4.cloned.1.call-done, f32[]{:T(128)S(6)} %sqrt.4), kind=kOutput, calls=%fused_computation.16 | convolution fusion | flops 1611923456 | bytes 2097156 | tf_op jit(solution)/shard_map/sik,skj->sij/dot_general | solution.py:24
  226.1 0.0 copy-start.1
  226.1 1.8 fusion.68
  227.9 0.0 copy-done.1
  227.9 1.9 fusion.6
  229.8 1.9 fusion.12
  231.7 1.8 fusion.69
  233.6 1.9 fusion
  235.4 2.0 fusion.8
  237.4 2.7 convolution_convert_fusion
  240.1 0.0 all-gather.6.cloned.1.call-update
  247.7 84.2 %all-gather.6.cloned.1.call-done = bf16[4096,512]{1,0:T(8,128)(2,1)} async-done(((bf16[512,512]{1,0:T(8,128)(2,1)}), bf16[4096,512]{1,0:T(8,128)(2,1)}) %all-gather.6.cloned.1.call-update) | async-done | bytes 4194320 | tf_op jit(solution)/shard_map/all_gather | solution.py:85
  331.9 1.5 fusion.1
  333.5 1.5 fusion.2
  335.0 0.6 pad_maximum_fusion
Async XLA Ops:
  7.2 4.3 %copy-start = (bf16[768,1024]{1,0:T(8,128)(2,1)S(1)}, bf16[768,1024]{1,0:T(8,128)(2,1)}, u32[]{:S(2)}) copy-start(bf16[768,1024]{1,0:T(8,128)(2,1)} %param.4) | copy-start | bytes 4718596
  7.2 212.6 %all-gather.4.cloned.1.call-start = ((), (), s32[]{:S(2)}) async-start(), calls=%async_computation | async-start | bytes 1064960 | tf_op jit(solution)/shard_map/all_gather | solution.py:70
  139.4 2.5 copy-start.2
  142.8 189.1 %all-gather.6.cloned.1.call-start = ((), (), s32[]{:S(2)}) async-start(), calls=%async_computation.1 | async-start | bytes 4718592 | tf_op jit(solution)/shard_map/all_gather | solution.py:85
  226.1 1.9 copy-start.1
Sparse Core Ops, SparseCore 0:
  143.0 76.7 all-gather.3
  240.2 91.6 all-gather.5
where the time goes:
time: 343 us; the launch traced here: 342 us
  waiting for transfers between devices  161 us (47%)
  blocking collectives  123 us (36%)
  matrix products  26.7 us (8%)
  between operations  25 us (7%)
  other arithmetic  5.47 us (2%)
    psum x1, blocking collectives, body(): summed = lax.psum(grad_term(0, grad_rows), ('rep', 'shard'))  123 us
    all_gather x1, waiting for transfers between devices, body(): lax.all_gather(root_whole.astype(jnp.bfloat16), 'rep', axis=0, tiled=True)  84.2 us
    all_gather x1, waiting for transfers between devices, body(): updated_whole = lax.all_gather(updated, 'shard', axis=1, tiled=True)  76.7 us
    dot_general x8, matrix products, slot_product(): jnp.einsum('sik,skj->sij', left, right, precision=highest, preferred_elem...  17.6 us
  transfers between devices with their start and end apart: 2, of which 2 were waited for; matrix products, arithmetic and copies ran while one was open for 0% of the time, Pallas kernels for 0%

commit v1 on v0

v1 whole, which is shorter than its diff:
```python
import functools

import jax
import jax.numpy as jnp
from jax import lax
from jax.experimental import pallas as pl
from jax.experimental.pallas import tpu as pltpu
from jax.sharding import Mesh
from jax.sharding import PartitionSpec as P

ema_decay = 0.9
BLOCK = 512
HALF = BLOCK // 2
QUARTER = BLOCK // 4
LANES = 128
BLOCKS = 4
COLS = 2
REPS = 8
CHIPS = 32
CORES = 2
f32 = jnp.float32
bf16 = jnp.bfloat16
WHOLE = ("chip", "core")
VMEM_LIMIT = 48 * 1024 * 1024


def grad_kernel(owner_ref, core_ref, act_ref, cot_ref, mine_ref, other_ref):
    core = core_ref[0]
    for half in range(2):
        for row in range(2):
            start = row * BLOCK + half * HALF
            act = act_ref[:, start : start + HALF]
            for col in range(COLS):
                cot = cot_ref[:, col * BLOCK : (col + 1) * BLOCK]
                term = lax.dot_general(
                    act, cot, (((0,), (0,)), ((), ())), preferred_element_type=f32
                )
                slot = owner_ref[half * BLOCKS + row * COLS + col]
                low, high = term[:QUARTER], term[QUARTER:]
                mine = jnp.where(core == 0, low, high)
                other = jnp.where(core == 0, high, low)
                for lane in range(BLOCK // LANES):
                    part = slice(lane * LANES, (lane + 1) * LANES)
                    mine_ref[slot, lane] = mine[:, part]
                    other_ref[slot, lane] = other[:, part].astype(other_ref.dtype)


def split(value):
    high = value.astype(bf16)
    return high, (value - high.astype(f32)).astype(bf16)


def product(left, right):
    (lh, ll), (rh, rl) = left, right
    dot = functools.partial(jnp.dot, preferred_element_type=f32)
    return dot(lh, rh) + (dot(lh, rl) + dot(ll, rh))


def root_kernel(place_ref, stats_ref, tiles_ref, updated_ref, root_ref, mixed_ref, grad, full):
    for lane in range(BLOCK // LANES):
        for group in range(QUARTER // 16):
            for core in range(CORES):
                for half in range(2):
                    row = half * HALF + core * QUARTER + group * 16
                    source = (lane * (QUARTER // 16) + group) * CORES + core
                    grad[row : row + 16, lane * LANES : (lane + 1) * LANES] = tiles_ref[source, half]

    @pl.when(place_ref[0] == 1)
    def _left():
        full[...] = lax.dot_general(
            grad[...], grad[...], (((1,), (1,)), ((), ())), preferred_element_type=f32
        )

    @pl.when(place_ref[0] == 0)
    def _right():
        full[...] = lax.dot_general(
            grad[...], grad[...], (((0,), (0,)), ((), ())), preferred_element_type=f32
        )

    updated = ema_decay * stats_ref[...] + (1.0 - ema_decay) * full[...]
    full[...] = updated
    updated_ref[...] = full[pl.ds(pl.multiple_of(place_ref[1], 8), 8), :]
    scale = jnp.sqrt(jnp.sum(updated * updated, keepdims=True) + 1e-06)
    state = updated / scale
    rows = lax.broadcasted_iota(jnp.int32, (BLOCK, BLOCK), 0)
    cols = lax.broadcasted_iota(jnp.int32, (BLOCK, BLOCK), 1)
    five = jnp.where(rows == cols, 1.25, 0.0).astype(f32)

    def step(current):
        factor = split(five - 0.25 * current)
        square = split(product(factor, factor))
        fourth = split(product(square, square))
        return factor, product(fourth, split(current))

    first, state = step(state)
    second, state = step(state)
    third = split(five - 0.25 * state)
    root = product(split(product(first, second)), third)
    root_ref[...] = root.astype(bf16)
    own = root_ref[pl.ds(pl.multiple_of(place_ref[2], 16), 16), :]
    mixed_ref[...] = jnp.dot(own, grad[...], preferred_element_type=f32).astype(bf16)


def exchange(value, axes):
    return lax.all_to_all(value, axes, split_axis=0, concat_axis=0, tiled=True)


def spread(value, axes, count):
    return exchange(jnp.broadcast_to(value[None], (count, *value.shape)), axes)


def pick(table, index):
    return lax.dynamic_index_in_dim(table, index, 0, keepdims=False)


def body(activations, cotangents, statistics, owner):
    replica = lax.axis_index("rep")
    chip = lax.axis_index("chip")
    core = lax.axis_index("core")
    position = chip * CORES + core
    vmem = pl.BlockSpec(memory_space=pltpu.VMEM)
    smem = pl.BlockSpec(memory_space=pltpu.SMEM)
    params = pltpu.CompilerParams(vmem_limit_bytes=VMEM_LIMIT)

    stats = lax.all_gather(statistics[0], WHOLE, axis=0, tiled=True)

    quarter = (REPS, BLOCK // LANES, QUARTER, LANES)
    mine, other = pl.pallas_call(
        grad_kernel,
        out_shape=(jax.ShapeDtypeStruct(quarter, f32), jax.ShapeDtypeStruct(quarter, f32)),
        in_specs=[smem, smem, vmem, vmem],
        out_specs=(vmem, vmem),
        compiler_params=params,
        name="grad_term",
    )(owner, core.reshape(1), activations, cotangents)
    other = lax.ppermute(other, "core", [(0, 1), (1, 0)])
    by_slot = exchange((mine + other).astype(bf16), "rep")
    summed = jnp.sum(by_slot.astype(f32), axis=0).reshape(CHIPS, 16, LANES)
    gradient = jnp.sum(exchange(summed, "chip"), axis=0).astype(bf16)

    roots = jnp.arange(2 * BLOCKS, dtype=jnp.int32)
    held = jnp.sum(jnp.where(owner == replica, roots, 0))
    block = held % BLOCKS
    left_slot, right_slot = pick(owner, block), pick(owner, block + BLOCKS)
    all_slots = spread(gradient, "rep", REPS)
    both = jnp.stack([pick(all_slots, left_slot), pick(all_slots, right_slot)])
    tiles = spread(both, WHOLE, CHIPS * CORES)

    out_rows = 16
    place = jnp.stack(
        [
            (held < BLOCKS).astype(jnp.int32),
            position * 8,
            position % (BLOCK // out_rows) * out_rows,
        ]
    )
    updated, root, mixed = pl.pallas_call(
        root_kernel,
        out_shape=(
            jax.ShapeDtypeStruct((8, BLOCK), f32),
            jax.ShapeDtypeStruct((BLOCK, BLOCK), bf16),
            jax.ShapeDtypeStruct((out_rows, BLOCK), bf16),
        ),
        in_specs=[smem, vmem, vmem],
        out_specs=(vmem, vmem, vmem),
        scratch_shapes=[pltpu.VMEM((BLOCK, BLOCK), bf16), pltpu.VMEM((BLOCK, BLOCK), f32)],
        compiler_params=params,
        name="root",
    )(place, stats, tiles)

    left_rows = pick(spread(mixed, "rep", REPS), left_slot)
    piece = jnp.dot(left_rows, root, preferred_element_type=f32)
    pieces = spread(piece, "rep", REPS)
    first = position // (BLOCK // out_rows) * COLS + BLOCKS
    direction = jnp.concatenate(
        [pick(pieces, pick(owner, first + col)) for col in range(COLS)], axis=1
    )
    return updated[None], direction


def solution(mesh):
    fine = Mesh(mesh.devices.reshape(REPS, CHIPS, CORES), ("rep", "chip", "core"))
    every = ("rep", "chip", "core")
    return jax.shard_map(
        body,
        mesh=fine,
        in_specs=(P(every, None), P(every, None), P("rep", WHOLE, None), P()),
        out_specs=(P("rep", WHOLE, None), P(WHOLE, None)),
        check_vma=False,
    )
```

time: 343 us -> 173 us (0.50)
  blocking collectives: 123 us -> 18 us
  waiting for transfers between devices: 161 us -> 66.2 us
  starting transfers between devices: 0.26 us -> 38.4 us
  matrix products: 26.7 us -> 0.17 us
  Pallas kernels: 0 us -> 13.1 us
  local copies, waits for them, and re-layouts: 1.32 us -> 7.66 us
    all_gather x2 -> x1, waiting for transfers between devices: 161 us -> 32.6 us  [body(): stats = lax.all_gather(statistics[0], WHOLE, axis=0, tiled=True)]
    psum x1 -> x0, blocking collectives: 123 us -> none  [body(): summed = lax.psum(grad_term(0, grad_rows), ('rep', 'shard'))]
    all_to_all x0 -> x5, starting transfers between devices: none -> 29.6 us  [exchange(): return lax.all_to_all(value, axes, split_axis=0, concat_axis=0, tiled=True)]
    all_to_all x0 -> x5, waiting for transfers between devices: none -> 28.9 us  [exchange(): return lax.all_to_all(value, axes, split_axis=0, concat_axis=0, tiled=True)]
    dot_general x12 -> x1, matrix products: 26.7 us -> 0.17 us  [body(): piece = jnp.dot(left_rows, root, preferred_element_type=f32)]
    all_to_all x0 -> x1, blocking collectives: none -> 18 us  [exchange(): return lax.all_to_all(value, axes, split_axis=0, concat_axis=0, tiled=True)]
    pallas_call x0 -> x2, Pallas kernels: none -> 13.1 us  [the longest x1 9.33 us: body(): pl.pallas_call(root_kernel, out_shape=(jax.ShapeDtypeStruct((8, BLOCK), f...]
    ppermute x0 -> x1, starting transfers between devices: none -> 8.77 us  [body(): other = lax.ppermute(other, 'core', [(0, 1), (1, 0)])]
  transfers between devices with their start and end apart: 2 -> 7, of which waited for: 2 -> 5; matrix products, arithmetic and copies ran while one was open for 0% -> 2% of each run, Pallas kernels for 0% -> 0%
where the time goes in v1:
time: 173 us; the launch traced here: 172 us
  waiting for transfers between devices  66.2 us (38%)
  starting transfers between devices  38.4 us (22%)
  between operations  24.6 us (14%)
  blocking collectives  18 us (10%)
  Pallas kernels  13.1 us (8%)
  local copies, waits for them, and re-layouts  7.66 us (4%)
  other arithmetic  3.64 us (2%)
    all_gather x1, waiting for transfers between devices, body(): stats = lax.all_gather(statistics[0], WHOLE, axis=0, tiled=True)  32.6 us
    all_to_all x5, starting transfers between devices, exchange(): return lax.all_to_all(value, axes, split_axis=0, concat_axis=0, tiled=True)  29.6 us
    all_to_all x5, waiting for transfers between devices, exchange(): return lax.all_to_all(value, axes, split_axis=0, concat_axis=0, tiled=True)  28.9 us
    all_to_all x1, blocking collectives, exchange(): return lax.all_to_all(value, axes, split_axis=0, concat_axis=0, tiled=True)  18 us
    pallas_call x1, Pallas kernels, body(): pl.pallas_call(root_kernel, out_shape=(jax.ShapeDtypeStruct((8, BLOCK), f...  9.33 us
    ppermute x1, starting transfers between devices, body(): other = lax.ppermute(other, 'core', [(0, 1), (1, 0)])  8.77 us
    unnamed x10, local copies, waits for them, and re-layouts  4.69 us
    ppermute x1, waiting for transfers between devices, body(): other = lax.ppermute(other, 'core', [(0, 1), (1, 0)])  3.97 us
  transfers between devices with their start and end apart: 7, of which 5 were waited for; matrix products, arithmetic and copies ran while one was open for 2% of the time, Pallas kernels for 0%

profile of v1, /device:TPU:1, one launch (start us, length us, event | category | flops | bytes accessed | tf_op | source)
XLA Modules:
  0.0 171.8 jit_solution(274105026623074041)
XLA Ops:
  7.2 1.4 copy-done
  8.6 1.4 copy-done.1
  10.0 0.7 copy-done.3
  10.6 3.8 %grad_term.1 = (f32[8,4,128,128]{3,2,1,0:T(8,128)S(1)}, f32[8,4,128,128]{3,2,1,0:T(8,128)}) custom-call(s32[8]{0:T(128)S(1)} %copy-done.3, s32[1]{0:T(128)} %bitcast.4.core_ref, bf16[768,1024]{1,0:T(8,128)(2,1)S(1)} %copy-done, bf16[768,1024]{1,0:T(8,128)(2,1)S(1)} %copy-done.1), custom_call_target="tpu_custom_call" | custom-call | tf_op jit(solution)/shard_map/grad_term/pallas_call | solution.py:128
  14.4 8.8 %collective-permute-start = (f32[8,4,128,128]{3,2,1,0:T(8,128)}, f32[8,4,128,128]{3,2,1,0:T(8,128)S(1)}, u32[]{:S(2)}, u32[]{:S(2)}) collective-permute-start(f32[8,4,128,128]{3,2,1,0:T(8,128)} %get-tuple-element.8), channel_id=1, source_target_pairs={{0,1},{1,0},{2,3},{3,2},{4,5},{5,4},{6,7},{7,6},{8,9},{9,8},{10,11... | collective-permute-start | bytes 6291464 | tf_op jit(solution)/shard_map/ppermute | solution.py:136
  23.2 4.0 %collective-permute-done = f32[8,4,128,128]{3,2,1,0:T(8,128)S(1)} collective-permute-done((f32[8,4,128,128]{3,2,1,0:T(8,128)}, f32[8,4,128,128]{3,2,1,0:T(8,128)S(1)}, u32[]{:S(2)}, u32[]{:S(2)}) %collective-permute-start) | collective-permute-done | bytes 2097184 | tf_op jit(solution)/shard_map/ppermute | solution.py:136
  27.2 1.3 add_convert_fusion
  28.5 3.7 %all-to-all-start = ((bf16[8,4,128,128]{3,2,1,0:T(8,128)(2,1)}), bf16[8,4,128,128]{3,2,1,0:T(8,128)(2,1)S(1)}, u32[]{:S(2)}, u32[]{:S(2)}) async-start(bf16[8,4,128,128]{3,2,1,0:T(8,128)(2,1)} %add_convert_fusion), calls=%async_computation | async-start | bytes 2097152 | tf_op jit(solution)/shard_map/all_to_all | solution.py:105
  32.2 0.0 all-gather.3.cloned.1.call-start
  32.2 0.7 all-gather.3.cloned.1.call-update
  32.9 14.7 %all-to-all-done = bf16[8,4,128,128]{3,2,1,0:T(8,128)(2,1)S(1)} async-done(((bf16[8,4,128,128]{3,2,1,0:T(8,128)(2,1)}), bf16[8,4,128,128]{3,2,1,0:T(8,128)(2,1)S(1)}, u32[]{:S(2)}, u32[]{:S(2)}) %all-to-all-start) | async-done | bytes 1048608 | tf_op jit(solution)/shard_map/all_to_all | solution.py:105
  47.6 0.9 convert_reduce_fusion
  48.5 10.6 %all-to-all-start.1 = ((f32[32,16,128]{2,1,0:T(8,128)}), f32[32,16,128]{2,1,0:T(8,128)S(1)}, u32[]{:S(2)}, u32[]{:S(2)}) async-start(f32[32,16,128]{2,1,0:T(8,128)} %bitcast.5), calls=%async_computation.1 | async-start | bytes 524288 | tf_op jit(solution)/shard_map/all_to_all | solution.py:105
  59.1 11.8 %all-to-all-done.1 = f32[32,16,128]{2,1,0:T(8,128)S(1)} async-done(((f32[32,16,128]{2,1,0:T(8,128)}), f32[32,16,128]{2,1,0:T(8,128)S(1)}, u32[]{:S(2)}, u32[]{:S(2)}) %all-to-all-start.1) | async-done | bytes 262176 | tf_op jit(solution)/shard_map/all_to_all | solution.py:105
  71.0 0.6 broadcast_in_dim.15
  71.6 4.4 %all-to-all-start.2 = ((bf16[8,16,128]{2,1,0:T(8,128)(2,1)}), bf16[8,16,128]{2,1,0:T(8,128)(2,1)S(1)}, u32[]{:S(2)}, u32[]{:S(2)}) async-start(bf16[8,16,128]{2,1,0:T(8,128)(2,1)} %broadcast_in_dim.15), calls=%async_computation.2 | async-start | bytes 65536 | tf_op jit(solution)/shard_map/all_to_all | solution.py:105
  76.0 0.7 fusion.4
  78.9 0.7 fusion.5
  83.4 0.0 all-to-all-done.2
  83.4 0.9 broadcast_in_dim.16
  84.3 7.5 %all-to-all-start.3 = ((bf16[64,2,16,128]{3,2,1,0:T(8,128)(2,1)}), bf16[64,2,16,128]{3,2,1,0:T(8,128)(2,1)S(1)}, u32[]{:S(2)}, u32[]{:S(2)}) async-start(bf16[64,2,16,128]{3,2,1,0:T(8,128)(2,1)} %broadcast_in_dim.16), calls=%async_computation.3 | async-start | bytes 1048576 | tf_op jit(solution)/shard_map/all_to_all | solution.py:105
  92.5 0.1 pad_add_fusion.place_ref
  92.5 32.6 %all-gather.3.cloned.1.call-done = f32[1,512,512]{2,1,0:T(8,128)} async-done(((f32[1,8,512]{2,1,0:T(8,128)}), f32[1,512,512]{2,1,0:T(8,128)}) %all-gather.3.cloned.1.call-update) | async-done | bytes 1048592 | tf_op jit(solution)/shard_map/all_gather | solution.py:125
  125.2 0.0 all-to-all-done.3.tiles_ref
  125.2 1.2 copy-done.2
  126.4 9.3 %root.1 = (f32[8,512]{1,0:T(8,128)}, bf16[512,512]{1,0:T(8,128)(2,1)S(1)}, bf16[16,512]{1,0:T(8,128)(2,1)S(1)}) custom-call(s32[3]{0:T(128)S(1)} %pad_add_fusion.place_ref, f32[512,512]{1,0:T(8,128)S(1)} %bitcast.19, bf16[64,2,16,128]{3,2,1,0:T(8,128)(2,1)S(1)} %all-to-all-done.3.tiles_ref), custom_call_target="tpu_custom_call" | custom-call | tf_op jit(solution)/shard_map/root/pallas_call | solution.py:157
  135.7 18.0 %all_to_all.30 = bf16[8,16,512]{2,1,0:T(8,128)(2,1)S(1)} all-to-all(bf16[8,16,512]{2,1,0:T(8,128)(2,1)S(1)} %broadcast_in_dim.18), channel_id=1, replica_groups=mesh['rep'=8,'chip'=32,'core'=2] {'rep'}, dimensions={0} | all-to-all | bytes 262144 | tf_op jit(solution)/shard_map/all_to_all | solution.py:105
  153.8 0.2 fusion
  153.9 0.7 broadcast_in_dim.36
  154.7 3.4 %all-to-all-start.5 = ((f32[8,16,512]{2,1,0:T(8,128)}), f32[8,16,512]{2,1,0:T(8,128)S(1)}, u32[]{:S(2)}, u32[]{:S(2)}) async-start(f32[8,16,512]{2,1,0:T(8,128)} %broadcast_in_dim.36), calls=%async_computation.5 | async-start | bytes 524288 | tf_op jit(solution)/shard_map/all_to_all | solution.py:105
  161.9 2.4 %all-to-all-done.5 = f32[8,16,512]{2,1,0:T(8,128)S(1)} async-done(((f32[8,16,512]{2,1,0:T(8,128)}), f32[8,16,512]{2,1,0:T(8,128)S(1)}, u32[]{:S(2)}, u32[]{:S(2)}) %all-to-all-start.5) | async-done | bytes 262176 | tf_op jit(solution)/shard_map/all_to_all | solution.py:105
  164.3 0.6 pad_maximum_fusion
  (11 shorter events, 0.1 us)
Async XLA Ops:
  7.2 1.4 copy-start
  8.6 1.4 copy-start.1
  10.0 0.7 copy-start.3
  14.4 12.8 %collective-permute-start = (f32[8,4,128,128]{3,2,1,0:T(8,128)}, f32[8,4,128,128]{3,2,1,0:T(8,128)S(1)}, u32[]{:S(2)}, u32[]{:S(2)}) collective-permute-start(f32[8,4,128,128]{3,2,1,0:T(8,128)} %get-tuple-element.8), channel_id=1, source_target_pairs={{0,1},{1,0},{2,3},{3,2},{4,5},{5,4},{6,7},{7,6},{8,9},{9,8},{10,11... | collective-permute-start | bytes 6291464 | tf_op jit(solution)/shard_map/ppermute | solution.py:136
  28.5 47.5 %copy-start.4 = (s32[8]{0:T(128)S(1)}, s32[8]{0:T(128)}, u32[]{:S(2)}) copy-start(s32[8]{0:T(128)} %owner_ref.1) | copy-start | bytes 100
  28.5 19.1 %all-to-all-start = ((bf16[8,4,128,128]{3,2,1,0:T(8,128)(2,1)}), bf16[8,4,128,128]{3,2,1,0:T(8,128)(2,1)S(1)}, u32[]{:S(2)}, u32[]{:S(2)}) async-start(bf16[8,4,128,128]{3,2,1,0:T(8,128)(2,1)} %add_convert_fusion), calls=%async_computation | async-start | bytes 2097152 | tf_op jit(solution)/shard_map/all_to_all | solution.py:105
  32.2 93.0 %all-gather.3.cloned.1.call-start = ((), (), s32[]{:S(2)}) async-start(), calls=%async_computation.6 | async-start | bytes 1064960 | tf_op jit(solution)/shard_map/all_gather | solution.py:125
  48.5 22.5 %all-to-all-start.1 = ((f32[32,16,128]{2,1,0:T(8,128)}), f32[32,16,128]{2,1,0:T(8,128)S(1)}, u32[]{:S(2)}, u32[]{:S(2)}) async-start(f32[32,16,128]{2,1,0:T(8,128)} %bitcast.5), calls=%async_computation.1 | async-start | bytes 524288 | tf_op jit(solution)/shard_map/all_to_all | solution.py:105
  71.6 11.8 %all-to-all-start.2 = ((bf16[8,16,128]{2,1,0:T(8,128)(2,1)}), bf16[8,16,128]{2,1,0:T(8,128)(2,1)S(1)}, u32[]{:S(2)}, u32[]{:S(2)}) async-start(bf16[8,16,128]{2,1,0:T(8,128)(2,1)} %broadcast_in_dim.15), calls=%async_computation.2 | async-start | bytes 65536 | tf_op jit(solution)/shard_map/all_to_all | solution.py:105
  84.3 40.9 %all-to-all-start.3 = ((bf16[64,2,16,128]{3,2,1,0:T(8,128)(2,1)}), bf16[64,2,16,128]{3,2,1,0:T(8,128)(2,1)S(1)}, u32[]{:S(2)}, u32[]{:S(2)}) async-start(bf16[64,2,16,128]{3,2,1,0:T(8,128)(2,1)} %broadcast_in_dim.16), calls=%async_computation.3 | async-start | bytes 1048576 | tf_op jit(solution)/shard_map/all_to_all | solution.py:105
  125.2 1.2 copy-start.2
  154.7 9.6 %all-to-all-start.5 = ((f32[8,16,512]{2,1,0:T(8,128)}), f32[8,16,512]{2,1,0:T(8,128)S(1)}, u32[]{:S(2)}, u32[]{:S(2)}) async-start(f32[8,16,512]{2,1,0:T(8,128)} %broadcast_in_dim.36), calls=%async_computation.5 | async-start | bytes 524288 | tf_op jit(solution)/shard_map/all_to_all | solution.py:105
Sparse Core Ops, SparseCore 0:
  36.4 88.7 all-gather.2

commit v2 on v1

v2 whole, which is shorter than its diff:
```python
import jax
import jax.numpy as jnp
from jax import lax
from jax.experimental import pallas as pl
from jax.experimental.pallas import tpu as pltpu
from jax.sharding import Mesh
from jax.sharding import PartitionSpec as P

ema_decay = 0.9
BLOCK = 512
HALF = BLOCK // 2
QUARTER = BLOCK // 4
LANES = 128
BLOCKS = 4
ROOTS = 8
COLS = 2
REPS = 8
CHIPS = 32
CORES = 2
SHARDS = CHIPS * CORES
OUT_ROWS = 16
STATS = 32
f32 = jnp.float32
bf16 = jnp.bfloat16
WHOLE = ("chip", "core")
VMEM_LIMIT = 40 * 1024 * 1024
GRAD_LIMIT = 60 * 1024 * 1024


def slots_of(device, owner_ref):
    replica = device // SHARDS
    held = jnp.int32(0)
    for root in range(1, ROOTS):
        held = jnp.where(owner_ref[root] == replica, root, held)
    block = held % BLOCKS
    return held, owner_ref[block], owner_ref[block + BLOCKS]


def grad_kernel(device_ref, owner_ref, act_hbm, cot_hbm, mine_ref, other_ref, act_ref, cot_ref, sems):
    core = device_ref[0] % CORES

    def fetch(source, target, number, sem):
        columns = pl.ds(number * BLOCK, BLOCK)
        return pltpu.make_async_copy(source.at[:, columns], target.at[:, columns], sems.at[sem])

    act_copies = [fetch(act_hbm, act_ref, row, row) for row in range(2)]
    cot_copies = [fetch(cot_hbm, cot_ref, col, 2 + col) for col in range(2)]
    for copy in (act_copies[0], cot_copies[0], cot_copies[1], act_copies[1]):
        copy.start()
    for row in range(2):
        act_copies[row].wait()
        for col in range(COLS):
            if row == 0:
                cot_copies[col].wait()
            cot = cot_ref[:, col * BLOCK : (col + 1) * BLOCK]
            for half in range(2):
                start = row * BLOCK + half * HALF
                term = lax.dot_general(
                    act_ref[:, start : start + HALF],
                    cot,
                    (((0,), (0,)), ((), ())),
                    preferred_element_type=f32,
                )
                slot = owner_ref[half * BLOCKS + row * COLS + col]
                low, high = term[:QUARTER], term[QUARTER:]
                mine = jnp.where(core == 0, low, high)
                other = jnp.where(core == 0, high, low)
                for lane in range(BLOCK // LANES):
                    part = slice(lane * LANES, (lane + 1) * LANES)
                    mine_ref[slot, lane] = mine[:, part]
                    other_ref[slot, lane] = other[:, part]


def pack_kernel(mine_ref, other_ref, own_ref, out_ref):
    for slot in range(REPS):
        for lane in range(BLOCK // LANES):
            place = slice(lane * QUARTER, (lane + 1) * QUARTER)
            out_ref[slot, place] = (mine_ref[slot, lane] + other_ref[slot, lane]).astype(bf16)
    parts = [own_ref[:, lane * LANES : (lane + 1) * LANES] for lane in range(BLOCK // LANES)]
    packed = jnp.concatenate(parts, axis=0).astype(bf16)
    for slot in range(REPS):
        out_ref[slot, BLOCK : BLOCK + STATS] = packed


def reduce_kernel(device_ref, owner_ref, terms_ref, out_ref):
    _, left, right = slots_of(device_ref[0], owner_ref)
    stats = [terms_ref[slot, BLOCK : BLOCK + STATS] for slot in (left, right)]
    for chip in range(CHIPS):
        part = slice(chip * 16, chip * 16 + 16)
        total = terms_ref[0, part].astype(f32)
        for slot in range(1, REPS):
            total += terms_ref[slot, part].astype(f32)
        high, low = split(total)
        out_ref[chip, 0:16] = high
        out_ref[chip, 16:32] = low
        for side in range(2):
            out_ref[chip, 32 + side * STATS : 32 + (side + 1) * STATS] = stats[side]


def total_kernel(parts_ref, out_ref):
    total = jnp.zeros((16, LANES), f32)
    for chip in range(CHIPS):
        total += parts_ref[chip, 0:16].astype(f32) + parts_ref[chip, 16:32].astype(f32)
    gradient = total.astype(bf16)
    for slot in range(REPS):
        out_ref[slot] = gradient


def pair_kernel(device_ref, owner_ref, slots_ref, out_ref):
    _, left, right = slots_of(device_ref[0], owner_ref)
    first, second = slots_ref[left], slots_ref[right]
    for receiver in range(SHARDS):
        out_ref[receiver, 0] = first
        out_ref[receiver, 1] = second


def split(value):
    high = value.astype(bf16)
    return high, (value - high.astype(f32)).astype(bf16)


def product(left, right):
    return jnp.dot(left.astype(bf16), right.astype(bf16), preferred_element_type=f32)


def newton(stats, gram):
    updated = ema_decay * stats + (1.0 - ema_decay) * gram
    scale = jnp.sqrt(jnp.sum(updated * updated, keepdims=True) + 1e-06)

    def step(state):
        low = 2.0 * state - product(state, state)
        high = 2.0 * low - product(low, low)
        return 1.25**4 * (state - product(high, state))

    first = updated * (0.2 / scale)
    second = step(first)
    return first, second, step(second)


def root_rows(first, second, third, diagonal):
    own_first, own_second, own_third = first
    both = own_first + own_second - product(own_first, second)
    return 1.25**3 * (diagonal - (both + own_third - product(both, third)))


def root_kernel(
    device_ref, owner_ref, own_ref, here_ref, there_ref, tiles_ref, updated_ref, piece_ref, grad, stats, gram, rows
):
    device = device_ref[0]
    held, _, _ = slots_of(device, owner_ref)
    position = device % SHARDS
    core = device % CORES
    for lane in range(BLOCK // LANES):
        for group in range(QUARTER // 16):
            for side in range(CORES):
                for half in range(2):
                    row = half * HALF + side * QUARTER + group * 16
                    source = (lane * (QUARTER // 16) + group) * CORES + side
                    grad[row : row + 16, lane * LANES : (lane + 1) * LANES] = tiles_ref[source, half]
    for chip in range(CHIPS):
        for part, at in ((here_ref, core), (there_ref, 1 - core)):
            place = pl.ds(pl.multiple_of((chip * CORES + at) * 8, 8), 8)
            for side in range(2):
                value = part[chip, 32 + side * STATS : 32 + (side + 1) * STATS].astype(f32)
                for lane in range(BLOCK // LANES):
                    stats[side, place, lane * LANES : (lane + 1) * LANES] = value[lane * 8 : lane * 8 + 8]

    gram[0] = lax.dot_general(
        grad[...], grad[...], (((1,), (1,)), ((), ())), preferred_element_type=f32
    )
    gram[1] = lax.dot_general(
        grad[...], grad[...], (((0,), (0,)), ((), ())), preferred_element_type=f32
    )
    own_gram = gram[held // BLOCKS, pl.ds(pl.multiple_of(position * 8, 8), 8), :]
    updated_ref[...] = ema_decay * own_ref[...] + (1.0 - ema_decay) * own_gram

    start = pl.multiple_of(position % (BLOCK // OUT_ROWS) * OUT_ROWS, OUT_ROWS)
    left = newton(stats[0], gram[0])
    for number in range(3):
        rows[number] = left[number]
    own = tuple(rows[number, pl.ds(start, OUT_ROWS), :] for number in range(3))
    shape = (OUT_ROWS, BLOCK)
    diagonal = lax.broadcasted_iota(jnp.int32, shape, 0) + start == lax.broadcasted_iota(jnp.int32, shape, 1)
    left_rows = root_rows(own, left[1], left[2], jnp.where(diagonal, 1.0, 0.0)).astype(bf16)
    mixed = jnp.dot(left_rows, grad[...], preferred_element_type=f32).astype(bf16)

    right = newton(stats[1], gram[1])
    shape = (BLOCK, BLOCK)
    diagonal = lax.broadcasted_iota(jnp.int32, shape, 0) == lax.broadcasted_iota(jnp.int32, shape, 1)
    right_root = root_rows(right, right[1], right[2], jnp.where(diagonal, 1.0, 0.0)).astype(bf16)
    piece = jnp.dot(mixed, right_root, preferred_element_type=f32)
    for receiver in range(REPS):
        piece_ref[receiver] = piece


def join_kernel(device_ref, owner_ref, pieces_ref, out_ref):
    first = device_ref[0] % SHARDS // (BLOCK // OUT_ROWS) * COLS + BLOCKS
    for col in range(COLS):
        out_ref[:, col * BLOCK : (col + 1) * BLOCK] = pieces_ref[owner_ref[first + col]]


def exchange(value, axes):
    return lax.all_to_all(value, axes, split_axis=0, concat_axis=0, tiled=True)


def call(kernel, name, outs, arrays, scratch=(), limit=VMEM_LIMIT):
    vmem = pl.BlockSpec(memory_space=pltpu.VMEM)
    smem = pl.BlockSpec(memory_space=pltpu.SMEM)
    rest = pl.BlockSpec(memory_space=pl.ANY) if limit > VMEM_LIMIT else vmem
    return pl.pallas_call(
        kernel,
        out_shape=outs,
        in_specs=[smem if array.ndim == 1 else rest for array in arrays],
        out_specs=tuple(vmem for _ in outs) if isinstance(outs, tuple) else vmem,
        scratch_shapes=list(scratch),
        compiler_params=pltpu.CompilerParams(vmem_limit_bytes=limit),
        name=name,
    )(*arrays)


def swap_cores(value):
    return lax.ppermute(value, "core", [(0, 1), (1, 0)])


def body(activations, cotangents, statistics, owner):
    device = lax.axis_index(("rep", "chip", "core")).astype(jnp.int32).reshape(1)
    array = jax.ShapeDtypeStruct
    own = statistics[0]

    quarter = array((REPS, BLOCK // LANES, QUARTER, LANES), f32)
    mine, other = call(
        grad_kernel,
        "grad_term",
        (quarter, quarter),
        (device, owner, activations, cotangents),
        scratch=[
            pltpu.VMEM(activations.shape, bf16),
            pltpu.VMEM(cotangents.shape, bf16),
            pltpu.SemaphoreType.DMA((4,)),
        ],
        limit=GRAD_LIMIT,
    )
    packed = call(
        pack_kernel,
        "pack",
        array((REPS, BLOCK + STATS, LANES), bf16),
        (mine, swap_cores(other), own),
    )
    terms = exchange(packed, "rep")
    reduced = call(
        reduce_kernel,
        "reduce",
        array((CHIPS, 32 + 2 * STATS, LANES), bf16),
        (device, owner, terms),
    )
    here = exchange(reduced, "chip")
    there = swap_cores(here)
    gradient = call(total_kernel, "total", array((REPS, 16, LANES), bf16), (here,))
    both = call(
        pair_kernel,
        "pair",
        array((SHARDS, 2, 16, LANES), bf16),
        (device, owner, exchange(gradient, "rep")),
    )
    tiles = exchange(both, WHOLE)

    updated, pieces = call(
        root_kernel,
        "root",
        (array((8, BLOCK), f32), array((REPS, OUT_ROWS, BLOCK), f32)),
        (device, owner, own, here, there, tiles),
        scratch=[
            pltpu.VMEM((BLOCK, BLOCK), bf16),
            pltpu.VMEM((2, BLOCK, BLOCK), f32),
            pltpu.VMEM((2, BLOCK, BLOCK), f32),
            pltpu.VMEM((3, BLOCK, BLOCK), f32),
        ],
    )
    direction = call(
        join_kernel,
        "join",
        array((OUT_ROWS, COLS * BLOCK), f32),
        (device, owner, exchange(pieces, "rep")),
    )
    return updated[None], direction


def solution(mesh):
    fine = Mesh(mesh.devices.reshape(REPS, CHIPS, CORES), ("rep", "chip", "core"))
    every = ("rep", "chip", "core")
    return jax.shard_map(
        body,
        mesh=fine,
        in_specs=(P(every, None), P(every, None), P("rep", WHOLE, None), P()),
        out_specs=(P("rep", WHOLE, None), P(WHOLE, None)),
        check_vma=False,
    )
```

time: 173 us -> 135 us (0.78)
  blocking collectives: 18 us -> 74.3 us
  waiting for transfers between devices: 66.2 us -> 22.5 us
  between operations: 24.6 us -> 0.71 us
  starting transfers between devices: 38.4 us -> 18.8 us
  local copies, waits for them, and re-layouts: 7.66 us -> 1.6 us
  Pallas kernels: 13.1 us -> 16.9 us
  other arithmetic: 3.64 us -> 0 us
    all_to_all x1 -> x4, blocking collectives: 18 us -> 74.3 us  [exchange(): return lax.all_to_all(value, axes, split_axis=0, concat_axis=0, tiled=True)]
    all_gather x1 -> x0, waiting for transfers between devices: 32.6 us -> none  [body(): stats = lax.all_gather(statistics[0], WHOLE, axis=0, tiled=True)]
    all_to_all x5 -> x1, starting transfers between devices: 29.6 us -> 7.64 us  [exchange(): return lax.all_to_all(value, axes, split_axis=0, concat_axis=0, tiled=True)]
    all_to_all x5 -> x1, waiting for transfers between devices: 28.9 us -> 16.6 us  [exchange(): return lax.all_to_all(value, axes, split_axis=0, concat_axis=0, tiled=True)]
    pallas_call x2 -> x7, Pallas kernels: 13.1 us -> 16.9 us  [call(): pl.pallas_call(kernel, out_shape=outs, in_specs=[smem if array.ndim == 1...]
    unnamed x10 -> x6, local copies, waits for them, and re-layouts: 4.69 us -> 1.6 us
    ppermute x1 -> x2, starting transfers between devices: 8.77 us -> 11.2 us  [swap_cores(): return lax.ppermute(value, 'core', [(0, 1), (1, 0)])]
    broadcast_in_dim x4 -> x0, local copies, waits for them, and re-layouts: 2.27 us -> none  [spread(): return exchange(jnp.broadcast_to(value[None], (count, *value.shape)), axes)]
  transfers between devices with their start and end apart: 7 -> 3, of which waited for: 5 -> 3; matrix products, arithmetic and copies ran while one was open for 2% -> 0% of each run, Pallas kernels for 0% -> 0%
where the time goes in v2:
time: 135 us
  blocking collectives  74.3 us (55%)
  waiting for transfers between devices  22.5 us (17%)
  starting transfers between devices  18.8 us (14%)
  Pallas kernels  16.9 us (13%)
  local copies, waits for them, and re-layouts  1.6 us (1%)
    all_to_all x4, blocking collectives, exchange(): return lax.all_to_all(value, axes, split_axis=0, concat_axis=0, tiled=True)  74.3 us
    pallas_call x7, Pallas kernels, call(): pl.pallas_call(kernel, out_shape=outs, in_specs=[smem if array.ndim == 1...  16.9 us
    all_to_all x1, waiting for transfers between devices, exchange(): return lax.all_to_all(value, axes, split_axis=0, concat_axis=0, tiled=True)  16.6 us
    ppermute x2, starting transfers between devices, swap_cores(): return lax.ppermute(value, 'core', [(0, 1), (1, 0)])  11.2 us
    all_to_all x1, starting transfers between devices, exchange(): return lax.all_to_all(value, axes, split_axis=0, concat_axis=0, tiled=True)  7.64 us
    ppermute x2, waiting for transfers between devices, swap_cores(): return lax.ppermute(value, 'core', [(0, 1), (1, 0)])  5.86 us
  transfers between devices with their start and end apart: 3, of which 3 were waited for; matrix products, arithmetic and copies ran while one was open for 0% of the time, Pallas kernels for 0%

profile of v2, /device:TPU:1, one launch (start us, length us, event | category | flops | bytes accessed | tf_op | source)
XLA Modules:
  0.0 134.8 jit_solution(12310760389923320135)
XLA Ops:
  0.6 0.0 copy-start.1
  0.6 6.4 %grad_term.1 = (f32[8,4,128,128]{3,2,1,0:T(8,128)}, f32[8,4,128,128]{3,2,1,0:T(8,128)}) custom-call(s32[1]{0:T(128)} %bitcast.device_ref, s32[8]{0:T(128)} %owner_ref.9, bf16[768,1024]{1,0:T(8,128)(2,1)} %act_hbm.1, bf16[768,1024]{1,0:T(8,128)(2,1)} %cot_hbm.1), custom_call_target="tpu_custom_call" | custom-call | tf_op jit(solution)/shard_map/grad_term/pallas_call | solution.py:210
  7.1 8.8 %collective-permute-start = (f32[8,4,128,128]{3,2,1,0:T(8,128)}, f32[8,4,128,128]{3,2,1,0:T(8,128)S(1)}, u32[]{:S(2)}, u32[]{:S(2)}) collective-permute-start(f32[8,4,128,128]{3,2,1,0:T(8,128)} %get-tuple-element.7), channel_id=1, source_target_pairs={{0,1},{1,0},{2,3},{3,2},{4,5},{5,4},{6,7},{7,6},{8,9},{9,8},{10,11... | collective-permute-start | bytes 6291464 | tf_op jit(solution)/shard_map/ppermute | solution.py:222
  15.9 4.0 %collective-permute-done.other_ref = f32[8,4,128,128]{3,2,1,0:T(8,128)S(1)} collective-permute-done((f32[8,4,128,128]{3,2,1,0:T(8,128)}, f32[8,4,128,128]{3,2,1,0:T(8,128)S(1)}, u32[]{:S(2)}, u32[]{:S(2)}) %collective-permute-start) | collective-permute-done | bytes 2097184 | tf_op jit(solution)/shard_map/ppermute | solution.py:222
  19.8 0.0 copy-done.1
  19.8 0.0 copy-start
  19.8 1.6 %copy-done = f32[8,4,128,128]{3,2,1,0:T(8,128)S(1)} copy-done((f32[8,4,128,128]{3,2,1,0:T(8,128)S(1)}, f32[8,4,128,128]{3,2,1,0:T(8,128)}, u32[]{:S(2)}) %copy-start) | copy-done | bytes 2097176
  21.4 0.2 pack.1
  21.6 0.0 copy-start.2
  21.6 18.3 %all_to_all.25.terms_ref = bf16[8,544,128]{2,1,0:T(8,128)(2,1)S(1)} all-to-all(bf16[8,544,128]{2,1,0:T(8,128)(2,1)S(1)} %pack.1), channel_id=1, replica_groups=mesh['rep'=8,'chip'=32,'core'=2] {'rep'}, dimensions={0} | all-to-all | bytes 2228224 | tf_op jit(solution)/shard_map/all_to_all | solution.py:203
  40.0 0.0 copy-done.2
  40.0 0.8 reduce.1
  40.7 31.5 %all_to_all.26.parts_ref.here_ref = bf16[32,96,128]{2,1,0:T(8,128)(2,1)S(1)} all-to-all(bf16[32,96,128]{2,1,0:T(8,128)(2,1)S(1)} %reduce.1), channel_id=1, replica_groups=mesh['rep'=8,'chip'=32,'core'=2] {'chip'}, dimensions={0} | all-to-all | bytes 1572864 | tf_op jit(solution)/shard_map/all_to_all | solution.py:203
  72.2 14.9 %all_to_all.27.slots_ref = bf16[8,16,128]{2,1,0:T(8,128)(2,1)S(1)} all-to-all(bf16[8,16,128]{2,1,0:T(8,128)(2,1)S(1)} %total.1), channel_id=1, replica_groups=mesh['rep'=8,'chip'=32,'core'=2] {'rep'}, dimensions={0} | all-to-all | bytes 65536 | tf_op jit(solution)/shard_map/all_to_all | solution.py:203
  87.1 1.4 %pair.1 = bf16[64,2,16,128]{3,2,1,0:T(8,128)(2,1)} custom-call(s32[1]{0:T(128)} %bitcast.device_ref, s32[8]{0:T(128)S(1)} %copy-done.2, bf16[8,16,128]{2,1,0:T(8,128)(2,1)S(1)} %all_to_all.27.slots_ref), custom_call_target="tpu_custom_call" | custom-call | tf_op jit(solution)/shard_map/pair/pallas_call | solution.py:210
  88.5 7.6 %all-to-all-start.3 = ((bf16[64,2,16,128]{3,2,1,0:T(8,128)(2,1)}), bf16[64,2,16,128]{3,2,1,0:T(8,128)(2,1)S(1)}, u32[]{:S(2)}, u32[]{:S(2)}) async-start(bf16[64,2,16,128]{3,2,1,0:T(8,128)(2,1)} %pair.1), calls=%async_computation.3 | async-start | bytes 1048576 | tf_op jit(solution)/shard_map/all_to_all | solution.py:203
  96.2 2.4 %collective-permute-start.1 = (bf16[32,96,128]{2,1,0:T(8,128)(2,1)S(1)}, bf16[32,96,128]{2,1,0:T(8,128)(2,1)S(1)}, u32[]{:S(2)}, u32[]{:S(2)}) collective-permute-start(bf16[32,96,128]{2,1,0:T(8,128)(2,1)S(1)} %all_to_all.26.parts_ref.here_ref), channel_id=1, source_target_pairs={{0,1},{1,0},{2,3},{3,2},{4,5},{5,4},{6,7},{7,6},{8,9},{9,8},{10,11... | collective-permute-start | bytes 2359304 | tf_op jit(solution)/shard_map/ppermute | solution.py:222
  98.6 1.9 %collective-permute-done.1.there_ref = bf16[32,96,128]{2,1,0:T(8,128)(2,1)S(1)} collective-permute-done((bf16[32,96,128]{2,1,0:T(8,128)(2,1)S(1)}, bf16[32,96,128]{2,1,0:T(8,128)(2,1)S(1)}, u32[]{:S(2)}, u32[]{:S(2)}) %collective-permute-start.1) | collective-permute-done | bytes 786464 | tf_op jit(solution)/shard_map/ppermute | solution.py:222
  100.4 16.6 %all-to-all-done.3.tiles_ref = bf16[64,2,16,128]{3,2,1,0:T(8,128)(2,1)S(1)} async-done(((bf16[64,2,16,128]{3,2,1,0:T(8,128)(2,1)}), bf16[64,2,16,128]{3,2,1,0:T(8,128)(2,1)S(1)}, u32[]{:S(2)}, u32[]{:S(2)}) %all-to-all-start.3) | async-done | bytes 524320 | tf_op jit(solution)/shard_map/all_to_all | solution.py:203
  117.0 6.9 %root.1 = (f32[8,512]{1,0:T(8,128)}, f32[8,16,512]{2,1,0:T(8,128)S(1)}) custom-call(s32[1]{0:T(128)} %bitcast.device_ref, s32[8]{0:T(128)S(1)} %copy-done.2, f32[8,512]{1,0:T(8,128)S(1)} %bitcast.4, bf16[32,96,128]{2,1,0:T(8,128)(2,1)S(1)} %all_to_all.26.parts_ref.here_ref, bf16[32,96,128]{2,1,0:T(8,128)(2,1)S(1)} %collective-permute-done.1.there_ref, ...), custom_call_target="tpu_custom_call" | custom-call | tf_op jit(solution)/shard_map/root/pallas_call | solution.py:210
  124.0 9.6 %all_to_all.28.pieces_ref = f32[8,16,512]{2,1,0:T(8,128)S(1)} all-to-all(f32[8,16,512]{2,1,0:T(8,128)S(1)} %get-tuple-element.9), channel_id=1, replica_groups=mesh['rep'=8,'chip'=32,'core'=2] {'rep'}, dimensions={0} | all-to-all | bytes 524288 | tf_op jit(solution)/shard_map/all_to_all | solution.py:203
  133.6 1.2 join.1
  (1 shorter events, 0.0 us)
Async XLA Ops:
  0.6 19.2 %copy-start.1 = (f32[1,8,512]{2,1,0:T(8,128)S(1)}, f32[1,8,512]{2,1,0:T(8,128)}, u32[]{:S(2)}) copy-start(f32[1,8,512]{2,1,0:T(8,128)} %param.6) | copy-start | bytes 49156
  7.1 12.8 %collective-permute-start = (f32[8,4,128,128]{3,2,1,0:T(8,128)}, f32[8,4,128,128]{3,2,1,0:T(8,128)S(1)}, u32[]{:S(2)}, u32[]{:S(2)}) collective-permute-start(f32[8,4,128,128]{3,2,1,0:T(8,128)} %get-tuple-element.7), channel_id=1, source_target_pairs={{0,1},{1,0},{2,3},{3,2},{4,5},{5,4},{6,7},{7,6},{8,9},{9,8},{10,11... | collective-permute-start | bytes 6291464 | tf_op jit(solution)/shard_map/ppermute | solution.py:222
  19.8 1.6 %copy-start = (f32[8,4,128,128]{3,2,1,0:T(8,128)S(1)}, f32[8,4,128,128]{3,2,1,0:T(8,128)}, u32[]{:S(2)}) copy-start(f32[8,4,128,128]{3,2,1,0:T(8,128)} %get-tuple-element.6.mine_ref) | copy-start | bytes 6291460
  21.6 18.4 %copy-start.2 = (s32[8]{0:T(128)S(1)}, s32[8]{0:T(128)}, u32[]{:S(2)}) copy-start(s32[8]{0:T(128)} %owner_ref.9) | copy-start | bytes 100
  88.5 28.5 %all-to-all-start.3 = ((bf16[64,2,16,128]{3,2,1,0:T(8,128)(2,1)}), bf16[64,2,16,128]{3,2,1,0:T(8,128)(2,1)S(1)}, u32[]{:S(2)}, u32[]{:S(2)}) async-start(bf16[64,2,16,128]{3,2,1,0:T(8,128)(2,1)} %pair.1), calls=%async_computation.3 | async-start | bytes 1048576 | tf_op jit(solution)/shard_map/all_to_all | solution.py:203
  96.2 4.3 %collective-permute-start.1 = (bf16[32,96,128]{2,1,0:T(8,128)(2,1)S(1)}, bf16[32,96,128]{2,1,0:T(8,128)(2,1)S(1)}, u32[]{:S(2)}, u32[]{:S(2)}) collective-permute-start(bf16[32,96,128]{2,1,0:T(8,128)(2,1)S(1)} %all_to_all.26.parts_ref.here_ref), channel_id=1, source_target_pairs={{0,1},{1,0},{2,3},{3,2},{4,5},{5,4},{6,7},{7,6},{8,9},{9,8},{10,11... | collective-permute-start | bytes 2359304 | tf_op jit(solution)/shard_map/ppermute | solution.py:222

commit v3 on v2

v3 whole, which is shorter than its diff:
```python
import functools

import jax
import jax.numpy as jnp
from jax import lax
from jax.experimental import pallas as pl
from jax.experimental.pallas import tpu as pltpu
from jax.sharding import Mesh
from jax.sharding import PartitionSpec as P

ema_decay = 0.9
BLOCK = 512
HALF = BLOCK // 2
GRAD = BLOCK * HALF // 128
LANES = 128
BLOCKS = 4
ROOTS = 8
COLS = 2
XS = 4
YS = 2
CHIPS = 32
CORES = 2
SHARDS = CHIPS * CORES
PARTS = YS * CHIPS
OUT_ROWS = 16
OWN_ROWS = 8
STATS = 32
TILE = 16
f32 = jnp.float32
bf16 = jnp.bfloat16
PLANE = ("yl", "chip")
VMEM_LIMIT = 40 * 1024 * 1024
GRAD_LIMIT = 60 * 1024 * 1024


def held_by(slot, owner_ref):
    held = jnp.int32(0)
    for root in range(1, ROOTS):
        held = jnp.where(owner_ref[root] == slot, root, held)
    return held


def grad_kernel(theirs, device_ref, act_hbm, cot_hbm, out_ref, act_ref, cot_ref, sems):
    core = device_ref[0] % CORES
    half = 1 - core if theirs else core

    def fetch(source, target, number, sem):
        columns = pl.ds(number * BLOCK, BLOCK)
        return pltpu.make_async_copy(source.at[:, columns], target.at[:, columns], sems.at[sem])

    act_copies = [fetch(act_hbm, act_ref, row, row) for row in range(2)]
    cot_copies = [fetch(cot_hbm, cot_ref, col, 2 + col) for col in range(COLS)]
    for copy in (act_copies[0], cot_copies[0], cot_copies[1], act_copies[1]):
        copy.start()
    for row in range(2):
        act_copies[row].wait()
        start = pl.multiple_of(row * BLOCK + half * HALF, HALF)
        act = act_ref[:, pl.ds(start, HALF)]
        for col in range(COLS):
            if row == 0:
                cot_copies[col].wait()
            term = lax.dot_general(
                act,
                cot_ref[:, col * BLOCK : (col + 1) * BLOCK],
                (((0,), (0,)), ((), ())),
                preferred_element_type=f32,
            ).astype(out_ref.dtype)
            for lane in range(BLOCK // LANES):
                out_ref[row * COLS + col, lane] = term[:, lane * LANES : (lane + 1) * LANES]


def stats_kernel(own_ref, out_ref):
    parts = [own_ref[:, lane * LANES : (lane + 1) * LANES] for lane in range(BLOCK // LANES)]
    out_ref[...] = jnp.concatenate(parts, axis=0).astype(bf16)


def pack_kernel(mine_ref, other_ref, own_ref, next_ref, out_ref):
    for block in range(BLOCKS):
        for lane in range(BLOCK // LANES):
            place = slice(lane * HALF, (lane + 1) * HALF)
            total = mine_ref[block, lane] + other_ref[block, lane].astype(f32)
            out_ref[block, place] = total.astype(bf16)
        out_ref[block, GRAD : GRAD + STATS] = own_ref[...]
        out_ref[block, GRAD + STATS : GRAD + 2 * STATS] = next_ref[...]


def reduce_kernel(device_ref, owner_ref, terms_ref, out_ref):
    replica = device_ref[0] // SHARDS
    block, side = replica // YS, replica % YS
    slot = owner_ref[side * BLOCKS + block]
    place = pl.multiple_of(GRAD + jnp.where(slot % YS == side, 0, STATS), STATS)
    stats = terms_ref[slot // YS, pl.ds(place, STATS)]
    for part in range(PARTS):
        rows = slice(part * TILE, (part + 1) * TILE)
        total = terms_ref[0, rows].astype(f32)
        for source in range(1, XS):
            total += terms_ref[source, rows].astype(f32)
        out_ref[part, :TILE] = total.astype(bf16)
        out_ref[part, TILE:] = stats


def total_kernel(parts_ref, gradient_ref, stats_ref):
    total = parts_ref[0, :TILE].astype(f32)
    for part in range(1, PARTS):
        total += parts_ref[part, :TILE].astype(f32)
    gradient = total.astype(bf16)
    for part in range(PARTS):
        gradient_ref[part] = gradient
        stats_ref[part] = parts_ref[part, TILE:]


def product(left, right):
    return jnp.dot(left.astype(bf16), right.astype(bf16), preferred_element_type=f32)


def newton(stats, gram):
    updated = ema_decay * stats + (1.0 - ema_decay) * gram
    scale = jnp.sqrt(jnp.sum(updated * updated, keepdims=True) + 1e-06)

    def step(state):
        low = 2.0 * state - product(state, state)
        high = 2.0 * low - product(low, low)
        return 1.25**4 * (state - product(high, state))

    first = updated * (0.2 / scale)
    second = step(first)
    return first, second, step(second)


def root_rows(first, second, third, diagonal):
    own_first, own_second, own_third = first
    both = own_first + own_second - product(own_first, second)
    return 1.25**3 * (diagonal - (both + own_third - product(both, third)))


def root_kernel(
    device_ref,
    owner_ref,
    stats_here_ref,
    stats_there_ref,
    tiles_here_ref,
    tiles_there_ref,
    out_ref,
    grad,
    stats,
    gram,
    rows,
):
    device = device_ref[0]
    replica = device // SHARDS
    position = device % SHARDS
    core = device % CORES
    for tiles_ref, at in ((tiles_here_ref, core), (tiles_there_ref, 1 - core)):
        for part in range(PARTS):
            lane, group = divmod(part, HALF // TILE)
            place = pl.ds(pl.multiple_of(at * HALF + group * TILE, TILE), TILE)
            grad[place, lane * LANES : (lane + 1) * LANES] = tiles_ref[part]
    for stats_ref, at in ((stats_here_ref, core), (stats_there_ref, 1 - core)):
        for side in range(2):
            for chip in range(CHIPS):
                value = stats_ref[side * CHIPS + chip].astype(f32)
                place = pl.ds(pl.multiple_of((chip * CORES + at) * 8, 8), 8)
                for lane in range(BLOCK // LANES):
                    stats[side, place, lane * LANES : (lane + 1) * LANES] = value[lane * 8 : lane * 8 + 8]

    gram[0] = lax.dot_general(
        grad[...], grad[...], (((1,), (1,)), ((), ())), preferred_element_type=f32
    )
    gram[1] = lax.dot_general(
        grad[...], grad[...], (((0,), (0,)), ((), ())), preferred_element_type=f32
    )
    own = pl.ds(pl.multiple_of(position * OWN_ROWS, OWN_ROWS), OWN_ROWS)
    for receiver in range(XS):
        held = held_by(receiver * YS + replica % YS, owner_ref)
        out_ref[receiver, OUT_ROWS:] = gram[held // BLOCKS, own, :]

    start = pl.multiple_of(position % (BLOCK // OUT_ROWS) * OUT_ROWS, OUT_ROWS)
    left = newton(stats[0], gram[0])
    for number in range(3):
        rows[number] = left[number]
    own = tuple(rows[number, pl.ds(start, OUT_ROWS), :] for number in range(3))
    shape = (OUT_ROWS, BLOCK)
    diagonal = lax.broadcasted_iota(jnp.int32, shape, 0) + start == lax.broadcasted_iota(jnp.int32, shape, 1)
    left_rows = root_rows(own, left[1], left[2], jnp.where(diagonal, 1.0, 0.0)).astype(bf16)
    mixed = jnp.dot(left_rows, grad[...], preferred_element_type=f32).astype(bf16)

    right = newton(stats[1], gram[1])
    shape = (BLOCK, BLOCK)
    diagonal = lax.broadcasted_iota(jnp.int32, shape, 0) == lax.broadcasted_iota(jnp.int32, shape, 1)
    right_root = root_rows(right, right[1], right[2], jnp.where(diagonal, 1.0, 0.0)).astype(bf16)
    piece = jnp.dot(mixed, right_root, preferred_element_type=f32)
    for receiver in range(XS):
        out_ref[receiver, :OUT_ROWS] = piece


def join_kernel(device_ref, owner_ref, own_ref, pieces_ref, updated_ref, direction_ref):
    device = device_ref[0]
    block = held_by(device // SHARDS, owner_ref) % BLOCKS
    updated_ref[...] = ema_decay * own_ref[...] + (1.0 - ema_decay) * pieces_ref[block, OUT_ROWS:]
    first = device % SHARDS // (BLOCK // OUT_ROWS) * COLS
    for col in range(COLS):
        direction_ref[:, col * BLOCK : (col + 1) * BLOCK] = pieces_ref[first + col, :OUT_ROWS]


def exchange(value, axes):
    return lax.all_to_all(value, axes, split_axis=0, concat_axis=0, tiled=True)


def call(kernel, name, outs, arrays, scratch=(), limit=VMEM_LIMIT):
    vmem = pl.BlockSpec(memory_space=pltpu.VMEM)
    smem = pl.BlockSpec(memory_space=pltpu.SMEM)
    rest = pl.BlockSpec(memory_space=pl.ANY) if limit > VMEM_LIMIT else vmem
    return pl.pallas_call(
        kernel,
        out_shape=outs,
        in_specs=[smem if array.ndim == 1 else rest for array in arrays],
        out_specs=tuple(vmem for _ in outs) if isinstance(outs, tuple) else vmem,
        scratch_shapes=list(scratch),
        compiler_params=pltpu.CompilerParams(vmem_limit_bytes=limit),
        name=name,
    )(*arrays)


def swap(value, axis):
    return lax.ppermute(value, axis, [(0, 1), (1, 0)])


def body(activations, cotangents, statistics, owner):
    device = lax.axis_index(("x", "yl", "chip", "core")).astype(jnp.int32).reshape(1)
    array = jax.ShapeDtypeStruct
    own = statistics[0]

    def gradient_half(theirs, kind):
        return call(
            functools.partial(grad_kernel, theirs),
            "grad_theirs" if theirs else "grad_mine",
            array((BLOCKS, BLOCK // LANES, HALF, LANES), kind),
            (device, activations, cotangents),
            scratch=[
                pltpu.VMEM(activations.shape, bf16),
                pltpu.VMEM(cotangents.shape, bf16),
                pltpu.SemaphoreType.DMA((4,)),
            ],
            limit=GRAD_LIMIT,
        )

    own_stats = call(stats_kernel, "stats", array((STATS, LANES), bf16), (own,))
    next_stats = swap(own_stats, "yl")
    other = swap(gradient_half(True, bf16), "core")
    mine = gradient_half(False, f32)
    packed = call(
        pack_kernel,
        "pack",
        array((XS, GRAD + 2 * STATS, LANES), bf16),
        (mine, other, own_stats, next_stats),
    )
    terms = exchange(packed, "x")
    reduced = call(
        reduce_kernel,
        "reduce",
        array((PARTS, TILE + STATS, LANES), bf16),
        (device, owner, terms),
    )
    gradient, stats = call(
        total_kernel,
        "total",
        (array((PARTS, TILE, LANES), bf16), array((PARTS, STATS, LANES), bf16)),
        (exchange(reduced, PLANE),),
    )
    tiles = exchange(gradient, PLANE)
    pieces = call(
        root_kernel,
        "root",
        array((XS, OUT_ROWS + OWN_ROWS, BLOCK), f32),
        (device, owner, stats, swap(stats, "core"), tiles, swap(tiles, "core")),
        scratch=[
            pltpu.VMEM((BLOCK, BLOCK), bf16),
            pltpu.VMEM((2, BLOCK, BLOCK), f32),
            pltpu.VMEM((2, BLOCK, BLOCK), f32),
            pltpu.VMEM((3, BLOCK, BLOCK), f32),
        ],
    )
    updated, direction = call(
        join_kernel,
        "join",
        (array((OWN_ROWS, BLOCK), f32), array((OUT_ROWS, COLS * BLOCK), f32)),
        (device, owner, own, exchange(pieces, "x")),
    )
    return updated[None], direction


def solution(mesh):
    fine = Mesh(mesh.devices.reshape(XS, YS, CHIPS, CORES), ("x", "yl", "chip", "core"))
    rep, shard = ("x", "yl"), ("chip", "core")
    every = rep + shard
    return jax.shard_map(
        body,
        mesh=fine,
        in_specs=(P(every, None), P(every, None), P(rep, shard, None), P()),
        out_specs=(P(rep, shard, None), P(shard, None)),
        check_vma=False,
    )
```

time: 135 us -> 117 us (0.87)
  blocking collectives: 74.3 us -> 58.9 us
  waiting for transfers between devices: 22.5 us -> 8.88 us
  starting transfers between devices: 18.8 us -> 28.5 us
    all_to_all x4 -> x3, blocking collectives: 74.3 us -> 58.9 us  [exchange(): return lax.all_to_all(value, axes, split_axis=0, concat_axis=0, tiled=True)]
    ppermute x2 -> x4, starting transfers between devices: 11.2 us -> 20.2 us  [swap(): return lax.ppermute(value, axis, [(0, 1), (1, 0)])]
    all_to_all x1, waiting for transfers between devices: 16.6 us -> 7.74 us  [exchange(): return lax.all_to_all(value, axes, split_axis=0, concat_axis=0, tiled=True)]
    ppermute x2 -> x4, waiting for transfers between devices: 5.86 us -> 1.14 us  [swap(): return lax.ppermute(value, axis, [(0, 1), (1, 0)])]
    pallas_call x7 -> x8, Pallas kernels: 16.9 us -> 17.8 us  [call(): pl.pallas_call(kernel, out_shape=outs, in_specs=[smem if array.ndim == 1...]
  transfers between devices with their start and end apart: 3 -> 5, of which waited for: 3 -> 2; matrix products, arithmetic and copies ran while one was open for 0% -> 0% of each run, Pallas kernels for 0% -> 4%
where the time goes in v3:
time: 117 us; the launch traced here: 116 us
  blocking collectives  58.9 us (50%)
  starting transfers between devices  28.5 us (24%)
  Pallas kernels  17.8 us (15%)
  waiting for transfers between devices  8.88 us (8%)
  local copies, waits for them, and re-layouts  1.59 us (1%)
    all_to_all x3, blocking collectives, exchange(): return lax.all_to_all(value, axes, split_axis=0, concat_axis=0, tiled=True)  58.9 us
    ppermute x4, starting transfers between devices, swap(): return lax.ppermute(value, axis, [(0, 1), (1, 0)])  20.2 us
    pallas_call x8, Pallas kernels, call(): pl.pallas_call(kernel, out_shape=outs, in_specs=[smem if array.ndim == 1...  17.8 us
    all_to_all x1, starting transfers between devices, exchange(): return lax.all_to_all(value, axes, split_axis=0, concat_axis=0, tiled=True)  8.28 us
    all_to_all x1, waiting for transfers between devices, exchange(): return lax.all_to_all(value, axes, split_axis=0, concat_axis=0, tiled=True)  7.74 us
  transfers between devices with their start and end apart: 5, of which 2 were waited for; matrix products, arithmetic and copies ran while one was open for 0% of the time, Pallas kernels for 4%

profile of v3, /device:TPU:1, one launch (start us, length us, event | category | flops | bytes accessed | tf_op | source)
XLA Modules:
  0.0 116.4 jit_solution(6768292032091844524)
XLA Ops:
  0.6 0.0 copy-start.1
  0.6 3.8 %grad_theirs.1 = bf16[4,4,256,128]{3,2,1,0:T(8,128)(2,1)} custom-call(s32[1]{0:T(128)} %bitcast.device_ref, bf16[768,1024]{1,0:T(8,128)(2,1)} %act_hbm.3, bf16[768,1024]{1,0:T(8,128)(2,1)} %cot_hbm.3), custom_call_target="tpu_custom_call" | custom-call | tf_op jit(solution)/shard_map/grad_theirs/pallas_call | solution.py:213
  4.5 8.8 %collective-permute-start = (bf16[4,4,256,128]{3,2,1,0:T(8,128)(2,1)}, bf16[4,4,256,128]{3,2,1,0:T(8,128)(2,1)S(1)}, u32[]{:S(2)}, u32[]{:S(2)}) collective-permute-start(bf16[4,4,256,128]{3,2,1,0:T(8,128)(2,1)} %grad_theirs.1), channel_id=1, source_target_pairs={{0,1},{1,0},{2,3},{3,2},{4,5},{5,4},{6,7},{7,6},{8,9},{9,8},{10,11... | collective-permute-start | bytes 3145736 | tf_op jit(solution)/shard_map/ppermute | solution.py:225
  13.2 0.0 copy-done.1
  13.3 1.9 %collective-permute-start.1 = (bf16[32,128]{1,0:T(8,128)(2,1)S(1)}, bf16[32,128]{1,0:T(8,128)(2,1)S(1)}, u32[]{:S(2)}, u32[]{:S(2)}) collective-permute-start(bf16[32,128]{1,0:T(8,128)(2,1)S(1)} %stats.1.own_ref), channel_id=1, source_target_pairs={{0,64},{64,0},{1,65},{65,1},{2,66},{66,2},{3,67},{67,3},{4,68},{68... | collective-permute-start | bytes 24584 | tf_op jit(solution)/shard_map/ppermute | solution.py:225
  15.2 4.1 %grad_mine.1.mine_ref = f32[4,4,256,128]{3,2,1,0:T(8,128)} custom-call(s32[1]{0:T(128)} %bitcast.device_ref, bf16[768,1024]{1,0:T(8,128)(2,1)} %act_hbm.3, bf16[768,1024]{1,0:T(8,128)(2,1)} %cot_hbm.3), custom_call_target="tpu_custom_call" | custom-call | tf_op jit(solution)/shard_map/grad_mine/pallas_call | solution.py:213
  19.3 0.0 collective-permute-done.1.next_ref
  19.4 0.0 collective-permute-done.other_ref
  19.4 0.0 copy-start
  19.4 1.6 %copy-done = f32[4,4,256,128]{3,2,1,0:T(8,128)S(1)} copy-done((f32[4,4,256,128]{3,2,1,0:T(8,128)S(1)}, f32[4,4,256,128]{3,2,1,0:T(8,128)}, u32[]{:S(2)}) %copy-start) | copy-done | bytes 2097176
  21.0 0.2 pack.1
  21.1 0.0 copy-start.2
  21.1 18.4 %all_to_all.20.terms_ref = bf16[4,1088,128]{2,1,0:T(8,128)(2,1)S(1)} all-to-all(bf16[4,1088,128]{2,1,0:T(8,128)(2,1)S(1)} %pack.1), channel_id=1, replica_groups=mesh['x'=4,'yl'=2,'chip'=32,'core'=2] {'x'}, dimensions={0} | all-to-all | bytes 2228224 | tf_op jit(solution)/shard_map/all_to_all | solution.py:206
  39.5 0.0 copy-done.2
  39.5 0.7 reduce.1
  40.2 32.7 %all_to_all.21.parts_ref = bf16[64,48,128]{2,1,0:T(8,128)(2,1)S(1)} all-to-all(bf16[64,48,128]{2,1,0:T(8,128)(2,1)S(1)} %reduce.1), channel_id=1, replica_groups=mesh['x'=4,'yl'=2,'chip'=32,'core'=2] {'yl','chip'}, dimensions={0} | all-to-all | bytes 1572864 | tf_op jit(solution)/shard_map/all_to_all | solution.py:206
  72.9 0.8 total.1
  73.7 8.3 %all-to-all-start.2 = ((bf16[64,16,128]{2,1,0:T(8,128)(2,1)}), bf16[64,16,128]{2,1,0:T(8,128)(2,1)S(1)}, u32[]{:S(2)}, u32[]{:S(2)}) async-start(bf16[64,16,128]{2,1,0:T(8,128)(2,1)} %get-tuple-element.7), calls=%async_computation.2 | async-start | bytes 524288 | tf_op jit(solution)/shard_map/all_to_all | solution.py:206
  82.0 4.0 %collective-permute-start.2 = (bf16[64,32,128]{2,1,0:T(8,128)(2,1)S(1)}, bf16[64,32,128]{2,1,0:T(8,128)(2,1)S(1)}, u32[]{:S(2)}, u32[]{:S(2)}) collective-permute-start(bf16[64,32,128]{2,1,0:T(8,128)(2,1)S(1)} %get-tuple-element.6.stats_here_ref), channel_id=1, source_target_pairs={{0,1},{1,0},{2,3},{3,2},{4,5},{5,4},{6,7},{7,6},{8,9},{9,8},{10,11... | collective-permute-start | bytes 1572872 | tf_op jit(solution)/shard_map/ppermute | solution.py:225
  86.1 7.7 %all-to-all-done.2.tiles_here_ref = bf16[64,16,128]{2,1,0:T(8,128)(2,1)S(1)} async-done(((bf16[64,16,128]{2,1,0:T(8,128)(2,1)}), bf16[64,16,128]{2,1,0:T(8,128)(2,1)S(1)}, u32[]{:S(2)}, u32[]{:S(2)}) %all-to-all-start.2) | async-done | bytes 262176 | tf_op jit(solution)/shard_map/all_to_all | solution.py:206
  93.8 5.5 %collective-permute-start.3 = (bf16[64,16,128]{2,1,0:T(8,128)(2,1)S(1)}, bf16[64,16,128]{2,1,0:T(8,128)(2,1)S(1)}, u32[]{:S(2)}, u32[]{:S(2)}) collective-permute-start(bf16[64,16,128]{2,1,0:T(8,128)(2,1)S(1)} %all-to-all-done.2.tiles_here_ref), channel_id=1, source_target_pairs={{0,1},{1,0},{2,3},{3,2},{4,5},{5,4},{6,7},{7,6},{8,9},{9,8},{10,11... | collective-permute-start | bytes 786440 | tf_op jit(solution)/shard_map/ppermute | solution.py:225
  99.3 0.0 collective-permute-done.2.stats_there_ref
  99.3 1.1 collective-permute-done.3.tiles_there_ref
  100.4 7.0 %root.1 = f32[4,24,512]{2,1,0:T(8,128)S(1)} custom-call(s32[1]{0:T(128)} %bitcast.device_ref, s32[8]{0:T(128)S(1)} %copy-done.2, bf16[64,32,128]{2,1,0:T(8,128)(2,1)S(1)} %get-tuple-element.6.stats_here_ref, bf16[64,32,128]{2,1,0:T(8,128)(2,1)S(1)} %collective-permute-done.2.stats_there_ref, bf16[64,16,128]{2,1,0:T(8,128)(2,1)S(1)} %all-to-all-done.2.tiles_here_ref, ...), custom_call_target="tpu_custom_call" | custom-call | tf_op jit(solution)/shard_map/root/pallas_call | solution.py:213
  107.4 7.8 %all_to_all.22.pieces_ref = f32[4,24,512]{2,1,0:T(8,128)S(1)} all-to-all(f32[4,24,512]{2,1,0:T(8,128)S(1)} %root.1), channel_id=1, replica_groups=mesh['x'=4,'yl'=2,'chip'=32,'core'=2] {'x'}, dimensions={0} | all-to-all | bytes 393216 | tf_op jit(solution)/shard_map/all_to_all | solution.py:206
  115.2 1.2 %join.1 = (f32[8,512]{1,0:T(8,128)}, f32[16,1024]{1,0:T(8,128)}) custom-call(s32[1]{0:T(128)} %bitcast.device_ref, s32[8]{0:T(128)S(1)} %copy-done.2, f32[8,512]{1,0:T(8,128)S(1)} %bitcast.4, f32[4,24,512]{2,1,0:T(8,128)S(1)} %all_to_all.22.pieces_ref), custom_call_target="tpu_custom_call" | custom-call | tf_op jit(solution)/shard_map/join/pallas_call | solution.py:213
  (1 shorter events, 0.0 us)
Async XLA Ops:
  0.6 12.6 %copy-start.1 = (f32[1,8,512]{2,1,0:T(8,128)S(1)}, f32[1,8,512]{2,1,0:T(8,128)}, u32[]{:S(2)}) copy-start(f32[1,8,512]{2,1,0:T(8,128)} %param.6) | copy-start | bytes 49156
  4.5 14.9 %collective-permute-start = (bf16[4,4,256,128]{3,2,1,0:T(8,128)(2,1)}, bf16[4,4,256,128]{3,2,1,0:T(8,128)(2,1)S(1)}, u32[]{:S(2)}, u32[]{:S(2)}) collective-permute-start(bf16[4,4,256,128]{3,2,1,0:T(8,128)(2,1)} %grad_theirs.1), channel_id=1, source_target_pairs={{0,1},{1,0},{2,3},{3,2},{4,5},{5,4},{6,7},{7,6},{8,9},{9,8},{10,11... | collective-permute-start | bytes 3145736 | tf_op jit(solution)/shard_map/ppermute | solution.py:225
  13.3 6.1 %collective-permute-start.1 = (bf16[32,128]{1,0:T(8,128)(2,1)S(1)}, bf16[32,128]{1,0:T(8,128)(2,1)S(1)}, u32[]{:S(2)}, u32[]{:S(2)}) collective-permute-start(bf16[32,128]{1,0:T(8,128)(2,1)S(1)} %stats.1.own_ref), channel_id=1, source_target_pairs={{0,64},{64,0},{1,65},{65,1},{2,66},{66,2},{3,67},{67,3},{4,68},{68... | collective-permute-start | bytes 24584 | tf_op jit(solution)/shard_map/ppermute | solution.py:225
  19.4 1.6 %copy-start = (f32[4,4,256,128]{3,2,1,0:T(8,128)S(1)}, f32[4,4,256,128]{3,2,1,0:T(8,128)}, u32[]{:S(2)}) copy-start(f32[4,4,256,128]{3,2,1,0:T(8,128)} %grad_mine.1.mine_ref) | copy-start | bytes 6291460
  21.1 18.4 %copy-start.2 = (s32[8]{0:T(128)S(1)}, s32[8]{0:T(128)}, u32[]{:S(2)}) copy-start(s32[8]{0:T(128)} %owner_ref.5) | copy-start | bytes 100
  73.7 20.0 %all-to-all-start.2 = ((bf16[64,16,128]{2,1,0:T(8,128)(2,1)}), bf16[64,16,128]{2,1,0:T(8,128)(2,1)S(1)}, u32[]{:S(2)}, u32[]{:S(2)}) async-start(bf16[64,16,128]{2,1,0:T(8,128)(2,1)} %get-tuple-element.7), calls=%async_computation.2 | async-start | bytes 524288 | tf_op jit(solution)/shard_map/all_to_all | solution.py:206
  82.0 17.3 %collective-permute-start.2 = (bf16[64,32,128]{2,1,0:T(8,128)(2,1)S(1)}, bf16[64,32,128]{2,1,0:T(8,128)(2,1)S(1)}, u32[]{:S(2)}, u32[]{:S(2)}) collective-permute-start(bf16[64,32,128]{2,1,0:T(8,128)(2,1)S(1)} %get-tuple-element.6.stats_here_ref), channel_id=1, source_target_pairs={{0,1},{1,0},{2,3},{3,2},{4,5},{5,4},{6,7},{7,6},{8,9},{9,8},{10,11... | collective-permute-start | bytes 1572872 | tf_op jit(solution)/shard_map/ppermute | solution.py:225
  93.8 6.6 %collective-permute-start.3 = (bf16[64,16,128]{2,1,0:T(8,128)(2,1)S(1)}, bf16[64,16,128]{2,1,0:T(8,128)(2,1)S(1)}, u32[]{:S(2)}, u32[]{:S(2)}) collective-permute-start(bf16[64,16,128]{2,1,0:T(8,128)(2,1)S(1)} %all-to-all-done.2.tiles_here_ref), channel_id=1, source_target_pairs={{0,1},{1,0},{2,3},{3,2},{4,5},{5,4},{6,7},{7,6},{8,9},{9,8},{10,11... | collective-permute-start | bytes 786440 | tf_op jit(solution)/shard_map/ppermute | solution.py:225

commit v4 on v3

v4 whole, which is shorter than its diff:
```python
import jax
import jax.numpy as jnp
from jax import lax
from jax.experimental import pallas as pl
from jax.experimental.pallas import tpu as pltpu
from jax.sharding import Mesh
from jax.sharding import PartitionSpec as P

ema_decay = 0.9
BLOCK = 512
HALF = BLOCK // 2
LANES = 128
BLOCKS = 4
ROOTS = 8
COLS = 2
XS = 4
PAIR = 2
CORES = 2
SHARDS = 64
QUADS = 4
FAR = 16
PARTS = QUADS * FAR
OUT_ROWS = 16
OWN_ROWS = 8
STATS = 32
TILE = 16
f32 = jnp.float32
bf16 = jnp.bfloat16
NEAR_AXES = ("x", "yl", "zp")
FAR_AXES = ("z4", "yh")
PLANE = ("yl", "zp") + FAR_AXES
VMEM_LIMIT = 40 * 1024 * 1024
GRAD_LIMIT = 60 * 1024 * 1024


def held_by(slot, owner_ref):
    held = jnp.int32(0)
    for root in range(1, ROOTS):
        held = jnp.where(owner_ref[root] == slot, root, held)
    return held


def near_place(device):
    return device // (PAIR * SHARDS), device // SHARDS % PAIR, device // 8 % PAIR, device % CORES


def theirs_kernel(device_ref, act_hbm, cot_hbm, out_ref, act_ref, cot_ref, sems):
    half = 1 - device_ref[0] % CORES
    copies = []
    for row in range(2):
        start = pl.multiple_of(row * BLOCK + half * HALF, HALF)
        copies.append(
            pltpu.make_async_copy(act_hbm.at[:, pl.ds(start, HALF)], act_ref.at[row], sems.at[row])
        )
    for col in range(COLS):
        columns = pl.ds(col * BLOCK, BLOCK)
        copies.append(
            pltpu.make_async_copy(cot_hbm.at[:, columns], cot_ref.at[col], sems.at[2 + col])
        )
    for number in (0, 2, 3, 1):
        copies[number].start()
    for row in range(2):
        copies[row].wait()
        for col in range(COLS):
            if row == 0:
                copies[2 + col].wait()
            term = half_term(act_ref[row], cot_ref[col]).astype(bf16)
            for lane in range(QUADS):
                out_ref[row * COLS + col, lane] = term[:, lane * LANES : (lane + 1) * LANES]


def half_term(act, cot):
    return lax.dot_general(act, cot, (((0,), (0,)), ((), ())), preferred_element_type=f32)


def mine_kernel(device_ref, act_ref, cot_ref, other_ref, own_ref, out_ref):
    half = device_ref[0] % CORES
    parts = [own_ref[:, lane * LANES : (lane + 1) * LANES] for lane in range(BLOCK // LANES)]
    stats = jnp.concatenate(parts, axis=0).astype(bf16)
    for row in range(2):
        start = pl.multiple_of(row * BLOCK + half * HALF, HALF)
        act = act_ref[:, pl.ds(start, HALF)]
        for col in range(COLS):
            block = row * COLS + col
            term = half_term(act, cot_ref[:, col * BLOCK : (col + 1) * BLOCK])
            for lane in range(QUADS):
                total = term[:, lane * LANES : (lane + 1) * LANES] + other_ref[block, lane].astype(f32)
                out_ref[block * QUADS + lane, :HALF] = total.astype(bf16)
                out_ref[block * QUADS + lane, HALF:] = stats


def reduce_kernel(device_ref, owner_ref, terms_ref, out_ref):
    block, side, low, _ = near_place(device_ref[0])
    stats = terms_ref[owner_ref[side * BLOCKS + block] * PAIR + low, HALF:]
    for part in range(FAR):
        rows = slice(part * TILE, (part + 1) * TILE)
        total = terms_ref[0, rows].astype(f32)
        for source in range(1, XS * QUADS):
            total += terms_ref[source, rows].astype(f32)
        out_ref[part, :TILE] = total.astype(bf16)
        out_ref[part, TILE:] = stats


def total_kernel(parts_ref, gradient_ref, stats_ref):
    total = parts_ref[0, :TILE].astype(f32)
    for part in range(1, FAR):
        total += parts_ref[part, :TILE].astype(f32)
    gradient = total.astype(bf16)
    for part in range(PARTS):
        gradient_ref[part] = gradient
    for part in range(FAR):
        stats_ref[part] = parts_ref[part, TILE:]


def product(left, right):
    return jnp.dot(left.astype(bf16), right.astype(bf16), preferred_element_type=f32)


def newton(stats, gram):
    updated = ema_decay * stats + (1.0 - ema_decay) * gram
    scale = jnp.sqrt(jnp.sum(updated * updated, keepdims=True) + 1e-06)

    def step(state):
        low = 2.0 * state - product(state, state)
        high = 2.0 * low - product(low, low)
        return 1.25**4 * (state - product(high, state))

    first = updated * (0.2 / scale)
    second = step(first)
    return first, second, step(second)


def root_rows(first, second, third, diagonal):
    own_first, own_second, own_third = first
    both = own_first + own_second - product(own_first, second)
    return 1.25**3 * (diagonal - (both + own_third - product(both, third)))


def root_kernel(
    device_ref,
    owner_ref,
    stats_here_ref,
    stats_there_ref,
    tiles_here_ref,
    tiles_there_ref,
    out_ref,
    grad,
    stats,
    gram,
    rows,
):
    device = device_ref[0]
    position = device % SHARDS
    _, near_y, near_z, core = near_place(device)
    for tiles_ref, at in ((tiles_here_ref, core), (tiles_there_ref, 1 - core)):
        for part in range(PARTS):
            lane, group = divmod(part, FAR)
            place = pl.ds(pl.multiple_of(at * HALF + group * TILE, TILE), TILE)
            grad[place, lane * LANES : (lane + 1) * LANES] = tiles_ref[part]
    for stats_ref, at in ((stats_here_ref, core), (stats_there_ref, 1 - core)):
        for quad in range(QUADS):
            side = near_y if quad // PAIR == 0 else 1 - near_y
            low = near_z if quad % PAIR == 0 else 1 - near_z
            for part in range(FAR):
                high, column = divmod(part, 4)
                value = stats_ref[quad, part].astype(f32)
                shard = (high * PAIR + low) * 8 + column * CORES + at
                place = pl.ds(pl.multiple_of(shard * OWN_ROWS, OWN_ROWS), OWN_ROWS)
                for lane in range(BLOCK // LANES):
                    columns = slice(lane * LANES, (lane + 1) * LANES)
                    stats[side, place, columns] = value[lane * OWN_ROWS : (lane + 1) * OWN_ROWS]

    gram[0] = lax.dot_general(
        grad[...], grad[...], (((1,), (1,)), ((), ())), preferred_element_type=f32
    )
    gram[1] = lax.dot_general(
        grad[...], grad[...], (((0,), (0,)), ((), ())), preferred_element_type=f32
    )
    own = pl.ds(pl.multiple_of(position * OWN_ROWS, OWN_ROWS), OWN_ROWS)
    for receiver in range(XS):
        held = held_by(receiver * PAIR + near_y, owner_ref)
        out_ref[receiver, OUT_ROWS:] = gram[held // BLOCKS, own, :]

    start = pl.multiple_of(position % (BLOCK // OUT_ROWS) * OUT_ROWS, OUT_ROWS)
    left = newton(stats[0], gram[0])
    for number in range(3):
        rows[number] = left[number]
    own = tuple(rows[number, pl.ds(start, OUT_ROWS), :] for number in range(3))
    shape = (OUT_ROWS, BLOCK)
    diagonal = lax.broadcasted_iota(jnp.int32, shape, 0) + start == lax.broadcasted_iota(jnp.int32, shape, 1)
    left_rows = root_rows(own, left[1], left[2], jnp.where(diagonal, 1.0, 0.0)).astype(bf16)
    mixed = jnp.dot(left_rows, grad[...], preferred_element_type=f32).astype(bf16)

    right = newton(stats[1], gram[1])
    shape = (BLOCK, BLOCK)
    diagonal = lax.broadcasted_iota(jnp.int32, shape, 0) == lax.broadcasted_iota(jnp.int32, shape, 1)
    right_root = root_rows(right, right[1], right[2], jnp.where(diagonal, 1.0, 0.0)).astype(bf16)
    piece = jnp.dot(mixed, right_root, preferred_element_type=f32)
    for receiver in range(XS):
        out_ref[receiver, :OUT_ROWS] = piece


def join_kernel(device_ref, owner_ref, own_ref, pieces_ref, updated_ref, direction_ref):
    device = device_ref[0]
    block = held_by(device // SHARDS, owner_ref) % BLOCKS
    updated_ref[...] = ema_decay * own_ref[...] + (1.0 - ema_decay) * pieces_ref[block, OUT_ROWS:]
    first = device % SHARDS // (BLOCK // OUT_ROWS) * COLS
    for col in range(COLS):
        direction_ref[:, col * BLOCK : (col + 1) * BLOCK] = pieces_ref[first + col, :OUT_ROWS]


def exchange(value, axes):
    return lax.all_to_all(value, axes, split_axis=0, concat_axis=0, tiled=True)


def call(kernel, name, outs, arrays, scratch=(), limit=VMEM_LIMIT):
    vmem = pl.BlockSpec(memory_space=pltpu.VMEM)
    smem = pl.BlockSpec(memory_space=pltpu.SMEM)
    rest = pl.BlockSpec(memory_space=pl.ANY) if limit > VMEM_LIMIT else vmem
    return pl.pallas_call(
        kernel,
        out_shape=outs,
        in_specs=[smem if array.ndim == 1 else rest for array in arrays],
        out_specs=tuple(vmem for _ in outs) if isinstance(outs, tuple) else vmem,
        scratch_shapes=list(scratch),
        compiler_params=pltpu.CompilerParams(vmem_limit_bytes=limit),
        name=name,
    )(*arrays)


def swap(value, axis):
    return lax.ppermute(value, axis, [(0, 1), (1, 0)])


def swap_near(value):
    both = [(place, 3 - place) for place in range(QUADS)]
    return jnp.stack(
        [value, swap(value, "zp"), swap(value, "yl"), lax.ppermute(value, ("yl", "zp"), both)]
    )


def body(activations, cotangents, statistics, owner):
    device = lax.axis_index(("x", "yl", "z4", "zp", "yh", "core")).astype(jnp.int32).reshape(1)
    array = jax.ShapeDtypeStruct
    own = statistics[0]
    tokens = activations.shape[0]

    other = call(
        theirs_kernel,
        "grad_theirs",
        array((BLOCKS, QUADS, HALF, LANES), bf16),
        (device, activations, cotangents),
        scratch=[
            pltpu.VMEM((2, tokens, HALF), bf16),
            pltpu.VMEM((COLS, tokens, BLOCK), bf16),
            pltpu.SemaphoreType.DMA((4,)),
        ],
        limit=GRAD_LIMIT,
    )
    packed = call(
        mine_kernel,
        "grad_mine",
        array((XS * QUADS, HALF + STATS, LANES), bf16),
        (device, activations, cotangents, swap(other, "core"), own),
    )
    reduced = call(
        reduce_kernel,
        "reduce",
        array((FAR, TILE + STATS, LANES), bf16),
        (device, owner, exchange(packed, NEAR_AXES)),
    )
    gradient, stats = call(
        total_kernel,
        "total",
        (array((PARTS, TILE, LANES), bf16), array((FAR, STATS, LANES), bf16)),
        (exchange(reduced, FAR_AXES),),
    )
    stats = swap_near(stats)
    tiles = exchange(gradient, PLANE)
    pieces = call(
        root_kernel,
        "root",
        array((XS, OUT_ROWS + OWN_ROWS, BLOCK), f32),
        (device, owner, stats, swap(stats, "core"), tiles, swap(tiles, "core")),
        scratch=[
            pltpu.VMEM((BLOCK, BLOCK), bf16),
            pltpu.VMEM((2, BLOCK, BLOCK), f32),
            pltpu.VMEM((2, BLOCK, BLOCK), f32),
            pltpu.VMEM((3, BLOCK, BLOCK), f32),
        ],
    )
    updated, direction = call(
        join_kernel,
        "join",
        (array((OWN_ROWS, BLOCK), f32), array((OUT_ROWS, COLS * BLOCK), f32)),
        (device, owner, own, exchange(pieces, "x")),
    )
    return updated[None], direction


def solution(mesh):
    sizes = {"x": 4, "yl": 2, "z4": 4, "zp": 2, "yh": 4, "core": 2}
    fine = Mesh(mesh.devices.reshape(tuple(sizes.values())), tuple(sizes))
    every = tuple(sizes)
    rep, shard = every[:2], every[2:]
    return jax.shard_map(
        body,
        mesh=fine,
        in_specs=(P(every, None), P(every, None), P(rep, shard, None), P()),
        out_specs=(P(rep, shard, None), P(shard, None)),
        check_vma=False,
    )
```

time: 117 us -> 112 us (0.957)
  blocking collectives: 58.9 us -> 51 us
  starting transfers between devices: 28.5 us -> 34.3 us
  Pallas kernels: 17.8 us -> 14.3 us
  waiting for transfers between devices: 8.88 us -> 11.3 us
  local copies, waits for them, and re-layouts: 1.59 us -> 0.02 us
    all_to_all x3, blocking collectives: 58.9 us -> 51 us  [exchange(): return lax.all_to_all(value, axes, split_axis=0, concat_axis=0, tiled=True)]
    ppermute x0 -> x1, starting transfers between devices: none -> 3.85 us  [swap_near(): lax.ppermute(value, ('yl', 'zp'), both)]
    ppermute x4 -> x5, starting transfers between devices: 20.2 us -> 23.8 us  [swap(): return lax.ppermute(value, axis, [(0, 1), (1, 0)])]
    pallas_call x8 -> x6, Pallas kernels: 17.8 us -> 14.3 us  [call(): pl.pallas_call(kernel, out_shape=outs, in_specs=[smem if array.ndim == 1...]
    ppermute x4 -> x5, waiting for transfers between devices: 1.14 us -> 3.61 us  [swap(): return lax.ppermute(value, axis, [(0, 1), (1, 0)])]
    all_to_all x1, starting transfers between devices: 8.28 us -> 6.63 us  [exchange(): return lax.all_to_all(value, axes, split_axis=0, concat_axis=0, tiled=True)]
    unnamed x6 -> x8, local copies, waits for them, and re-layouts: 1.59 us -> 0.02 us
  transfers between devices with their start and end apart: 5 -> 7, of which waited for: 2 -> 3; matrix products, arithmetic and copies ran while one was open for 0% -> 0% of each run, Pallas kernels for 4% -> 0%
where the time goes in v4:
time: 112 us
  blocking collectives  51 us (46%)
  starting transfers between devices  34.3 us (31%)
  Pallas kernels  14.3 us (13%)
  waiting for transfers between devices  11.3 us (10%)
    all_to_all x3, blocking collectives, exchange(): return lax.all_to_all(value, axes, split_axis=0, concat_axis=0, tiled=True)  51 us
    ppermute x5, starting transfers between devices, swap(): return lax.ppermute(value, axis, [(0, 1), (1, 0)])  23.8 us
    pallas_call x6, Pallas kernels, call(): pl.pallas_call(kernel, out_shape=outs, in_specs=[smem if array.ndim == 1...  14.3 us
    all_to_all x1, waiting for transfers between devices, exchange(): return lax.all_to_all(value, axes, split_axis=0, concat_axis=0, tiled=True)  7.71 us
    all_to_all x1, starting transfers between devices, exchange(): return lax.all_to_all(value, axes, split_axis=0, concat_axis=0, tiled=True)  6.63 us
    ppermute x1, starting transfers between devices, swap_near(): lax.ppermute(value, ('yl', 'zp'), both)  3.85 us
    ppermute x5, waiting for transfers between devices, swap(): return lax.ppermute(value, axis, [(0, 1), (1, 0)])  3.61 us
  transfers between devices with their start and end apart: 7, of which 3 were waited for; matrix products, arithmetic and copies ran while one was open for 0% of the time, Pallas kernels for 0%

profile of v4, /device:TPU:1, one launch (start us, length us, event | category | flops | bytes accessed | tf_op | source)
XLA Modules:
  0.0 111.8 jit_solution(8577683891292904342)
XLA Ops:
  0.6 0.0 copy-start
  0.7 0.0 copy-start.1
  0.7 0.0 copy-start.2
  0.7 3.8 %grad_theirs.1 = bf16[4,4,256,128]{3,2,1,0:T(8,128)(2,1)} custom-call(s32[1]{0:T(128)} %bitcast.device_ref, bf16[768,1024]{1,0:T(8,128)(2,1)} %act_ref.1, bf16[768,1024]{1,0:T(8,128)(2,1)} %cot_ref.1), custom_call_target="tpu_custom_call" | custom-call | tf_op jit(solution)/shard_map/grad_theirs/pallas_call | solution.py:220
  4.5 8.8 %collective-permute-start = (bf16[4,4,256,128]{3,2,1,0:T(8,128)(2,1)}, bf16[4,4,256,128]{3,2,1,0:T(8,128)(2,1)S(1)}, u32[]{:S(2)}, u32[]{:S(2)}) collective-permute-start(bf16[4,4,256,128]{3,2,1,0:T(8,128)(2,1)} %grad_theirs.1), channel_id=1, source_target_pairs={{0,1},{1,0},{2,3},{3,2},{4,5},{5,4},{6,7},{7,6},{8,9},{9,8},{10,11... | collective-permute-start | bytes 3145736 | tf_op jit(solution)/shard_map/ppermute | solution.py:232
  13.3 2.5 %collective-permute-done.other_ref = bf16[4,4,256,128]{3,2,1,0:T(8,128)(2,1)S(1)} collective-permute-done((bf16[4,4,256,128]{3,2,1,0:T(8,128)(2,1)}, bf16[4,4,256,128]{3,2,1,0:T(8,128)(2,1)S(1)}, u32[]{:S(2)}, u32[]{:S(2)}) %collective-permute-start) | collective-permute-done | bytes 1048608 | tf_op jit(solution)/shard_map/ppermute | solution.py:232
  15.8 0.0 copy-done
  15.8 0.0 copy-done.1
  15.8 0.0 copy-done.2
  15.8 1.1 grad_mine.1
  16.8 0.0 copy-start.3
  16.9 19.8 %all_to_all.20.terms_ref = bf16[16,288,128]{2,1,0:T(8,128)(2,1)S(1)} all-to-all(bf16[16,288,128]{2,1,0:T(8,128)(2,1)S(1)} %grad_mine.1), channel_id=1, replica_groups=mesh['x'=4,'yl'=2,'z4'=4,'zp'=2,'yh'=4,'core'=2] {'x','yl','zp'}, dimensions={0} | all-to-all | bytes 2359296 | tf_op jit(solution)/shard_map/all_to_all | solution.py:213
  36.7 0.0 copy-done.3
  36.7 0.7 reduce.1
  37.4 23.4 %all_to_all.21.parts_ref = bf16[16,48,128]{2,1,0:T(8,128)(2,1)S(1)} all-to-all(bf16[16,48,128]{2,1,0:T(8,128)(2,1)S(1)} %reduce.1), channel_id=1, replica_groups=mesh['x'=4,'yl'=2,'z4'=4,'zp'=2,'yh'=4,'core'=2] {'z4','yh'}, dimensions={0} | all-to-all | bytes 393216 | tf_op jit(solution)/shard_map/all_to_all | solution.py:213
  60.8 0.7 total.1
  61.5 3.8 %collective-permute-start.3 = (bf16[16,32,128]{2,1,0:T(8,128)(2,1)S(1)}, bf16[16,32,128]{2,1,0:T(8,128)(2,1)S(1)}, u32[]{:S(2)}, u32[]{:S(2)}) collective-permute-start(bf16[16,32,128]{2,1,0:T(8,128)(2,1)S(1)} %get-tuple-element.6), channel_id=1, source_target_pairs={{0,72},{8,64},{64,8},{72,0},{1,73},{9,65},{65,9},{73,1},{2,74},{10... | collective-permute-start | bytes 393224 | tf_op jit(solution)/shard_map/ppermute | solution.py:238
  65.4 2.1 %collective-permute-start.2 = (bf16[16,32,128]{2,1,0:T(8,128)(2,1)S(1)}, bf16[16,32,128]{2,1,0:T(8,128)(2,1)S(1)}, u32[]{:S(2)}, u32[]{:S(2)}) collective-permute-start(bf16[16,32,128]{2,1,0:T(8,128)(2,1)S(1)} %get-tuple-element.6), channel_id=1, source_target_pairs={{0,64},{64,0},{1,65},{65,1},{2,66},{66,2},{3,67},{67,3},{4,68},{68... | collective-permute-start | bytes 393224 | tf_op jit(solution)/shard_map/ppermute | solution.py:232
  67.4 2.4 %collective-permute-start.1 = (bf16[16,32,128]{2,1,0:T(8,128)(2,1)S(1)}, bf16[16,32,128]{2,1,0:T(8,128)(2,1)S(1)}, u32[]{:S(2)}, u32[]{:S(2)}) collective-permute-start(bf16[16,32,128]{2,1,0:T(8,128)(2,1)S(1)} %get-tuple-element.6), channel_id=1, source_target_pairs={{0,8},{8,0},{1,9},{9,1},{2,10},{10,2},{3,11},{11,3},{4,12},{12,4},... | collective-permute-start | bytes 393224 | tf_op jit(solution)/shard_map/ppermute | solution.py:232
  69.9 6.6 %all-to-all-start.2 = ((bf16[64,16,128]{2,1,0:T(8,128)(2,1)}), bf16[64,16,128]{2,1,0:T(8,128)(2,1)S(1)}, u32[]{:S(2)}, u32[]{:S(2)}) async-start(bf16[64,16,128]{2,1,0:T(8,128)(2,1)} %get-tuple-element.7), calls=%async_computation.2 | async-start | bytes 524288 | tf_op jit(solution)/shard_map/all_to_all | solution.py:213
  76.5 0.0 collective-permute-done.3
  76.5 0.0 collective-permute-done.2
  76.5 0.0 collective-permute-done.1
  76.6 0.1 pad_maximum_fusion.stats_here_ref
  76.6 4.6 %collective-permute-start.4 = (bf16[4,16,32,128]{3,2,1,0:T(8,128)(2,1)S(1)}, bf16[4,16,32,128]{3,2,1,0:T(8,128)(2,1)S(1)}, u32[]{:S(2)}, u32[]{:S(2)}) collective-permute-start(bf16[4,16,32,128]{3,2,1,0:T(8,128)(2,1)S(1)} %pad_maximum_fusion.stats_here_ref), channel_id=1, source_target_pairs={{0,1},{1,0},{2,3},{3,2},{4,5},{5,4},{6,7},{7,6},{8,9},{9,8},{10,11... | collective-permute-start | bytes 1572872 | tf_op jit(solution)/shard_map/ppermute | solution.py:232
  81.2 7.7 %all-to-all-done.2.tiles_here_ref = bf16[64,16,128]{2,1,0:T(8,128)(2,1)S(1)} async-done(((bf16[64,16,128]{2,1,0:T(8,128)(2,1)}), bf16[64,16,128]{2,1,0:T(8,128)(2,1)S(1)}, u32[]{:S(2)}, u32[]{:S(2)}) %all-to-all-start.2) | async-done | bytes 262176 | tf_op jit(solution)/shard_map/all_to_all | solution.py:213
  88.9 6.0 %collective-permute-start.5 = (bf16[64,16,128]{2,1,0:T(8,128)(2,1)S(1)}, bf16[64,16,128]{2,1,0:T(8,128)(2,1)S(1)}, u32[]{:S(2)}, u32[]{:S(2)}) collective-permute-start(bf16[64,16,128]{2,1,0:T(8,128)(2,1)S(1)} %all-to-all-done.2.tiles_here_ref), channel_id=1, source_target_pairs={{0,1},{1,0},{2,3},{3,2},{4,5},{5,4},{6,7},{7,6},{8,9},{9,8},{10,11... | collective-permute-start | bytes 786440 | tf_op jit(solution)/shard_map/ppermute | solution.py:232
  94.9 0.0 collective-permute-done.4.stats_there_ref
  94.9 1.1 %collective-permute-done.5.tiles_there_ref = bf16[64,16,128]{2,1,0:T(8,128)(2,1)S(1)} collective-permute-done((bf16[64,16,128]{2,1,0:T(8,128)(2,1)S(1)}, bf16[64,16,128]{2,1,0:T(8,128)(2,1)S(1)}, u32[]{:S(2)}, u32[]{:S(2)}) %collective-permute-start.5) | collective-permute-done | bytes 262176 | tf_op jit(solution)/shard_map/ppermute | solution.py:232
  96.0 6.8 %root.1 = f32[4,24,512]{2,1,0:T(8,128)S(1)} custom-call(s32[1]{0:T(128)} %bitcast.device_ref, s32[8]{0:T(128)S(1)} %copy-done.3, bf16[4,16,32,128]{3,2,1,0:T(8,128)(2,1)S(1)} %pad_maximum_fusion.stats_here_ref, bf16[4,16,32,128]{3,2,1,0:T(8,128)(2,1)S(1)} %collective-permute-done.4.stats_there_ref, bf16[64,16,128]{2,1,0:T(8,128)(2,1)S(1)} %all-to-all-done.2.tiles_here_ref, ...), custom_call_target="tpu_custom_call" | custom-call | tf_op jit(solution)/shard_map/root/pallas_call | solution.py:220
  102.8 7.8 %all_to_all.22.pieces_ref = f32[4,24,512]{2,1,0:T(8,128)S(1)} all-to-all(f32[4,24,512]{2,1,0:T(8,128)S(1)} %root.1), channel_id=1, replica_groups=mesh['x'=4,'yl'=2,'z4'=4,'zp'=2,'yh'=4,'core'=2] {'x'}, dimensions={0} | all-to-all | bytes 393216 | tf_op jit(solution)/shard_map/all_to_all | solution.py:213
  110.6 1.2 %join.1 = (f32[8,512]{1,0:T(8,128)}, f32[16,1024]{1,0:T(8,128)}) custom-call(s32[1]{0:T(128)} %bitcast.device_ref, s32[8]{0:T(128)S(1)} %copy-done.3, f32[8,512]{1,0:T(8,128)S(1)} %bitcast.9, f32[4,24,512]{2,1,0:T(8,128)S(1)} %all_to_all.22.pieces_ref), custom_call_target="tpu_custom_call" | custom-call | tf_op jit(solution)/shard_map/join/pallas_call | solution.py:220
Async XLA Ops:
  0.6 15.1 %copy-start = (bf16[768,1024]{1,0:T(8,128)(2,1)S(1)}, bf16[768,1024]{1,0:T(8,128)(2,1)}, u32[]{:S(2)}) copy-start(bf16[768,1024]{1,0:T(8,128)(2,1)} %act_ref.1) | copy-start | bytes 4718596
  0.7 15.1 %copy-start.1 = (bf16[768,1024]{1,0:T(8,128)(2,1)S(1)}, bf16[768,1024]{1,0:T(8,128)(2,1)}, u32[]{:S(2)}) copy-start(bf16[768,1024]{1,0:T(8,128)(2,1)} %cot_ref.1) | copy-start | bytes 4718596
  0.7 15.1 %copy-start.2 = (f32[1,8,512]{2,1,0:T(8,128)S(1)}, f32[1,8,512]{2,1,0:T(8,128)}, u32[]{:S(2)}) copy-start(f32[1,8,512]{2,1,0:T(8,128)} %param.6) | copy-start | bytes 49156
  4.5 11.3 %collective-permute-start = (bf16[4,4,256,128]{3,2,1,0:T(8,128)(2,1)}, bf16[4,4,256,128]{3,2,1,0:T(8,128)(2,1)S(1)}, u32[]{:S(2)}, u32[]{:S(2)}) collective-permute-start(bf16[4,4,256,128]{3,2,1,0:T(8,128)(2,1)} %grad_theirs.1), channel_id=1, source_target_pairs={{0,1},{1,0},{2,3},{3,2},{4,5},{5,4},{6,7},{7,6},{8,9},{9,8},{10,11... | collective-permute-start | bytes 3145736 | tf_op jit(solution)/shard_map/ppermute | solution.py:232
  16.8 19.8 %copy-start.3 = (s32[8]{0:T(128)S(1)}, s32[8]{0:T(128)}, u32[]{:S(2)}) copy-start(s32[8]{0:T(128)} %owner_ref.5) | copy-start | bytes 100
  61.5 15.0 %collective-permute-start.3 = (bf16[16,32,128]{2,1,0:T(8,128)(2,1)S(1)}, bf16[16,32,128]{2,1,0:T(8,128)(2,1)S(1)}, u32[]{:S(2)}, u32[]{:S(2)}) collective-permute-start(bf16[16,32,128]{2,1,0:T(8,128)(2,1)S(1)} %get-tuple-element.6), channel_id=1, source_target_pairs={{0,72},{8,64},{64,8},{72,0},{1,73},{9,65},{65,9},{73,1},{2,74},{10... | collective-permute-start | bytes 393224 | tf_op jit(solution)/shard_map/ppermute | solution.py:238
  65.4 11.2 %collective-permute-start.2 = (bf16[16,32,128]{2,1,0:T(8,128)(2,1)S(1)}, bf16[16,32,128]{2,1,0:T(8,128)(2,1)S(1)}, u32[]{:S(2)}, u32[]{:S(2)}) collective-permute-start(bf16[16,32,128]{2,1,0:T(8,128)(2,1)S(1)} %get-tuple-element.6), channel_id=1, source_target_pairs={{0,64},{64,0},{1,65},{65,1},{2,66},{66,2},{3,67},{67,3},{4,68},{68... | collective-permute-start | bytes 393224 | tf_op jit(solution)/shard_map/ppermute | solution.py:232
  67.4 9.1 %collective-permute-start.1 = (bf16[16,32,128]{2,1,0:T(8,128)(2,1)S(1)}, bf16[16,32,128]{2,1,0:T(8,128)(2,1)S(1)}, u32[]{:S(2)}, u32[]{:S(2)}) collective-permute-start(bf16[16,32,128]{2,1,0:T(8,128)(2,1)S(1)} %get-tuple-element.6), channel_id=1, source_target_pairs={{0,8},{8,0},{1,9},{9,1},{2,10},{10,2},{3,11},{11,3},{4,12},{12,4},... | collective-permute-start | bytes 393224 | tf_op jit(solution)/shard_map/ppermute | solution.py:232
  69.9 19.1 %all-to-all-start.2 = ((bf16[64,16,128]{2,1,0:T(8,128)(2,1)}), bf16[64,16,128]{2,1,0:T(8,128)(2,1)S(1)}, u32[]{:S(2)}, u32[]{:S(2)}) async-start(bf16[64,16,128]{2,1,0:T(8,128)(2,1)} %get-tuple-element.7), calls=%async_computation.2 | async-start | bytes 524288 | tf_op jit(solution)/shard_map/all_to_all | solution.py:213
  76.6 18.3 %collective-permute-start.4 = (bf16[4,16,32,128]{3,2,1,0:T(8,128)(2,1)S(1)}, bf16[4,16,32,128]{3,2,1,0:T(8,128)(2,1)S(1)}, u32[]{:S(2)}, u32[]{:S(2)}) collective-permute-start(bf16[4,16,32,128]{3,2,1,0:T(8,128)(2,1)S(1)} %pad_maximum_fusion.stats_here_ref), channel_id=1, source_target_pairs={{0,1},{1,0},{2,3},{3,2},{4,5},{5,4},{6,7},{7,6},{8,9},{9,8},{10,11... | collective-permute-start | bytes 1572872 | tf_op jit(solution)/shard_map/ppermute | solution.py:232
  88.9 7.1 %collective-permute-start.5 = (bf16[64,16,128]{2,1,0:T(8,128)(2,1)S(1)}, bf16[64,16,128]{2,1,0:T(8,128)(2,1)S(1)}, u32[]{:S(2)}, u32[]{:S(2)}) collective-permute-start(bf16[64,16,128]{2,1,0:T(8,128)(2,1)S(1)} %all-to-all-done.2.tiles_here_ref), channel_id=1, source_target_pairs={{0,1},{1,0},{2,3},{3,2},{4,5},{5,4},{6,7},{7,6},{8,9},{9,8},{10,11... | collective-permute-start | bytes 786440 | tf_op jit(solution)/shard_map/ppermute | solution.py:232

commit v5 on v4

--- a/solution.py
+++ b/solution.py
@@ -90,15 +90,17 @@
 
 
 def reduce_kernel(device_ref, owner_ref, terms_ref, out_ref):
-    block, side, low, _ = near_place(device_ref[0])
-    stats = terms_ref[owner_ref[side * BLOCKS + block] * PAIR + low, HALF:]
+    block, side, _, _ = near_place(device_ref[0])
+    first = owner_ref[side * BLOCKS + block] * PAIR
+    stats = [terms_ref[first + low, HALF:] for low in range(PAIR)]
     for part in range(FAR):
         rows = slice(part * TILE, (part + 1) * TILE)
         total = terms_ref[0, rows].astype(f32)
         for source in range(1, XS * QUADS):
             total += terms_ref[source, rows].astype(f32)
         out_ref[part, :TILE] = total.astype(bf16)
-        out_ref[part, TILE:] = stats
+        for low in range(PAIR):
+            out_ref[part, TILE + low * STATS : TILE + (low + 1) * STATS] = stats[low]
 
 
 def total_kernel(parts_ref, gradient_ref, stats_ref):
@@ -109,58 +111,17 @@
     for part in range(PARTS):
         gradient_ref[part] = gradient
     for part in range(FAR):
-        stats_ref[part] = parts_ref[part, TILE:]
-
-
-def product(left, right):
-    return jnp.dot(left.astype(bf16), right.astype(bf16), preferred_element_type=f32)
-
-
-def newton(stats, gram):
-    updated = ema_decay * stats + (1.0 - ema_decay) * gram
-    scale = jnp.sqrt(jnp.sum(updated * updated, keepdims=True) + 1e-06)
-
-    def step(state):
-        low = 2.0 * state - product(state, state)
-        high = 2.0 * low - product(low, low)
-        return 1.25**4 * (state - product(high, state))
-
-    first = updated * (0.2 / scale)
-    second = step(first)
-    return first, second, step(second)
-
-
-def root_rows(first, second, third, diagonal):
-    own_first, own_second, own_third = first
-    both = own_first + own_second - product(own_first, second)
-    return 1.25**3 * (diagonal - (both + own_third - product(both, third)))
-
-
-def root_kernel(
-    device_ref,
-    owner_ref,
-    stats_here_ref,
-    stats_there_ref,
-    tiles_here_ref,
-    tiles_there_ref,
-    out_ref,
-    grad,
-    stats,
-    gram,
-    rows,
-):
-    device = device_ref[0]
-    position = device % SHARDS
-    _, near_y, near_z, core = near_place(device)
-    for tiles_ref, at in ((tiles_here_ref, core), (tiles_there_ref, 1 - core)):
-        for part in range(PARTS):
-            lane, group = divmod(part, FAR)
-            place = pl.ds(pl.multiple_of(at * HALF + group * TILE, TILE), TILE)
-            grad[place, lane * LANES : (lane + 1) * LANES] = tiles_ref[part]
+        for low in range(PAIR):
+            place = slice(TILE + low * STATS, TILE + (low + 1) * STATS)
+            stats_ref[low, part] = parts_ref[part, place]
+
+
+def unpack_kernel(device_ref, stats_here_ref, stats_there_ref, stats):
+    _, near_y, _, core = near_place(device_ref[0])
     for stats_ref, at in ((stats_here_ref, core), (stats_there_ref, 1 - core)):
         for quad in range(QUADS):
             side = near_y if quad // PAIR == 0 else 1 - near_y
-            low = near_z if quad % PAIR == 0 else 1 - near_z
+            low = quad % PAIR
             for part in range(FAR):
                 high, column = divmod(part, 4)
                 value = stats_ref[quad, part].astype(f32)
@@ -170,6 +131,50 @@
                     columns = slice(lane * LANES, (lane + 1) * LANES)
                     stats[side, place, columns] = value[lane * OWN_ROWS : (lane + 1) * OWN_ROWS]
 
+def product(left, right):
+    return jnp.dot(left.astype(bf16), right.astype(bf16), preferred_element_type=f32)
+
+
+def newton(stats, gram):
+    sides = range(2)
+    updated = [ema_decay * stats[side] + (1.0 - ema_decay) * gram[side] for side in sides]
+    scales = [jnp.sqrt(jnp.sum(value * value, keepdims=True) + 1e-06) for value in updated]
+
+    def step(state):
+        low = [2.0 * state[side] - product(state[side], state[side]) for side in sides]
+        high = [2.0 * low[side] - product(low[side], low[side]) for side in sides]
+        return [1.25**4 * (state[side] - product(high[side], state[side])) for side in sides]
+
+    first = [updated[side] * (0.2 / scales[side]) for side in sides]
+    second = step(first)
+    return first, second, step(second)
+
+
+def root_rows(first, second, third, diagonal):
+    own_first, own_second, own_third = first
+    both = own_first + own_second - product(own_first, second)
+    return 1.25**3 * (diagonal - (both + own_third - product(both, third)))
+
+
+def root_kernel(
+    device_ref,
+    owner_ref,
+    stats,
+    tiles_here_ref,
+    tiles_there_ref,
+    out_ref,
+    grad,
+    gram,
+    rows,
+):
+    device = device_ref[0]
+    position = device % SHARDS
+    _, near_y, _, core = near_place(device)
+    for tiles_ref, at in ((tiles_here_ref, core), (tiles_there_ref, 1 - core)):
+        for part in range(PARTS):
+            lane, group = divmod(part, FAR)
+            place = pl.ds(pl.multiple_of(at * HALF + group * TILE, TILE), TILE)
+            grad[place, lane * LANES : (lane + 1) * LANES] = tiles_ref[part]
     gram[0] = lax.dot_general(
         grad[...], grad[...], (((1,), (1,)), ((), ())), preferred_element_type=f32
     )
@@ -182,7 +187,8 @@
         out_ref[receiver, OUT_ROWS:] = gram[held // BLOCKS, own, :]
 
     start = pl.multiple_of(position % (BLOCK // OUT_ROWS) * OUT_ROWS, OUT_ROWS)
-    left = newton(stats[0], gram[0])
+    states = newton(stats, gram)
+    left, right = [[state[side] for state in states] for side in range(2)]
     for number in range(3):
         rows[number] = left[number]
     own = tuple(rows[number, pl.ds(start, OUT_ROWS), :] for number in range(3))
@@ -191,7 +197,6 @@
     left_rows = root_rows(own, left[1], left[2], jnp.where(diagonal, 1.0, 0.0)).astype(bf16)
     mixed = jnp.dot(left_rows, grad[...], preferred_element_type=f32).astype(bf16)
 
-    right = newton(stats[1], gram[1])
     shape = (BLOCK, BLOCK)
     diagonal = lax.broadcasted_iota(jnp.int32, shape, 0) == lax.broadcasted_iota(jnp.int32, shape, 1)
     right_root = root_rows(right, right[1], right[2], jnp.where(diagonal, 1.0, 0.0)).astype(bf16)
@@ -232,13 +237,6 @@
     return lax.ppermute(value, axis, [(0, 1), (1, 0)])
 
 
-def swap_near(value):
-    both = [(place, 3 - place) for place in range(QUADS)]
-    return jnp.stack(
-        [value, swap(value, "zp"), swap(value, "yl"), lax.ppermute(value, ("yl", "zp"), both)]
-    )
-
-
 def body(activations, cotangents, statistics, owner):
     device = lax.axis_index(("x", "yl", "z4", "zp", "yh", "core")).astype(jnp.int32).reshape(1)
     array = jax.ShapeDtypeStruct
@@ -266,25 +264,30 @@
     reduced = call(
         reduce_kernel,
         "reduce",
-        array((FAR, TILE + STATS, LANES), bf16),
+        array((FAR, TILE + PAIR * STATS, LANES), bf16),
         (device, owner, exchange(packed, NEAR_AXES)),
     )
     gradient, stats = call(
         total_kernel,
         "total",
-        (array((PARTS, TILE, LANES), bf16), array((FAR, STATS, LANES), bf16)),
+        (array((PARTS, TILE, LANES), bf16), array((PAIR, FAR, STATS, LANES), bf16)),
         (exchange(reduced, FAR_AXES),),
     )
-    stats = swap_near(stats)
+    stats = jnp.concatenate([stats, swap(stats, "yl")])
+    rows = call(
+        unpack_kernel,
+        "unpack",
+        array((2, BLOCK, BLOCK), f32),
+        (device, stats, swap(stats, "core")),
+    )
     tiles = exchange(gradient, PLANE)
     pieces = call(
         root_kernel,
         "root",
         array((XS, OUT_ROWS + OWN_ROWS, BLOCK), f32),
-        (device, owner, stats, swap(stats, "core"), tiles, swap(tiles, "core")),
+        (device, owner, rows, tiles, swap(tiles, "core")),
         scratch=[
             pltpu.VMEM((BLOCK, BLOCK), bf16),
-            pltpu.VMEM((2, BLOCK, BLOCK), f32),
             pltpu.VMEM((2, BLOCK, BLOCK), f32),
             pltpu.VMEM((3, BLOCK, BLOCK), f32),
         ],

time: 112 us -> 109 us (0.973)
  starting transfers between devices: 34.3 us -> 27.5 us
  blocking collectives: 51 us -> 53.3 us
  waiting for transfers between devices: 11.3 us -> 12.5 us
    ppermute x5 -> x4, starting transfers between devices: 23.8 us -> 19.2 us  [swap(): return lax.ppermute(value, axis, [(0, 1), (1, 0)])]
    ppermute x1 -> x0, starting transfers between devices: 3.85 us -> none  [swap_near(): lax.ppermute(value, ('yl', 'zp'), both)]
    all_to_all x3, blocking collectives: 51 us -> 53.3 us  [exchange(): return lax.all_to_all(value, axes, split_axis=0, concat_axis=0, tiled=True)]
    all_to_all x1, starting transfers between devices: 6.63 us -> 8.26 us  [exchange(): return lax.all_to_all(value, axes, split_axis=0, concat_axis=0, tiled=True)]
    all_to_all x1, waiting for transfers between devices: 7.71 us -> 9.12 us  [exchange(): return lax.all_to_all(value, axes, split_axis=0, concat_axis=0, tiled=True)]
    ppermute x5 -> x4, waiting for transfers between devices: 3.61 us -> 3.37 us  [swap(): return lax.ppermute(value, axis, [(0, 1), (1, 0)])]
    pallas_call x6 -> x7, Pallas kernels: 14.3 us -> 14.1 us  [call(): pl.pallas_call(kernel, out_shape=outs, in_specs=[smem if array.ndim == 1...]
  transfers between devices with their start and end apart: 7 -> 5, of which waited for: 3 -> 3; matrix products, arithmetic and copies ran while one was open for 0% -> 0% of each run, Pallas kernels for 0% -> 0%
where the time goes in v5:
time: 109 us; the launch traced here: 108 us
  blocking collectives  53.3 us (49%)
  starting transfers between devices  27.5 us (25%)
  Pallas kernels  14.1 us (13%)
  waiting for transfers between devices  12.5 us (11%)
    all_to_all x3, blocking collectives, exchange(): return lax.all_to_all(value, axes, split_axis=0, concat_axis=0, tiled=True)  53.3 us
    ppermute x4, starting transfers between devices, swap(): return lax.ppermute(value, axis, [(0, 1), (1, 0)])  19.2 us
    pallas_call x7, Pallas kernels, call(): pl.pallas_call(kernel, out_shape=outs, in_specs=[smem if array.ndim == 1...  14.1 us
    all_to_all x1, waiting for transfers between devices, exchange(): return lax.all_to_all(value, axes, split_axis=0, concat_axis=0, tiled=True)  9.12 us
    all_to_all x1, starting transfers between devices, exchange(): return lax.all_to_all(value, axes, split_axis=0, concat_axis=0, tiled=True)  8.26 us
    ppermute x4, waiting for transfers between devices, swap(): return lax.ppermute(value, axis, [(0, 1), (1, 0)])  3.37 us
  transfers between devices with their start and end apart: 5, of which 3 were waited for; matrix products, arithmetic and copies ran while one was open for 0% of the time, Pallas kernels for 0%

profile of v5, /device:TPU:1, one launch (start us, length us, event | category | flops | bytes accessed | tf_op | source)
XLA Modules:
  0.0 108.2 jit_solution(17476651420617366508)
XLA Ops:
  0.6 0.0 copy-start
  0.7 0.0 copy-start.1
  0.7 0.0 copy-start.2
  0.7 3.8 %grad_theirs.1 = bf16[4,4,256,128]{3,2,1,0:T(8,128)(2,1)} custom-call(s32[1]{0:T(128)} %bitcast.device_ref, bf16[768,1024]{1,0:T(8,128)(2,1)} %act_ref.1, bf16[768,1024]{1,0:T(8,128)(2,1)} %cot_ref.1), custom_call_target="tpu_custom_call" | custom-call | tf_op jit(solution)/shard_map/grad_theirs/pallas_call | solution.py:225
  4.5 8.8 %collective-permute-start = (bf16[4,4,256,128]{3,2,1,0:T(8,128)(2,1)}, bf16[4,4,256,128]{3,2,1,0:T(8,128)(2,1)S(1)}, u32[]{:S(2)}, u32[]{:S(2)}) collective-permute-start(bf16[4,4,256,128]{3,2,1,0:T(8,128)(2,1)} %grad_theirs.1), channel_id=1, source_target_pairs={{0,1},{1,0},{2,3},{3,2},{4,5},{5,4},{6,7},{7,6},{8,9},{9,8},{10,11... | collective-permute-start | bytes 3145736 | tf_op jit(solution)/shard_map/ppermute | solution.py:237
  13.3 2.5 %collective-permute-done.other_ref = bf16[4,4,256,128]{3,2,1,0:T(8,128)(2,1)S(1)} collective-permute-done((bf16[4,4,256,128]{3,2,1,0:T(8,128)(2,1)}, bf16[4,4,256,128]{3,2,1,0:T(8,128)(2,1)S(1)}, u32[]{:S(2)}, u32[]{:S(2)}) %collective-permute-start) | collective-permute-done | bytes 1048608 | tf_op jit(solution)/shard_map/ppermute | solution.py:237
  15.8 0.0 copy-done
  15.8 0.0 copy-done.1
  15.8 0.0 copy-done.2
  15.8 1.1 grad_mine.1
  16.8 0.0 copy-start.3
  16.9 19.8 %all_to_all.20.terms_ref = bf16[16,288,128]{2,1,0:T(8,128)(2,1)S(1)} all-to-all(bf16[16,288,128]{2,1,0:T(8,128)(2,1)S(1)} %grad_mine.1), channel_id=1, replica_groups=mesh['x'=4,'yl'=2,'z4'=4,'zp'=2,'yh'=4,'core'=2] {'x','yl','zp'}, dimensions={0} | all-to-all | bytes 2359296 | tf_op jit(solution)/shard_map/all_to_all | solution.py:218
  36.7 0.0 copy-done.3
  36.7 0.7 reduce.1
  37.4 25.7 %all_to_all.21.parts_ref = bf16[16,80,128]{2,1,0:T(8,128)(2,1)S(1)} all-to-all(bf16[16,80,128]{2,1,0:T(8,128)(2,1)S(1)} %reduce.1), channel_id=1, replica_groups=mesh['x'=4,'yl'=2,'z4'=4,'zp'=2,'yh'=4,'core'=2] {'z4','yh'}, dimensions={0} | all-to-all | bytes 655360 | tf_op jit(solution)/shard_map/all_to_all | solution.py:218
  63.1 0.7 total.1
  63.8 1.9 %collective-permute-start.1 = (bf16[2,16,32,128]{3,2,1,0:T(8,128)(2,1)S(1)}, bf16[2,16,32,128]{3,2,1,0:T(8,128)(2,1)S(1)}, u32[]{:S(2)}, u32[]{:S(2)}) collective-permute-start(bf16[2,16,32,128]{3,2,1,0:T(8,128)(2,1)S(1)} %get-tuple-element.6), channel_id=1, source_target_pairs={{0,64},{64,0},{1,65},{65,1},{2,66},{66,2},{3,67},{67,3},{4,68},{68... | collective-permute-start | bytes 786440 | tf_op jit(solution)/shard_map/ppermute | solution.py:237
  65.7 8.3 %all-to-all-start.2 = ((bf16[64,16,128]{2,1,0:T(8,128)(2,1)}), bf16[64,16,128]{2,1,0:T(8,128)(2,1)S(1)}, u32[]{:S(2)}, u32[]{:S(2)}) async-start(bf16[64,16,128]{2,1,0:T(8,128)(2,1)} %get-tuple-element.7), calls=%async_computation.2 | async-start | bytes 524288 | tf_op jit(solution)/shard_map/all_to_all | solution.py:218
  74.0 0.0 collective-permute-done.1
  74.1 3.2 %collective-permute-start.2 = (bf16[4,16,32,128]{3,2,1,0:T(8,128)(2,1)S(1)}, bf16[4,16,32,128]{3,2,1,0:T(8,128)(2,1)S(1)}, u32[]{:S(2)}, u32[]{:S(2)}) collective-permute-start(bf16[4,16,32,128]{3,2,1,0:T(8,128)(2,1)S(1)} %constant_dynamic-update-slice_fusion.stats_here_ref), channel_id=1, source_target_pairs={{0,1},{1,0},{2,3},{3,2},{4,5},{5,4},{6,7},{7,6},{8,9},{9,8},{10,11... | collective-permute-start | bytes 1572872 | tf_op jit(solution)/shard_map/ppermute | solution.py:237
  77.3 9.1 %all-to-all-done.2.tiles_here_ref = bf16[64,16,128]{2,1,0:T(8,128)(2,1)S(1)} async-done(((bf16[64,16,128]{2,1,0:T(8,128)(2,1)}), bf16[64,16,128]{2,1,0:T(8,128)(2,1)S(1)}, u32[]{:S(2)}, u32[]{:S(2)}) %all-to-all-start.2) | async-done | bytes 262176 | tf_op jit(solution)/shard_map/all_to_all | solution.py:218
  86.4 5.3 %collective-permute-start.3 = (bf16[64,16,128]{2,1,0:T(8,128)(2,1)S(1)}, bf16[64,16,128]{2,1,0:T(8,128)(2,1)S(1)}, u32[]{:S(2)}, u32[]{:S(2)}) collective-permute-start(bf16[64,16,128]{2,1,0:T(8,128)(2,1)S(1)} %all-to-all-done.2.tiles_here_ref), channel_id=1, source_target_pairs={{0,1},{1,0},{2,3},{3,2},{4,5},{5,4},{6,7},{7,6},{8,9},{9,8},{10,11... | collective-permute-start | bytes 786440 | tf_op jit(solution)/shard_map/ppermute | solution.py:237
  91.7 0.0 collective-permute-done.2.stats_there_ref
  91.8 0.2 unpack.1.stats
  92.0 0.9 collective-permute-done.3.tiles_there_ref
  92.9 6.4 %root.1 = f32[4,24,512]{2,1,0:T(8,128)S(1)} custom-call(s32[1]{0:T(128)} %bitcast.device_ref, s32[8]{0:T(128)S(1)} %copy-done.3, f32[2,512,512]{2,1,0:T(8,128)S(1)} %unpack.1.stats, bf16[64,16,128]{2,1,0:T(8,128)(2,1)S(1)} %all-to-all-done.2.tiles_here_ref, bf16[64,16,128]{2,1,0:T(8,128)(2,1)S(1)} %collective-permute-done.3.tiles_there_ref), custom_call_target="tpu_custom_call" | custom-call | tf_op jit(solution)/shard_map/root/pallas_call | solution.py:225
  99.2 7.8 %all_to_all.22.pieces_ref = f32[4,24,512]{2,1,0:T(8,128)S(1)} all-to-all(f32[4,24,512]{2,1,0:T(8,128)S(1)} %root.1), channel_id=1, replica_groups=mesh['x'=4,'yl'=2,'z4'=4,'zp'=2,'yh'=4,'core'=2] {'x'}, dimensions={0} | all-to-all | bytes 393216 | tf_op jit(solution)/shard_map/all_to_all | solution.py:218
  107.0 1.2 %join.1 = (f32[8,512]{1,0:T(8,128)}, f32[16,1024]{1,0:T(8,128)}) custom-call(s32[1]{0:T(128)} %bitcast.device_ref, s32[8]{0:T(128)S(1)} %copy-done.3, f32[8,512]{1,0:T(8,128)S(1)} %bitcast.4, f32[4,24,512]{2,1,0:T(8,128)S(1)} %all_to_all.22.pieces_ref), custom_call_target="tpu_custom_call" | custom-call | tf_op jit(solution)/shard_map/join/pallas_call | solution.py:225
  (2 shorter events, 0.1 us)
Async XLA Ops:
  0.6 15.1 %copy-start = (bf16[768,1024]{1,0:T(8,128)(2,1)S(1)}, bf16[768,1024]{1,0:T(8,128)(2,1)}, u32[]{:S(2)}) copy-start(bf16[768,1024]{1,0:T(8,128)(2,1)} %act_ref.1) | copy-start | bytes 4718596
  0.7 15.1 %copy-start.1 = (bf16[768,1024]{1,0:T(8,128)(2,1)S(1)}, bf16[768,1024]{1,0:T(8,128)(2,1)}, u32[]{:S(2)}) copy-start(bf16[768,1024]{1,0:T(8,128)(2,1)} %cot_ref.1) | copy-start | bytes 4718596
  0.7 15.1 %copy-start.2 = (f32[1,8,512]{2,1,0:T(8,128)S(1)}, f32[1,8,512]{2,1,0:T(8,128)}, u32[]{:S(2)}) copy-start(f32[1,8,512]{2,1,0:T(8,128)} %param.6) | copy-start | bytes 49156
  4.5 11.3 %collective-permute-start = (bf16[4,4,256,128]{3,2,1,0:T(8,128)(2,1)}, bf16[4,4,256,128]{3,2,1,0:T(8,128)(2,1)S(1)}, u32[]{:S(2)}, u32[]{:S(2)}) collective-permute-start(bf16[4,4,256,128]{3,2,1,0:T(8,128)(2,1)} %grad_theirs.1), channel_id=1, source_target_pairs={{0,1},{1,0},{2,3},{3,2},{4,5},{5,4},{6,7},{7,6},{8,9},{9,8},{10,11... | collective-permute-start | bytes 3145736 | tf_op jit(solution)/shard_map/ppermute | solution.py:237
  16.8 19.8 %copy-start.3 = (s32[8]{0:T(128)S(1)}, s32[8]{0:T(128)}, u32[]{:S(2)}) copy-start(s32[8]{0:T(128)} %owner_ref.5) | copy-start | bytes 100
  63.8 10.2 %collective-permute-start.1 = (bf16[2,16,32,128]{3,2,1,0:T(8,128)(2,1)S(1)}, bf16[2,16,32,128]{3,2,1,0:T(8,128)(2,1)S(1)}, u32[]{:S(2)}, u32[]{:S(2)}) collective-permute-start(bf16[2,16,32,128]{3,2,1,0:T(8,128)(2,1)S(1)} %get-tuple-element.6), channel_id=1, source_target_pairs={{0,64},{64,0},{1,65},{65,1},{2,66},{66,2},{3,67},{67,3},{4,68},{68... | collective-permute-start | bytes 786440 | tf_op jit(solution)/shard_map/ppermute | solution.py:237
  65.7 20.7 %all-to-all-start.2 = ((bf16[64,16,128]{2,1,0:T(8,128)(2,1)}), bf16[64,16,128]{2,1,0:T(8,128)(2,1)S(1)}, u32[]{:S(2)}, u32[]{:S(2)}) async-start(bf16[64,16,128]{2,1,0:T(8,128)(2,1)} %get-tuple-element.7), calls=%async_computation.2 | async-start | bytes 524288 | tf_op jit(solution)/shard_map/all_to_all | solution.py:218
  74.1 17.7 %collective-permute-start.2 = (bf16[4,16,32,128]{3,2,1,0:T(8,128)(2,1)S(1)}, bf16[4,16,32,128]{3,2,1,0:T(8,128)(2,1)S(1)}, u32[]{:S(2)}, u32[]{:S(2)}) collective-permute-start(bf16[4,16,32,128]{3,2,1,0:T(8,128)(2,1)S(1)} %constant_dynamic-update-slice_fusion.stats_here_ref), channel_id=1, source_target_pairs={{0,1},{1,0},{2,3},{3,2},{4,5},{5,4},{6,7},{7,6},{8,9},{9,8},{10,11... | collective-permute-start | bytes 1572872 | tf_op jit(solution)/shard_map/ppermute | solution.py:237
  86.4 6.4 %collective-permute-start.3 = (bf16[64,16,128]{2,1,0:T(8,128)(2,1)S(1)}, bf16[64,16,128]{2,1,0:T(8,128)(2,1)S(1)}, u32[]{:S(2)}, u32[]{:S(2)}) collective-permute-start(bf16[64,16,128]{2,1,0:T(8,128)(2,1)S(1)} %all-to-all-done.2.tiles_here_ref), channel_id=1, source_target_pairs={{0,1},{1,0},{2,3},{3,2},{4,5},{5,4},{6,7},{7,6},{8,9},{9,8},{10,11... | collective-permute-start | bytes 786440 | tf_op jit(solution)/shard_map/ppermute | solution.py:237

commit v6 on v5

--- a/solution.py
+++ b/solution.py
@@ -44,7 +44,7 @@
     return device // (PAIR * SHARDS), device // SHARDS % PAIR, device // 8 % PAIR, device % CORES
 
 
-def theirs_kernel(device_ref, act_hbm, cot_hbm, out_ref, act_ref, cot_ref, sems):
+def theirs_kernel(device_ref, act_hbm, cot_hbm, out_hbm, act_ref, cot_ref, out_ref, sems, out_sems):
     half = 1 - device_ref[0] % CORES
     copies = []
     for row in range(2):
@@ -59,14 +59,22 @@
         )
     for number in (0, 2, 3, 1):
         copies[number].start()
+    sent = []
     for row in range(2):
         copies[row].wait()
         for col in range(COLS):
             if row == 0:
                 copies[2 + col].wait()
+            block = row * COLS + col
             term = half_term(act_ref[row], cot_ref[col]).astype(bf16)
             for lane in range(QUADS):
-                out_ref[row * COLS + col, lane] = term[:, lane * LANES : (lane + 1) * LANES]
+                out_ref[block, lane] = term[:, lane * LANES : (lane + 1) * LANES]
+            sent.append(
+                pltpu.make_async_copy(out_ref.at[block], out_hbm.at[block], out_sems.at[block])
+            )
+            sent[-1].start()
+    for copy in sent:
+        copy.wait()
 
 
 def half_term(act, cot):
@@ -90,46 +98,42 @@
 
 
 def reduce_kernel(device_ref, owner_ref, terms_ref, out_ref):
-    block, side, _, _ = near_place(device_ref[0])
-    first = owner_ref[side * BLOCKS + block] * PAIR
-    stats = [terms_ref[first + low, HALF:] for low in range(PAIR)]
+    block = near_place(device_ref[0])[0]
+    firsts = [owner_ref[side * BLOCKS + block] * PAIR for side in range(2)]
+    stats = [terms_ref[first + low, HALF:] for first in firsts for low in range(PAIR)]
     for part in range(FAR):
         rows = slice(part * TILE, (part + 1) * TILE)
         total = terms_ref[0, rows].astype(f32)
         for source in range(1, XS * QUADS):
             total += terms_ref[source, rows].astype(f32)
         out_ref[part, :TILE] = total.astype(bf16)
-        for low in range(PAIR):
-            out_ref[part, TILE + low * STATS : TILE + (low + 1) * STATS] = stats[low]
-
-
-def total_kernel(parts_ref, gradient_ref, stats_ref):
+        for quad in range(QUADS):
+            out_ref[part, TILE + quad * STATS : TILE + (quad + 1) * STATS] = stats[quad]
+
+
+def total_kernel(parts_ref, gradient_ref):
     total = parts_ref[0, :TILE].astype(f32)
     for part in range(1, FAR):
         total += parts_ref[part, :TILE].astype(f32)
     gradient = total.astype(bf16)
     for part in range(PARTS):
         gradient_ref[part] = gradient
-    for part in range(FAR):
-        for low in range(PAIR):
-            place = slice(TILE + low * STATS, TILE + (low + 1) * STATS)
-            stats_ref[low, part] = parts_ref[part, place]
-
-
-def unpack_kernel(device_ref, stats_here_ref, stats_there_ref, stats):
-    _, near_y, _, core = near_place(device_ref[0])
-    for stats_ref, at in ((stats_here_ref, core), (stats_there_ref, 1 - core)):
+
+
+def unpack_kernel(device_ref, parts_here_ref, parts_there_ref, stats):
+    core = device_ref[0] % CORES
+    for parts_ref, at in ((parts_here_ref, core), (parts_there_ref, 1 - core)):
         for quad in range(QUADS):
-            side = near_y if quad // PAIR == 0 else 1 - near_y
-            low = quad % PAIR
+            side, low = divmod(quad, PAIR)
             for part in range(FAR):
                 high, column = divmod(part, 4)
-                value = stats_ref[quad, part].astype(f32)
+                value = parts_ref[part, TILE + quad * STATS : TILE + (quad + 1) * STATS].astype(f32)
                 shard = (high * PAIR + low) * 8 + column * CORES + at
                 place = pl.ds(pl.multiple_of(shard * OWN_ROWS, OWN_ROWS), OWN_ROWS)
                 for lane in range(BLOCK // LANES):
                     columns = slice(lane * LANES, (lane + 1) * LANES)
                     stats[side, place, columns] = value[lane * OWN_ROWS : (lane + 1) * OWN_ROWS]
+
 
 def product(left, right):
     return jnp.dot(left.astype(bf16), right.astype(bf16), preferred_element_type=f32)
@@ -226,7 +230,7 @@
         kernel,
         out_shape=outs,
         in_specs=[smem if array.ndim == 1 else rest for array in arrays],
-        out_specs=tuple(vmem for _ in outs) if isinstance(outs, tuple) else vmem,
+        out_specs=tuple(rest for _ in outs) if isinstance(outs, tuple) else rest,
         scratch_shapes=list(scratch),
         compiler_params=pltpu.CompilerParams(vmem_limit_bytes=limit),
         name=name,
@@ -251,7 +255,9 @@
         scratch=[
             pltpu.VMEM((2, tokens, HALF), bf16),
             pltpu.VMEM((COLS, tokens, BLOCK), bf16),
+            pltpu.VMEM((BLOCKS, QUADS, HALF, LANES), bf16),
             pltpu.SemaphoreType.DMA((4,)),
+            pltpu.SemaphoreType.DMA((BLOCKS,)),
         ],
         limit=GRAD_LIMIT,
     )
@@ -264,21 +270,13 @@
     reduced = call(
         reduce_kernel,
         "reduce",
-        array((FAR, TILE + PAIR * STATS, LANES), bf16),
+        array((FAR, TILE + QUADS * STATS, LANES), bf16),
         (device, owner, exchange(packed, NEAR_AXES)),
     )
-    gradient, stats = call(
-        total_kernel,
-        "total",
-        (array((PARTS, TILE, LANES), bf16), array((PAIR, FAR, STATS, LANES), bf16)),
-        (exchange(reduced, FAR_AXES),),
-    )
-    stats = jnp.concatenate([stats, swap(stats, "yl")])
+    parts = exchange(reduced, FAR_AXES)
+    gradient = call(total_kernel, "total", array((PARTS, TILE, LANES), bf16), (parts,))
     rows = call(
-        unpack_kernel,
-        "unpack",
-        array((2, BLOCK, BLOCK), f32),
-        (device, stats, swap(stats, "core")),
+        unpack_kernel, "unpack", array((2, BLOCK, BLOCK), f32), (device, parts, swap(parts, "core"))
     )
     tiles = exchange(gradient, PLANE)
     pieces = call(

time: 109 us -> 111 us (1.018)
  blocking collectives: 53.3 us -> 60.4 us
  starting transfers between devices: 27.5 us -> 23.2 us
    all_to_all x3, blocking collectives: 53.3 us -> 60.4 us  [exchange(): return lax.all_to_all(value, axes, split_axis=0, concat_axis=0, tiled=True)]
    all_to_all x1, starting transfers between devices: 8.26 us -> 6.1 us  [exchange(): return lax.all_to_all(value, axes, split_axis=0, concat_axis=0, tiled=True)]
    ppermute x4 -> x3, starting transfers between devices: 19.2 us -> 17.1 us  [swap(): return lax.ppermute(value, axis, [(0, 1), (1, 0)])]
    ppermute x4 -> x3, waiting for transfers between devices: 3.37 us -> 3.45 us  [swap(): return lax.ppermute(value, axis, [(0, 1), (1, 0)])]
  transfers between devices with their start and end apart: 5 -> 4, of which waited for: 3 -> 3; matrix products, arithmetic and copies ran while one was open for 0% -> 0% of each run, Pallas kernels for 0% -> 0%
where the time goes in v6:
time: 111 us
  blocking collectives  60.4 us (54%)
  starting transfers between devices  23.2 us (21%)
  Pallas kernels  13.8 us (12%)
  waiting for transfers between devices  12.8 us (12%)
    all_to_all x3, blocking collectives, exchange(): return lax.all_to_all(value, axes, split_axis=0, concat_axis=0, tiled=True)  60.4 us
    ppermute x3, starting transfers between devices, swap(): return lax.ppermute(value, axis, [(0, 1), (1, 0)])  17.1 us
    pallas_call x7, Pallas kernels, call(): pl.pallas_call(kernel, out_shape=outs, in_specs=[smem if array.ndim == 1...  13.8 us
    all_to_all x1, waiting for transfers between devices, exchange(): return lax.all_to_all(value, axes, split_axis=0, concat_axis=0, tiled=True)  9.36 us
    all_to_all x1, starting transfers between devices, exchange(): return lax.all_to_all(value, axes, split_axis=0, concat_axis=0, tiled=True)  6.1 us
    ppermute x3, waiting for transfers between devices, swap(): return lax.ppermute(value, axis, [(0, 1), (1, 0)])  3.45 us
  transfers between devices with their start and end apart: 4, of which 3 were waited for; matrix products, arithmetic and copies ran while one was open for 0% of the time, Pallas kernels for 0%

profile of v6, /device:TPU:1, one launch (start us, length us, event | category | flops | bytes accessed | tf_op | source)
XLA Modules:
  0.0 110.9 jit_solution(305167638019784028)
XLA Ops:
  0.6 0.0 copy-start
  0.7 0.0 copy-start.1
  0.7 0.0 copy-start.2
  0.7 3.6 %grad_theirs.1 = bf16[4,4,256,128]{3,2,1,0:T(8,128)(2,1)} custom-call(s32[1]{0:T(128)} %bitcast.device_ref, bf16[768,1024]{1,0:T(8,128)(2,1)} %act_ref.1, bf16[768,1024]{1,0:T(8,128)(2,1)} %cot_ref.1), custom_call_target="tpu_custom_call" | custom-call | tf_op jit(solution)/shard_map/grad_theirs/pallas_call | solution.py:229
  4.3 8.8 %collective-permute-start = (bf16[4,4,256,128]{3,2,1,0:T(8,128)(2,1)}, bf16[4,4,256,128]{3,2,1,0:T(8,128)(2,1)S(1)}, u32[]{:S(2)}, u32[]{:S(2)}) collective-permute-start(bf16[4,4,256,128]{3,2,1,0:T(8,128)(2,1)} %grad_theirs.1), channel_id=1, source_target_pairs={{0,1},{1,0},{2,3},{3,2},{4,5},{5,4},{6,7},{7,6},{8,9},{9,8},{10,11... | collective-permute-start | bytes 3145736 | tf_op jit(solution)/shard_map/ppermute | solution.py:241
  13.1 2.5 %collective-permute-done.other_ref = bf16[4,4,256,128]{3,2,1,0:T(8,128)(2,1)S(1)} collective-permute-done((bf16[4,4,256,128]{3,2,1,0:T(8,128)(2,1)}, bf16[4,4,256,128]{3,2,1,0:T(8,128)(2,1)S(1)}, u32[]{:S(2)}, u32[]{:S(2)}) %collective-permute-start) | collective-permute-done | bytes 1048608 | tf_op jit(solution)/shard_map/ppermute | solution.py:241
  15.5 0.0 copy-done
  15.5 0.0 copy-done.1
  15.5 0.0 copy-done.2
  15.5 1.1 grad_mine.1
  16.6 0.0 copy-start.3
  16.6 19.8 %all_to_all.20.terms_ref = bf16[16,288,128]{2,1,0:T(8,128)(2,1)S(1)} all-to-all(bf16[16,288,128]{2,1,0:T(8,128)(2,1)S(1)} %grad_mine.1), channel_id=1, replica_groups=mesh['x'=4,'yl'=2,'z4'=4,'zp'=2,'yh'=4,'core'=2] {'x','yl','zp'}, dimensions={0} | all-to-all | bytes 2359296 | tf_op jit(solution)/shard_map/all_to_all | solution.py:222
  36.4 0.0 copy-done.3
  36.4 0.7 reduce.1
  37.2 32.8 %all_to_all.21.parts_here_ref.parts_ref = bf16[16,144,128]{2,1,0:T(8,128)(2,1)S(1)} all-to-all(bf16[16,144,128]{2,1,0:T(8,128)(2,1)S(1)} %reduce.1), channel_id=1, replica_groups=mesh['x'=4,'yl'=2,'z4'=4,'zp'=2,'yh'=4,'core'=2] {'z4','yh'}, dimensions={0} | all-to-all | bytes 1179648 | tf_op jit(solution)/shard_map/all_to_all | solution.py:222
  70.0 0.7 total.1
  70.7 6.1 %all-to-all-start.2 = ((bf16[64,16,128]{2,1,0:T(8,128)(2,1)}), bf16[64,16,128]{2,1,0:T(8,128)(2,1)S(1)}, u32[]{:S(2)}, u32[]{:S(2)}) async-start(bf16[64,16,128]{2,1,0:T(8,128)(2,1)} %total.1), calls=%async_computation.2 | async-start | bytes 524288 | tf_op jit(solution)/shard_map/all_to_all | solution.py:222
  76.8 3.0 %collective-permute-start.1 = (bf16[16,144,128]{2,1,0:T(8,128)(2,1)S(1)}, bf16[16,144,128]{2,1,0:T(8,128)(2,1)S(1)}, u32[]{:S(2)}, u32[]{:S(2)}) collective-permute-start(bf16[16,144,128]{2,1,0:T(8,128)(2,1)S(1)} %all_to_all.21.parts_here_ref.parts_ref), channel_id=1, source_target_pairs={{0,1},{1,0},{2,3},{3,2},{4,5},{5,4},{6,7},{7,6},{8,9},{9,8},{10,11... | collective-permute-start | bytes 1769480 | tf_op jit(solution)/shard_map/ppermute | solution.py:241
  79.9 9.4 %all-to-all-done.2.tiles_here_ref = bf16[64,16,128]{2,1,0:T(8,128)(2,1)S(1)} async-done(((bf16[64,16,128]{2,1,0:T(8,128)(2,1)}), bf16[64,16,128]{2,1,0:T(8,128)(2,1)S(1)}, u32[]{:S(2)}, u32[]{:S(2)}) %all-to-all-start.2) | async-done | bytes 262176 | tf_op jit(solution)/shard_map/all_to_all | solution.py:222
  89.2 5.3 %collective-permute-start.2 = (bf16[64,16,128]{2,1,0:T(8,128)(2,1)S(1)}, bf16[64,16,128]{2,1,0:T(8,128)(2,1)S(1)}, u32[]{:S(2)}, u32[]{:S(2)}) collective-permute-start(bf16[64,16,128]{2,1,0:T(8,128)(2,1)S(1)} %all-to-all-done.2.tiles_here_ref), channel_id=1, source_target_pairs={{0,1},{1,0},{2,3},{3,2},{4,5},{5,4},{6,7},{7,6},{8,9},{9,8},{10,11... | collective-permute-start | bytes 786440 | tf_op jit(solution)/shard_map/ppermute | solution.py:241
  94.5 0.0 collective-permute-done.1.parts_there_ref
  94.6 0.1 unpack.1.stats
  94.7 1.0 collective-permute-done.2.tiles_there_ref
  95.7 6.3 %root.1 = f32[4,24,512]{2,1,0:T(8,128)S(1)} custom-call(s32[1]{0:T(128)} %bitcast.device_ref, s32[8]{0:T(128)S(1)} %copy-done.3, f32[2,512,512]{2,1,0:T(8,128)S(1)} %unpack.1.stats, bf16[64,16,128]{2,1,0:T(8,128)(2,1)S(1)} %all-to-all-done.2.tiles_here_ref, bf16[64,16,128]{2,1,0:T(8,128)(2,1)S(1)} %collective-permute-done.2.tiles_there_ref), custom_call_target="tpu_custom_call" | custom-call | tf_op jit(solution)/shard_map/root/pallas_call | solution.py:229
  102.0 7.7 %all_to_all.22.pieces_ref = f32[4,24,512]{2,1,0:T(8,128)S(1)} all-to-all(f32[4,24,512]{2,1,0:T(8,128)S(1)} %root.1), channel_id=1, replica_groups=mesh['x'=4,'yl'=2,'z4'=4,'zp'=2,'yh'=4,'core'=2] {'x'}, dimensions={0} | all-to-all | bytes 393216 | tf_op jit(solution)/shard_map/all_to_all | solution.py:222
  109.7 1.2 %join.1 = (f32[8,512]{1,0:T(8,128)}, f32[16,1024]{1,0:T(8,128)}) custom-call(s32[1]{0:T(128)} %bitcast.device_ref, s32[8]{0:T(128)S(1)} %copy-done.3, f32[8,512]{1,0:T(8,128)S(1)} %bitcast.4, f32[4,24,512]{2,1,0:T(8,128)S(1)} %all_to_all.22.pieces_ref), custom_call_target="tpu_custom_call" | custom-call | tf_op jit(solution)/shard_map/join/pallas_call | solution.py:229
Async XLA Ops:
  0.6 14.9 %copy-start = (bf16[768,1024]{1,0:T(8,128)(2,1)S(1)}, bf16[768,1024]{1,0:T(8,128)(2,1)}, u32[]{:S(2)}) copy-start(bf16[768,1024]{1,0:T(8,128)(2,1)} %act_ref.1) | copy-start | bytes 4718596
  0.7 14.9 %copy-start.1 = (bf16[768,1024]{1,0:T(8,128)(2,1)S(1)}, bf16[768,1024]{1,0:T(8,128)(2,1)}, u32[]{:S(2)}) copy-start(bf16[768,1024]{1,0:T(8,128)(2,1)} %cot_ref.1) | copy-start | bytes 4718596
  0.7 14.9 %copy-start.2 = (f32[1,8,512]{2,1,0:T(8,128)S(1)}, f32[1,8,512]{2,1,0:T(8,128)}, u32[]{:S(2)}) copy-start(f32[1,8,512]{2,1,0:T(8,128)} %param.6) | copy-start | bytes 49156
  4.3 11.3 %collective-permute-start = (bf16[4,4,256,128]{3,2,1,0:T(8,128)(2,1)}, bf16[4,4,256,128]{3,2,1,0:T(8,128)(2,1)S(1)}, u32[]{:S(2)}, u32[]{:S(2)}) collective-permute-start(bf16[4,4,256,128]{3,2,1,0:T(8,128)(2,1)} %grad_theirs.1), channel_id=1, source_target_pairs={{0,1},{1,0},{2,3},{3,2},{4,5},{5,4},{6,7},{7,6},{8,9},{9,8},{10,11... | collective-permute-start | bytes 3145736 | tf_op jit(solution)/shard_map/ppermute | solution.py:241
  16.6 19.8 %copy-start.3 = (s32[8]{0:T(128)S(1)}, s32[8]{0:T(128)}, u32[]{:S(2)}) copy-start(s32[8]{0:T(128)} %owner_ref.5) | copy-start | bytes 100
  70.7 18.5 %all-to-all-start.2 = ((bf16[64,16,128]{2,1,0:T(8,128)(2,1)}), bf16[64,16,128]{2,1,0:T(8,128)(2,1)S(1)}, u32[]{:S(2)}, u32[]{:S(2)}) async-start(bf16[64,16,128]{2,1,0:T(8,128)(2,1)} %total.1), calls=%async_computation.2 | async-start | bytes 524288 | tf_op jit(solution)/shard_map/all_to_all | solution.py:222
  76.8 17.7 %collective-permute-start.1 = (bf16[16,144,128]{2,1,0:T(8,128)(2,1)S(1)}, bf16[16,144,128]{2,1,0:T(8,128)(2,1)S(1)}, u32[]{:S(2)}, u32[]{:S(2)}) collective-permute-start(bf16[16,144,128]{2,1,0:T(8,128)(2,1)S(1)} %all_to_all.21.parts_here_ref.parts_ref), channel_id=1, source_target_pairs={{0,1},{1,0},{2,3},{3,2},{4,5},{5,4},{6,7},{7,6},{8,9},{9,8},{10,11... | collective-permute-start | bytes 1769480 | tf_op jit(solution)/shard_map/ppermute | solution.py:241
  89.2 6.5 %collective-permute-start.2 = (bf16[64,16,128]{2,1,0:T(8,128)(2,1)S(1)}, bf16[64,16,128]{2,1,0:T(8,128)(2,1)S(1)}, u32[]{:S(2)}, u32[]{:S(2)}) collective-permute-start(bf16[64,16,128]{2,1,0:T(8,128)(2,1)S(1)} %all-to-all-done.2.tiles_here_ref), channel_id=1, source_target_pairs={{0,1},{1,0},{2,3},{3,2},{4,5},{5,4},{6,7},{7,6},{8,9},{9,8},{10,11... | collective-permute-start | bytes 786440 | tf_op jit(solution)/shard_map/ppermute | solution.py:241

commit v7 on v6

--- a/solution.py
+++ b/solution.py
@@ -23,6 +23,7 @@
 OUT_ROWS = 16
 OWN_ROWS = 8
 STATS = 32
+GROUPS = 5
 TILE = 16
 f32 = jnp.float32
 bf16 = jnp.bfloat16
@@ -97,18 +98,36 @@
                 out_ref[block * QUADS + lane, HALF:] = stats
 
 
+def sent_groups(row_block):
+    near = [(side, (row_block + step) % 4) for side in range(2) for step in range(2)]
+    return near + [(row_block // 2, (row_block + 2) % 4)]
+
+
 def reduce_kernel(device_ref, owner_ref, terms_ref, out_ref):
     block = near_place(device_ref[0])[0]
-    firsts = [owner_ref[side * BLOCKS + block] * PAIR for side in range(2)]
-    stats = [terms_ref[first + low, HALF:] for first in firsts for low in range(PAIR)]
+    row_block = device_ref[0] % SHARDS // 16
+    lanes = []
+    for side in range(2):
+        first = owner_ref[side * BLOCKS + block] * PAIR
+        low, high = (terms_ref[first + chip, HALF:].astype(f32) for chip in range(PAIR))
+        rows = [slice(lane * OWN_ROWS, (lane + 1) * OWN_ROWS) for lane in range(4)]
+        lanes.append([jnp.concatenate([low[place], high[place]], axis=0) for place in rows])
+    stats = []
+    for group in range(GROUPS):
+        chosen = None
+        for number in range(4):
+            side, lane = sent_groups(number)[group]
+            here = lanes[side][lane]
+            chosen = here if chosen is None else jnp.where(row_block == number, here, chosen)
+        stats.append(chosen.astype(bf16))
     for part in range(FAR):
         rows = slice(part * TILE, (part + 1) * TILE)
         total = terms_ref[0, rows].astype(f32)
         for source in range(1, XS * QUADS):
             total += terms_ref[source, rows].astype(f32)
         out_ref[part, :TILE] = total.astype(bf16)
-        for quad in range(QUADS):
-            out_ref[part, TILE + quad * STATS : TILE + (quad + 1) * STATS] = stats[quad]
+        for group in range(GROUPS):
+            out_ref[part, TILE * (group + 1) : TILE * (group + 2)] = stats[group]
 
 
 def total_kernel(parts_ref, gradient_ref):
@@ -123,20 +142,40 @@
 def unpack_kernel(device_ref, parts_here_ref, parts_there_ref, stats):
     core = device_ref[0] % CORES
     for parts_ref, at in ((parts_here_ref, core), (parts_there_ref, 1 - core)):
-        for quad in range(QUADS):
-            side, low = divmod(quad, PAIR)
-            for part in range(FAR):
-                high, column = divmod(part, 4)
-                value = parts_ref[part, TILE + quad * STATS : TILE + (quad + 1) * STATS].astype(f32)
-                shard = (high * PAIR + low) * 8 + column * CORES + at
-                place = pl.ds(pl.multiple_of(shard * OWN_ROWS, OWN_ROWS), OWN_ROWS)
-                for lane in range(BLOCK // LANES):
+        for part in range(FAR):
+            row_block, column = divmod(part, 4)
+            for group, (side, lane) in enumerate(sent_groups(row_block)):
+                value = parts_ref[part, TILE * (group + 1) : TILE * (group + 2)].astype(f32)
+                for low in range(PAIR):
+                    shard = (row_block * PAIR + low) * 8 + column * CORES + at
+                    place = pl.ds(pl.multiple_of(shard * OWN_ROWS, OWN_ROWS), OWN_ROWS)
                     columns = slice(lane * LANES, (lane + 1) * LANES)
-                    stats[side, place, columns] = value[lane * OWN_ROWS : (lane + 1) * OWN_ROWS]
+                    stats[side, place, columns] = value[low * OWN_ROWS : (low + 1) * OWN_ROWS]
+    for row_block in range(4):
+        for side, lane in sent_groups(row_block):
+            if lane != row_block:
+                rows = slice(row_block * LANES, (row_block + 1) * LANES)
+                columns = slice(lane * LANES, (lane + 1) * LANES)
+                stats[side, columns, rows] = stats[side, rows, columns].T
 
 
 def product(left, right):
     return jnp.dot(left.astype(bf16), right.astype(bf16), preferred_element_type=f32)
+
+
+def symmetric(left, right, dims=((1,), (0,))):
+    left, right = left[...].astype(bf16), right[...].astype(bf16)
+    (left_dim,), (right_dim,) = dims
+
+    def part(rows, columns):
+        first = left[rows] if left_dim == 1 else left[:, rows]
+        second = right[:, columns] if right_dim == 0 else right[columns]
+        return lax.dot_general(first, second, (dims, ((), ())), preferred_element_type=f32)
+
+    low, high = slice(0, HALF), slice(HALF, BLOCK)
+    top = part(low, slice(0, BLOCK))
+    corner = part(high, high)
+    return jnp.concatenate([top, jnp.concatenate([top[:, HALF:].T, corner], axis=1)], axis=0)
 
 
 def newton(stats, gram):
@@ -145,19 +184,19 @@
     scales = [jnp.sqrt(jnp.sum(value * value, keepdims=True) + 1e-06) for value in updated]
 
     def step(state):
-        low = [2.0 * state[side] - product(state[side], state[side]) for side in sides]
-        high = [2.0 * low[side] - product(low[side], low[side]) for side in sides]
-        return [1.25**4 * (state[side] - product(high[side], state[side])) for side in sides]
+        low = [2.0 * state[side] - symmetric(state[side], state[side]) for side in sides]
+        high = [2.0 * low[side] - symmetric(low[side], low[side]) for side in sides]
+        return [1.25**4 * (state[side] - symmetric(high[side], state[side])) for side in sides]
 
     first = [updated[side] * (0.2 / scales[side]) for side in sides]
     second = step(first)
     return first, second, step(second)
 
 
-def root_rows(first, second, third, diagonal):
+def root_rows(first, second, third, diagonal, times=product):
     own_first, own_second, own_third = first
-    both = own_first + own_second - product(own_first, second)
-    return 1.25**3 * (diagonal - (both + own_third - product(both, third)))
+    both = own_first + own_second - times(own_first, second)
+    return 1.25**3 * (diagonal - (both + own_third - times(both, third)))
 
 
 def root_kernel(
@@ -179,12 +218,8 @@
             lane, group = divmod(part, FAR)
             place = pl.ds(pl.multiple_of(at * HALF + group * TILE, TILE), TILE)
             grad[place, lane * LANES : (lane + 1) * LANES] = tiles_ref[part]
-    gram[0] = lax.dot_general(
-        grad[...], grad[...], (((1,), (1,)), ((), ())), preferred_element_type=f32
-    )
-    gram[1] = lax.dot_general(
-        grad[...], grad[...], (((0,), (0,)), ((), ())), preferred_element_type=f32
-    )
+    gram[0] = symmetric(grad, grad, ((1,), (1,)))
+    gram[1] = symmetric(grad, grad, ((0,), (0,)))
     own = pl.ds(pl.multiple_of(position * OWN_ROWS, OWN_ROWS), OWN_ROWS)
     for receiver in range(XS):
         held = held_by(receiver * PAIR + near_y, owner_ref)
@@ -203,7 +238,9 @@
 
     shape = (BLOCK, BLOCK)
     diagonal = lax.broadcasted_iota(jnp.int32, shape, 0) == lax.broadcasted_iota(jnp.int32, shape, 1)
-    right_root = root_rows(right, right[1], right[2], jnp.where(diagonal, 1.0, 0.0)).astype(bf16)
+    right_root = root_rows(
+        right, right[1], right[2], jnp.where(diagonal, 1.0, 0.0), symmetric
+    ).astype(bf16)
     piece = jnp.dot(mixed, right_root, preferred_element_type=f32)
     for receiver in range(XS):
         out_ref[receiver, :OUT_ROWS] = piece
@@ -270,7 +307,7 @@
     reduced = call(
         reduce_kernel,
         "reduce",
-        array((FAR, TILE + QUADS * STATS, LANES), bf16),
+        array((FAR, TILE * (1 + GROUPS), LANES), bf16),
         (device, owner, exchange(packed, NEAR_AXES)),
     )
     parts = exchange(reduced, FAR_AXES)

time: 111 us -> 106 us (0.955)
  blocking collectives: 60.4 us -> 53.7 us
  starting transfers between devices: 23.2 us -> 25.2 us
    all_to_all x3, blocking collectives: 60.4 us -> 53.7 us  [exchange(): return lax.all_to_all(value, axes, split_axis=0, concat_axis=0, tiled=True)]
    all_to_all x1, starting transfers between devices: 6.1 us -> 8.21 us  [exchange(): return lax.all_to_all(value, axes, split_axis=0, concat_axis=0, tiled=True)]
where the time goes in v7:
time: 106 us; the launch traced here: 105 us
  blocking collectives  53.7 us (51%)
  starting transfers between devices  25.2 us (24%)
  Pallas kernels  13.1 us (12%)
  waiting for transfers between devices  12.7 us (12%)
    all_to_all x3, blocking collectives, exchange(): return lax.all_to_all(value, axes, split_axis=0, concat_axis=0, tiled=True)  53.7 us
    ppermute x3, starting transfers between devices, swap(): return lax.ppermute(value, axis, [(0, 1), (1, 0)])  17 us
    pallas_call x7, Pallas kernels, call(): pl.pallas_call(kernel, out_shape=outs, in_specs=[smem if array.ndim == 1...  13.1 us
    all_to_all x1, waiting for transfers between devices, exchange(): return lax.all_to_all(value, axes, split_axis=0, concat_axis=0, tiled=True)  9.55 us
    all_to_all x1, starting transfers between devices, exchange(): return lax.all_to_all(value, axes, split_axis=0, concat_axis=0, tiled=True)  8.21 us
    ppermute x3, waiting for transfers between devices, swap(): return lax.ppermute(value, axis, [(0, 1), (1, 0)])  3.19 us
  transfers between devices with their start and end apart: 4, of which 3 were waited for; matrix products, arithmetic and copies ran while one was open for 0% of the time, Pallas kernels for 0%

profile of v7, /device:TPU:1, one launch (start us, length us, event | category | flops | bytes accessed | tf_op | source)
XLA Modules:
  0.0 105.5 jit_solution(13853092473324281872)
XLA Ops:
  0.6 0.0 copy-start
  0.7 0.0 copy-start.1
  0.7 0.0 copy-start.2
  0.7 3.6 %grad_theirs.1 = bf16[4,4,256,128]{3,2,1,0:T(8,128)(2,1)} custom-call(s32[1]{0:T(128)} %bitcast.device_ref, bf16[768,1024]{1,0:T(8,128)(2,1)} %act_ref.1, bf16[768,1024]{1,0:T(8,128)(2,1)} %cot_ref.1), custom_call_target="tpu_custom_call" | custom-call | tf_op jit(solution)/shard_map/grad_theirs/pallas_call | solution.py:266
  4.3 8.8 %collective-permute-start = (bf16[4,4,256,128]{3,2,1,0:T(8,128)(2,1)}, bf16[4,4,256,128]{3,2,1,0:T(8,128)(2,1)S(1)}, u32[]{:S(2)}, u32[]{:S(2)}) collective-permute-start(bf16[4,4,256,128]{3,2,1,0:T(8,128)(2,1)} %grad_theirs.1), channel_id=1, source_target_pairs={{0,1},{1,0},{2,3},{3,2},{4,5},{5,4},{6,7},{7,6},{8,9},{9,8},{10,11... | collective-permute-start | bytes 3145736 | tf_op jit(solution)/shard_map/ppermute | solution.py:278
  13.1 2.5 %collective-permute-done.other_ref = bf16[4,4,256,128]{3,2,1,0:T(8,128)(2,1)S(1)} collective-permute-done((bf16[4,4,256,128]{3,2,1,0:T(8,128)(2,1)}, bf16[4,4,256,128]{3,2,1,0:T(8,128)(2,1)S(1)}, u32[]{:S(2)}, u32[]{:S(2)}) %collective-permute-start) | collective-permute-done | bytes 1048608 | tf_op jit(solution)/shard_map/ppermute | solution.py:278
  15.5 0.0 copy-done
  15.5 0.0 copy-done.1
  15.5 0.0 copy-done.2
  15.5 1.1 grad_mine.1
  16.6 0.0 copy-start.3
  16.6 19.8 %all_to_all.20.terms_ref = bf16[16,288,128]{2,1,0:T(8,128)(2,1)S(1)} all-to-all(bf16[16,288,128]{2,1,0:T(8,128)(2,1)S(1)} %grad_mine.1), channel_id=1, replica_groups=mesh['x'=4,'yl'=2,'z4'=4,'zp'=2,'yh'=4,'core'=2] {'x','yl','zp'}, dimensions={0} | all-to-all | bytes 2359296 | tf_op jit(solution)/shard_map/all_to_all | solution.py:259
  36.4 0.0 copy-done.3
  36.4 0.7 reduce.1
  37.1 26.3 %all_to_all.21.parts_here_ref.parts_ref = bf16[16,96,128]{2,1,0:T(8,128)(2,1)S(1)} all-to-all(bf16[16,96,128]{2,1,0:T(8,128)(2,1)S(1)} %reduce.1), channel_id=1, replica_groups=mesh['x'=4,'yl'=2,'z4'=4,'zp'=2,'yh'=4,'core'=2] {'z4','yh'}, dimensions={0} | all-to-all | bytes 786432 | tf_op jit(solution)/shard_map/all_to_all | solution.py:259
  63.4 0.7 total.1
  64.1 8.2 %all-to-all-start.2 = ((bf16[64,16,128]{2,1,0:T(8,128)(2,1)}), bf16[64,16,128]{2,1,0:T(8,128)(2,1)S(1)}, u32[]{:S(2)}, u32[]{:S(2)}) async-start(bf16[64,16,128]{2,1,0:T(8,128)(2,1)} %total.1), calls=%async_computation.2 | async-start | bytes 524288 | tf_op jit(solution)/shard_map/all_to_all | solution.py:259
  72.3 3.0 %collective-permute-start.1 = (bf16[16,96,128]{2,1,0:T(8,128)(2,1)S(1)}, bf16[16,96,128]{2,1,0:T(8,128)(2,1)S(1)}, u32[]{:S(2)}, u32[]{:S(2)}) collective-permute-start(bf16[16,96,128]{2,1,0:T(8,128)(2,1)S(1)} %all_to_all.21.parts_here_ref.parts_ref), channel_id=1, source_target_pairs={{0,1},{1,0},{2,3},{3,2},{4,5},{5,4},{6,7},{7,6},{8,9},{9,8},{10,11... | collective-permute-start | bytes 1179656 | tf_op jit(solution)/shard_map/ppermute | solution.py:278
  75.3 9.5 %all-to-all-done.2.tiles_here_ref = bf16[64,16,128]{2,1,0:T(8,128)(2,1)S(1)} async-done(((bf16[64,16,128]{2,1,0:T(8,128)(2,1)}), bf16[64,16,128]{2,1,0:T(8,128)(2,1)S(1)}, u32[]{:S(2)}, u32[]{:S(2)}) %all-to-all-start.2) | async-done | bytes 262176 | tf_op jit(solution)/shard_map/all_to_all | solution.py:259
  84.9 5.2 %collective-permute-start.2 = (bf16[64,16,128]{2,1,0:T(8,128)(2,1)S(1)}, bf16[64,16,128]{2,1,0:T(8,128)(2,1)S(1)}, u32[]{:S(2)}, u32[]{:S(2)}) collective-permute-start(bf16[64,16,128]{2,1,0:T(8,128)(2,1)S(1)} %all-to-all-done.2.tiles_here_ref), channel_id=1, source_target_pairs={{0,1},{1,0},{2,3},{3,2},{4,5},{5,4},{6,7},{7,6},{8,9},{9,8},{10,11... | collective-permute-start | bytes 786440 | tf_op jit(solution)/shard_map/ppermute | solution.py:278
  90.1 0.0 collective-permute-done.1.parts_there_ref
  90.1 0.4 unpack.1.stats
  90.5 0.7 collective-permute-done.2.tiles_there_ref
  91.2 5.4 %root.1 = f32[4,24,512]{2,1,0:T(8,128)S(1)} custom-call(s32[1]{0:T(128)} %bitcast.device_ref, s32[8]{0:T(128)S(1)} %copy-done.3, f32[2,512,512]{2,1,0:T(8,128)S(1)} %unpack.1.stats, bf16[64,16,128]{2,1,0:T(8,128)(2,1)S(1)} %all-to-all-done.2.tiles_here_ref, bf16[64,16,128]{2,1,0:T(8,128)(2,1)S(1)} %collective-permute-done.2.tiles_there_ref), custom_call_target="tpu_custom_call" | custom-call | tf_op jit(solution)/shard_map/root/pallas_call | solution.py:266
  96.6 7.7 %all_to_all.22.pieces_ref = f32[4,24,512]{2,1,0:T(8,128)S(1)} all-to-all(f32[4,24,512]{2,1,0:T(8,128)S(1)} %root.1), channel_id=1, replica_groups=mesh['x'=4,'yl'=2,'z4'=4,'zp'=2,'yh'=4,'core'=2] {'x'}, dimensions={0} | all-to-all | bytes 393216 | tf_op jit(solution)/shard_map/all_to_all | solution.py:259
  104.3 1.2 %join.1 = (f32[8,512]{1,0:T(8,128)}, f32[16,1024]{1,0:T(8,128)}) custom-call(s32[1]{0:T(128)} %bitcast.device_ref, s32[8]{0:T(128)S(1)} %copy-done.3, f32[8,512]{1,0:T(8,128)S(1)} %bitcast.4, f32[4,24,512]{2,1,0:T(8,128)S(1)} %all_to_all.22.pieces_ref), custom_call_target="tpu_custom_call" | custom-call | tf_op jit(solution)/shard_map/join/pallas_call | solution.py:266
Async XLA Ops:
  0.6 14.9 %copy-start = (bf16[768,1024]{1,0:T(8,128)(2,1)S(1)}, bf16[768,1024]{1,0:T(8,128)(2,1)}, u32[]{:S(2)}) copy-start(bf16[768,1024]{1,0:T(8,128)(2,1)} %act_ref.1) | copy-start | bytes 4718596
  0.7 14.9 %copy-start.1 = (bf16[768,1024]{1,0:T(8,128)(2,1)S(1)}, bf16[768,1024]{1,0:T(8,128)(2,1)}, u32[]{:S(2)}) copy-start(bf16[768,1024]{1,0:T(8,128)(2,1)} %cot_ref.1) | copy-start | bytes 4718596
  0.7 14.9 %copy-start.2 = (f32[1,8,512]{2,1,0:T(8,128)S(1)}, f32[1,8,512]{2,1,0:T(8,128)}, u32[]{:S(2)}) copy-start(f32[1,8,512]{2,1,0:T(8,128)} %param.6) | copy-start | bytes 49156
  4.3 11.3 %collective-permute-start = (bf16[4,4,256,128]{3,2,1,0:T(8,128)(2,1)}, bf16[4,4,256,128]{3,2,1,0:T(8,128)(2,1)S(1)}, u32[]{:S(2)}, u32[]{:S(2)}) collective-permute-start(bf16[4,4,256,128]{3,2,1,0:T(8,128)(2,1)} %grad_theirs.1), channel_id=1, source_target_pairs={{0,1},{1,0},{2,3},{3,2},{4,5},{5,4},{6,7},{7,6},{8,9},{9,8},{10,11... | collective-permute-start | bytes 3145736 | tf_op jit(solution)/shard_map/ppermute | solution.py:278
  16.6 19.8 %copy-start.3 = (s32[8]{0:T(128)S(1)}, s32[8]{0:T(128)}, u32[]{:S(2)}) copy-start(s32[8]{0:T(128)} %owner_ref.5) | copy-start | bytes 100
  64.1 20.7 %all-to-all-start.2 = ((bf16[64,16,128]{2,1,0:T(8,128)(2,1)}), bf16[64,16,128]{2,1,0:T(8,128)(2,1)S(1)}, u32[]{:S(2)}, u32[]{:S(2)}) async-start(bf16[64,16,128]{2,1,0:T(8,128)(2,1)} %total.1), calls=%async_computation.2 | async-start | bytes 524288 | tf_op jit(solution)/shard_map/all_to_all | solution.py:259
  72.3 17.7 %collective-permute-start.1 = (bf16[16,96,128]{2,1,0:T(8,128)(2,1)S(1)}, bf16[16,96,128]{2,1,0:T(8,128)(2,1)S(1)}, u32[]{:S(2)}, u32[]{:S(2)}) collective-permute-start(bf16[16,96,128]{2,1,0:T(8,128)(2,1)S(1)} %all_to_all.21.parts_here_ref.parts_ref), channel_id=1, source_target_pairs={{0,1},{1,0},{2,3},{3,2},{4,5},{5,4},{6,7},{7,6},{8,9},{9,8},{10,11... | collective-permute-start | bytes 1179656 | tf_op jit(solution)/shard_map/ppermute | solution.py:278
  84.9 6.3 %collective-permute-start.2 = (bf16[64,16,128]{2,1,0:T(8,128)(2,1)S(1)}, bf16[64,16,128]{2,1,0:T(8,128)(2,1)S(1)}, u32[]{:S(2)}, u32[]{:S(2)}) collective-permute-start(bf16[64,16,128]{2,1,0:T(8,128)(2,1)S(1)} %all-to-all-done.2.tiles_here_ref), channel_id=1, source_target_pairs={{0,1},{1,0},{2,3},{3,2},{4,5},{5,4},{6,7},{7,6},{8,9},{9,8},{10,11... | collective-permute-start | bytes 786440 | tf_op jit(solution)/shard_map/ppermute | solution.py:278

commit v8 on v7

--- a/solution.py
+++ b/solution.py
@@ -98,17 +98,22 @@
                 out_ref[block * QUADS + lane, HALF:] = stats
 
 
+def slots_kernel(device_ref, owner_ref, out_ref):
+    block = near_place(device_ref[0])[0]
+    for side in range(2):
+        out_ref[side] = owner_ref[side * BLOCKS + block] * PAIR
+
+
 def sent_groups(row_block):
     near = [(side, (row_block + step) % 4) for side in range(2) for step in range(2)]
     return near + [(row_block // 2, (row_block + 2) % 4)]
 
 
-def reduce_kernel(device_ref, owner_ref, terms_ref, out_ref):
-    block = near_place(device_ref[0])[0]
+def reduce_kernel(device_ref, slots_ref, terms_ref, out_ref):
     row_block = device_ref[0] % SHARDS // 16
     lanes = []
     for side in range(2):
-        first = owner_ref[side * BLOCKS + block] * PAIR
+        first = slots_ref[side]
         low, high = (terms_ref[first + chip, HALF:].astype(f32) for chip in range(PAIR))
         rows = [slice(lane * OWN_ROWS, (lane + 1) * OWN_ROWS) for lane in range(4)]
         lanes.append([jnp.concatenate([low[place], high[place]], axis=0) for place in rows])
@@ -259,15 +264,17 @@
     return lax.all_to_all(value, axes, split_axis=0, concat_axis=0, tiled=True)
 
 
-def call(kernel, name, outs, arrays, scratch=(), limit=VMEM_LIMIT):
-    vmem = pl.BlockSpec(memory_space=pltpu.VMEM)
-    smem = pl.BlockSpec(memory_space=pltpu.SMEM)
-    rest = pl.BlockSpec(memory_space=pl.ANY) if limit > VMEM_LIMIT else vmem
+vmem = pl.BlockSpec(memory_space=pltpu.VMEM)
+smem = pl.BlockSpec(memory_space=pltpu.SMEM)
+anywhere = pl.BlockSpec(memory_space=pl.ANY)
+
+
+def call(kernel, name, outs, arrays, scratch=(), limit=VMEM_LIMIT, operands=vmem, results=vmem):
     return pl.pallas_call(
         kernel,
         out_shape=outs,
-        in_specs=[smem if array.ndim == 1 else rest for array in arrays],
-        out_specs=tuple(rest for _ in outs) if isinstance(outs, tuple) else rest,
+        in_specs=[smem if array.ndim == 1 else operands for array in arrays],
+        out_specs=tuple(results for _ in outs) if isinstance(outs, tuple) else results,
         scratch_shapes=list(scratch),
         compiler_params=pltpu.CompilerParams(vmem_limit_bytes=limit),
         name=name,
@@ -297,6 +304,8 @@
             pltpu.SemaphoreType.DMA((BLOCKS,)),
         ],
         limit=GRAD_LIMIT,
+        operands=anywhere,
+        results=anywhere,
     )
     packed = call(
         mine_kernel,
@@ -304,11 +313,14 @@
         array((XS * QUADS, HALF + STATS, LANES), bf16),
         (device, activations, cotangents, swap(other, "core"), own),
     )
+    slots = call(
+        slots_kernel, "slots", array((2,), jnp.int32), (device, owner), results=smem
+    )
     reduced = call(
         reduce_kernel,
         "reduce",
         array((FAR, TILE * (1 + GROUPS), LANES), bf16),
-        (device, owner, exchange(packed, NEAR_AXES)),
+        (device, slots, exchange(packed, NEAR_AXES)),
     )
     parts = exchange(reduced, FAR_AXES)
     gradient = call(total_kernel, "total", array((PARTS, TILE, LANES), bf16), (parts,))

time: 106 us -> 108 us (1.019)
  blocking collectives: 53.7 us -> 32.8 us
  waiting for transfers between devices: 12.7 us -> 28.3 us
  starting transfers between devices: 25.2 us -> 30.5 us
  Pallas kernels: 13.1 us -> 14.2 us
    all_to_all x3 -> x2, blocking collectives: 53.7 us -> 32.8 us  [exchange(): return lax.all_to_all(value, axes, split_axis=0, concat_axis=0, tiled=True)]
    all_to_all x1 -> x2, waiting for transfers between devices: 9.55 us -> 25.1 us  [exchange(): return lax.all_to_all(value, axes, split_axis=0, concat_axis=0, tiled=True)]
    all_to_all x1 -> x2, starting transfers between devices: 8.21 us -> 13.3 us  [exchange(): return lax.all_to_all(value, axes, split_axis=0, concat_axis=0, tiled=True)]
    pallas_call x7 -> x8, Pallas kernels: 13.1 us -> 14.2 us  [call(): pl.pallas_call(kernel, out_shape=outs, in_specs=[smem if array.ndim == 1...]
  transfers between devices with their start and end apart: 4 -> 5, of which waited for: 3 -> 4; matrix products, arithmetic and copies ran while one was open for 0% -> 0% of each run, Pallas kernels for 0% -> 1%
where the time goes in v8:
time: 108 us
  blocking collectives  32.8 us (30%)
  starting transfers between devices  30.5 us (28%)
  waiting for transfers between devices  28.3 us (26%)
  Pallas kernels  14.2 us (13%)
    all_to_all x2, blocking collectives, exchange(): return lax.all_to_all(value, axes, split_axis=0, concat_axis=0, tiled=True)  32.8 us
    all_to_all x2, waiting for transfers between devices, exchange(): return lax.all_to_all(value, axes, split_axis=0, concat_axis=0, tiled=True)  25.1 us
    ppermute x3, starting transfers between devices, swap(): return lax.ppermute(value, axis, [(0, 1), (1, 0)])  17.1 us
    pallas_call x8, Pallas kernels, call(): pl.pallas_call(kernel, out_shape=outs, in_specs=[smem if array.ndim == 1...  14.2 us
    all_to_all x2, starting transfers between devices, exchange(): return lax.all_to_all(value, axes, split_axis=0, concat_axis=0, tiled=True)  13.3 us
    ppermute x3, waiting for transfers between devices, swap(): return lax.ppermute(value, axis, [(0, 1), (1, 0)])  3.19 us
  transfers between devices with their start and end apart: 5, of which 4 were waited for; matrix products, arithmetic and copies ran while one was open for 0% of the time, Pallas kernels for 1%

profile of v8, /device:TPU:1, one launch (start us, length us, event | category | flops | bytes accessed | tf_op | source)
XLA Modules:
  0.0 107.5 jit_solution(7304031102306431216)
XLA Ops:
  0.6 0.0 copy-start
  0.7 0.0 copy-start.1
  0.7 0.0 copy-start.3
  0.7 3.6 %grad_theirs.1 = bf16[4,4,256,128]{3,2,1,0:T(8,128)(2,1)} custom-call(s32[1]{0:T(128)} %bitcast.device_ref, bf16[768,1024]{1,0:T(8,128)(2,1)} %act_ref.1, bf16[768,1024]{1,0:T(8,128)(2,1)} %cot_ref.1), custom_call_target="tpu_custom_call" | custom-call | tf_op jit(solution)/shard_map/grad_theirs/pallas_call | solution.py:273
  4.3 8.8 %collective-permute-start = (bf16[4,4,256,128]{3,2,1,0:T(8,128)(2,1)}, bf16[4,4,256,128]{3,2,1,0:T(8,128)(2,1)S(1)}, u32[]{:S(2)}, u32[]{:S(2)}) collective-permute-start(bf16[4,4,256,128]{3,2,1,0:T(8,128)(2,1)} %grad_theirs.1), channel_id=1, source_target_pairs={{0,1},{1,0},{2,3},{3,2},{4,5},{5,4},{6,7},{7,6},{8,9},{9,8},{10,11... | collective-permute-start | bytes 3145736 | tf_op jit(solution)/shard_map/ppermute | solution.py:285
  13.1 2.5 %collective-permute-done.other_ref = bf16[4,4,256,128]{3,2,1,0:T(8,128)(2,1)S(1)} collective-permute-done((bf16[4,4,256,128]{3,2,1,0:T(8,128)(2,1)}, bf16[4,4,256,128]{3,2,1,0:T(8,128)(2,1)S(1)}, u32[]{:S(2)}, u32[]{:S(2)}) %collective-permute-start) | collective-permute-done | bytes 1048608 | tf_op jit(solution)/shard_map/ppermute | solution.py:285
  15.6 0.0 copy-done
  15.6 0.0 copy-done.1
  15.6 0.0 copy-done.3
  15.6 1.1 grad_mine.1
  16.6 0.0 copy-start.2
  16.6 1.0 copy-done.2
  17.7 0.0 copy-start.4
  17.7 3.8 %all-to-all-start = ((bf16[16,288,128]{2,1,0:T(8,128)(2,1)}), bf16[16,288,128]{2,1,0:T(8,128)(2,1)S(1)}, u32[]{:S(2)}, u32[]{:S(2)}) async-start(bf16[16,288,128]{2,1,0:T(8,128)(2,1)} %copy-done.2), calls=%async_computation | async-start | bytes 2359296 | tf_op jit(solution)/shard_map/all_to_all | solution.py:264
  21.5 0.0 copy-done.4
  21.5 1.1 %slots.1.slots_ref = s32[2]{0:T(128)S(1)} custom-call(s32[1]{0:T(128)} %bitcast.device_ref, s32[8]{0:T(128)S(1)} %copy-done.4), custom_call_target="tpu_custom_call" | custom-call | tf_op jit(solution)/shard_map/slots/pallas_call | solution.py:273
  22.7 15.7 %all-to-all-done.terms_ref = bf16[16,288,128]{2,1,0:T(8,128)(2,1)S(1)} async-done(((bf16[16,288,128]{2,1,0:T(8,128)(2,1)}), bf16[16,288,128]{2,1,0:T(8,128)(2,1)S(1)}, u32[]{:S(2)}, u32[]{:S(2)}) %all-to-all-start) | async-done | bytes 1179680 | tf_op jit(solution)/shard_map/all_to_all | solution.py:264
  38.4 0.7 reduce.1
  39.1 25.0 %all_to_all.20.parts_here_ref.parts_ref = bf16[16,96,128]{2,1,0:T(8,128)(2,1)S(1)} all-to-all(bf16[16,96,128]{2,1,0:T(8,128)(2,1)S(1)} %reduce.1), channel_id=1, replica_groups=mesh['x'=4,'yl'=2,'z4'=4,'zp'=2,'yh'=4,'core'=2] {'z4','yh'}, dimensions={0} | all-to-all | bytes 786432 | tf_op jit(solution)/shard_map/all_to_all | solution.py:264
  64.0 0.7 total.1
  64.8 9.5 %all-to-all-start.2 = ((bf16[64,16,128]{2,1,0:T(8,128)(2,1)}), bf16[64,16,128]{2,1,0:T(8,128)(2,1)S(1)}, u32[]{:S(2)}, u32[]{:S(2)}) async-start(bf16[64,16,128]{2,1,0:T(8,128)(2,1)} %total.1), calls=%async_computation.2 | async-start | bytes 524288 | tf_op jit(solution)/shard_map/all_to_all | solution.py:264
  74.3 3.0 %collective-permute-start.1 = (bf16[16,96,128]{2,1,0:T(8,128)(2,1)S(1)}, bf16[16,96,128]{2,1,0:T(8,128)(2,1)S(1)}, u32[]{:S(2)}, u32[]{:S(2)}) collective-permute-start(bf16[16,96,128]{2,1,0:T(8,128)(2,1)S(1)} %all_to_all.20.parts_here_ref.parts_ref), channel_id=1, source_target_pairs={{0,1},{1,0},{2,3},{3,2},{4,5},{5,4},{6,7},{7,6},{8,9},{9,8},{10,11... | collective-permute-start | bytes 1179656 | tf_op jit(solution)/shard_map/ppermute | solution.py:285
  77.3 9.4 %all-to-all-done.2.tiles_here_ref = bf16[64,16,128]{2,1,0:T(8,128)(2,1)S(1)} async-done(((bf16[64,16,128]{2,1,0:T(8,128)(2,1)}), bf16[64,16,128]{2,1,0:T(8,128)(2,1)S(1)}, u32[]{:S(2)}, u32[]{:S(2)}) %all-to-all-start.2) | async-done | bytes 262176 | tf_op jit(solution)/shard_map/all_to_all | solution.py:264
  86.7 5.3 %collective-permute-start.2 = (bf16[64,16,128]{2,1,0:T(8,128)(2,1)S(1)}, bf16[64,16,128]{2,1,0:T(8,128)(2,1)S(1)}, u32[]{:S(2)}, u32[]{:S(2)}) collective-permute-start(bf16[64,16,128]{2,1,0:T(8,128)(2,1)S(1)} %all-to-all-done.2.tiles_here_ref), channel_id=1, source_target_pairs={{0,1},{1,0},{2,3},{3,2},{4,5},{5,4},{6,7},{7,6},{8,9},{9,8},{10,11... | collective-permute-start | bytes 786440 | tf_op jit(solution)/shard_map/ppermute | solution.py:285
  92.0 0.0 collective-permute-done.1.parts_there_ref
  92.0 0.4 unpack.1.stats
  92.4 0.7 collective-permute-done.2.tiles_there_ref
  93.1 5.4 %root.1 = f32[4,24,512]{2,1,0:T(8,128)S(1)} custom-call(s32[1]{0:T(128)} %bitcast.device_ref, s32[8]{0:T(128)S(1)} %copy-done.4, f32[2,512,512]{2,1,0:T(8,128)S(1)} %unpack.1.stats, bf16[64,16,128]{2,1,0:T(8,128)(2,1)S(1)} %all-to-all-done.2.tiles_here_ref, bf16[64,16,128]{2,1,0:T(8,128)(2,1)S(1)} %collective-permute-done.2.tiles_there_ref), custom_call_target="tpu_custom_call" | custom-call | tf_op jit(solution)/shard_map/root/pallas_call | solution.py:273
  98.5 7.8 %all_to_all.21.pieces_ref = f32[4,24,512]{2,1,0:T(8,128)S(1)} all-to-all(f32[4,24,512]{2,1,0:T(8,128)S(1)} %root.1), channel_id=1, replica_groups=mesh['x'=4,'yl'=2,'z4'=4,'zp'=2,'yh'=4,'core'=2] {'x'}, dimensions={0} | all-to-all | bytes 393216 | tf_op jit(solution)/shard_map/all_to_all | solution.py:264
  106.3 1.2 %join.1 = (f32[8,512]{1,0:T(8,128)}, f32[16,1024]{1,0:T(8,128)}) custom-call(s32[1]{0:T(128)} %bitcast.device_ref, s32[8]{0:T(128)S(1)} %copy-done.4, f32[8,512]{1,0:T(8,128)S(1)} %bitcast.4, f32[4,24,512]{2,1,0:T(8,128)S(1)} %all_to_all.21.pieces_ref), custom_call_target="tpu_custom_call" | custom-call | tf_op jit(solution)/shard_map/join/pallas_call | solution.py:273
Async XLA Ops:
  0.6 14.9 %copy-start = (bf16[768,1024]{1,0:T(8,128)(2,1)S(1)}, bf16[768,1024]{1,0:T(8,128)(2,1)}, u32[]{:S(2)}) copy-start(bf16[768,1024]{1,0:T(8,128)(2,1)} %act_ref.1) | copy-start | bytes 4718596
  0.7 14.9 %copy-start.1 = (bf16[768,1024]{1,0:T(8,128)(2,1)S(1)}, bf16[768,1024]{1,0:T(8,128)(2,1)}, u32[]{:S(2)}) copy-start(bf16[768,1024]{1,0:T(8,128)(2,1)} %cot_ref.1) | copy-start | bytes 4718596
  0.7 14.9 %copy-start.3 = (f32[1,8,512]{2,1,0:T(8,128)S(1)}, f32[1,8,512]{2,1,0:T(8,128)}, u32[]{:S(2)}) copy-start(f32[1,8,512]{2,1,0:T(8,128)} %param.6) | copy-start | bytes 49156
  4.3 11.3 %collective-permute-start = (bf16[4,4,256,128]{3,2,1,0:T(8,128)(2,1)}, bf16[4,4,256,128]{3,2,1,0:T(8,128)(2,1)S(1)}, u32[]{:S(2)}, u32[]{:S(2)}) collective-permute-start(bf16[4,4,256,128]{3,2,1,0:T(8,128)(2,1)} %grad_theirs.1), channel_id=1, source_target_pairs={{0,1},{1,0},{2,3},{3,2},{4,5},{5,4},{6,7},{7,6},{8,9},{9,8},{10,11... | collective-permute-start | bytes 3145736 | tf_op jit(solution)/shard_map/ppermute | solution.py:285
  16.6 1.0 copy-start.2
  17.7 3.8 %copy-start.4 = (s32[8]{0:T(128)S(1)}, s32[8]{0:T(128)}, u32[]{:S(2)}) copy-start(s32[8]{0:T(128)} %owner_ref.5) | copy-start | bytes 100
  17.7 20.7 %all-to-all-start = ((bf16[16,288,128]{2,1,0:T(8,128)(2,1)}), bf16[16,288,128]{2,1,0:T(8,128)(2,1)S(1)}, u32[]{:S(2)}, u32[]{:S(2)}) async-start(bf16[16,288,128]{2,1,0:T(8,128)(2,1)} %copy-done.2), calls=%async_computation | async-start | bytes 2359296 | tf_op jit(solution)/shard_map/all_to_all | solution.py:264
  64.8 21.9 %all-to-all-start.2 = ((bf16[64,16,128]{2,1,0:T(8,128)(2,1)}), bf16[64,16,128]{2,1,0:T(8,128)(2,1)S(1)}, u32[]{:S(2)}, u32[]{:S(2)}) async-start(bf16[64,16,128]{2,1,0:T(8,128)(2,1)} %total.1), calls=%async_computation.2 | async-start | bytes 524288 | tf_op jit(solution)/shard_map/all_to_all | solution.py:264
  74.3 17.7 %collective-permute-start.1 = (bf16[16,96,128]{2,1,0:T(8,128)(2,1)S(1)}, bf16[16,96,128]{2,1,0:T(8,128)(2,1)S(1)}, u32[]{:S(2)}, u32[]{:S(2)}) collective-permute-start(bf16[16,96,128]{2,1,0:T(8,128)(2,1)S(1)} %all_to_all.20.parts_here_ref.parts_ref), channel_id=1, source_target_pairs={{0,1},{1,0},{2,3},{3,2},{4,5},{5,4},{6,7},{7,6},{8,9},{9,8},{10,11... | collective-permute-start | bytes 1179656 | tf_op jit(solution)/shard_map/ppermute | solution.py:285
  86.7 6.5 %collective-permute-start.2 = (bf16[64,16,128]{2,1,0:T(8,128)(2,1)S(1)}, bf16[64,16,128]{2,1,0:T(8,128)(2,1)S(1)}, u32[]{:S(2)}, u32[]{:S(2)}) collective-permute-start(bf16[64,16,128]{2,1,0:T(8,128)(2,1)S(1)} %all-to-all-done.2.tiles_here_ref), channel_id=1, source_target_pairs={{0,1},{1,0},{2,3},{3,2},{4,5},{5,4},{6,7},{7,6},{8,9},{9,8},{10,11... | collective-permute-start | bytes 786440 | tf_op jit(solution)/shard_map/ppermute | solution.py:285

commit v9 on v7

--- a/solution.py
+++ b/solution.py
@@ -30,6 +30,7 @@
 NEAR_AXES = ("x", "yl", "zp")
 FAR_AXES = ("z4", "yh")
 PLANE = ("yl", "zp") + FAR_AXES
+DEVICE_AXES = ("x", "yl", "z4", "zp", "yh", "core")
 VMEM_LIMIT = 40 * 1024 * 1024
 GRAD_LIMIT = 60 * 1024 * 1024
 
@@ -41,12 +42,16 @@
     return held
 
 
+def this_device():
+    return lax.axis_index(DEVICE_AXES)
+
+
 def near_place(device):
     return device // (PAIR * SHARDS), device // SHARDS % PAIR, device // 8 % PAIR, device % CORES
 
 
-def theirs_kernel(device_ref, act_hbm, cot_hbm, out_hbm, act_ref, cot_ref, out_ref, sems, out_sems):
-    half = 1 - device_ref[0] % CORES
+def theirs_kernel(act_hbm, cot_hbm, out_hbm, act_ref, cot_ref, out_ref, sems, out_sems):
+    half = 1 - this_device() % CORES
     copies = []
     for row in range(2):
         start = pl.multiple_of(row * BLOCK + half * HALF, HALF)
@@ -82,20 +87,25 @@
     return lax.dot_general(act, cot, (((0,), (0,)), ((), ())), preferred_element_type=f32)
 
 
-def mine_kernel(device_ref, act_ref, cot_ref, other_ref, own_ref, out_ref):
-    half = device_ref[0] % CORES
-    parts = [own_ref[:, lane * LANES : (lane + 1) * LANES] for lane in range(BLOCK // LANES)]
-    stats = jnp.concatenate(parts, axis=0).astype(bf16)
+def mine_kernel(act_ref, cot_ref, out_ref):
+    half = this_device() % CORES
     for row in range(2):
         start = pl.multiple_of(row * BLOCK + half * HALF, HALF)
         act = act_ref[:, pl.ds(start, HALF)]
         for col in range(COLS):
-            block = row * COLS + col
             term = half_term(act, cot_ref[:, col * BLOCK : (col + 1) * BLOCK])
             for lane in range(QUADS):
-                total = term[:, lane * LANES : (lane + 1) * LANES] + other_ref[block, lane].astype(f32)
-                out_ref[block * QUADS + lane, :HALF] = total.astype(bf16)
-                out_ref[block * QUADS + lane, HALF:] = stats
+                out_ref[row * COLS + col, lane] = term[:, lane * LANES : (lane + 1) * LANES]
+
+
+def pack_kernel(mine_ref, other_ref, own_ref, out_ref):
+    parts = [own_ref[:, lane * LANES : (lane + 1) * LANES] for lane in range(BLOCK // LANES)]
+    stats = jnp.concatenate(parts, axis=0).astype(bf16)
+    for block in range(BLOCKS):
+        for lane in range(QUADS):
+            total = mine_ref[block, lane] + other_ref[block, lane].astype(f32)
+            out_ref[block * QUADS + lane, :HALF] = total.astype(bf16)
+            out_ref[block * QUADS + lane, HALF:] = stats
 
 
 def sent_groups(row_block):
@@ -103,9 +113,9 @@
     return near + [(row_block // 2, (row_block + 2) % 4)]
 
 
-def reduce_kernel(device_ref, owner_ref, terms_ref, out_ref):
-    block = near_place(device_ref[0])[0]
-    row_block = device_ref[0] % SHARDS // 16
+def reduce_kernel(owner_ref, terms_ref, out_ref):
+    block = near_place(this_device())[0]
+    row_block = this_device() % SHARDS // 16
     lanes = []
     for side in range(2):
         first = owner_ref[side * BLOCKS + block] * PAIR
@@ -139,8 +149,8 @@
         gradient_ref[part] = gradient
 
 
-def unpack_kernel(device_ref, parts_here_ref, parts_there_ref, stats):
-    core = device_ref[0] % CORES
+def unpack_kernel(parts_here_ref, parts_there_ref, stats):
+    core = this_device() % CORES
     for parts_ref, at in ((parts_here_ref, core), (parts_there_ref, 1 - core)):
         for part in range(FAR):
             row_block, column = divmod(part, 4)
@@ -200,7 +210,6 @@
 
 
 def root_kernel(
-    device_ref,
     owner_ref,
     stats,
     tiles_here_ref,
@@ -210,9 +219,9 @@
     gram,
     rows,
 ):
-    device = device_ref[0]
+    device = this_device()
     position = device % SHARDS
-    _, near_y, _, core = near_place(device)
+    block, near_y, _, core = near_place(device)
     for tiles_ref, at in ((tiles_here_ref, core), (tiles_there_ref, 1 - core)):
         for part in range(PARTS):
             lane, group = divmod(part, FAR)
@@ -223,7 +232,8 @@
     own = pl.ds(pl.multiple_of(position * OWN_ROWS, OWN_ROWS), OWN_ROWS)
     for receiver in range(XS):
         held = held_by(receiver * PAIR + near_y, owner_ref)
-        out_ref[receiver, OUT_ROWS:] = gram[held // BLOCKS, own, :]
+        here = held % BLOCKS == block
+        out_ref[receiver, OUT_ROWS:] = jnp.where(here, gram[held // BLOCKS, own, :], 0.0)
 
     start = pl.multiple_of(position % (BLOCK // OUT_ROWS) * OUT_ROWS, OUT_ROWS)
     states = newton(stats, gram)
@@ -246,11 +256,12 @@
         out_ref[receiver, :OUT_ROWS] = piece
 
 
-def join_kernel(device_ref, owner_ref, own_ref, pieces_ref, updated_ref, direction_ref):
-    device = device_ref[0]
-    block = held_by(device // SHARDS, owner_ref) % BLOCKS
-    updated_ref[...] = ema_decay * own_ref[...] + (1.0 - ema_decay) * pieces_ref[block, OUT_ROWS:]
-    first = device % SHARDS // (BLOCK // OUT_ROWS) * COLS
+def join_kernel(own_ref, pieces_ref, updated_ref, direction_ref):
+    rows = pieces_ref[0, OUT_ROWS:]
+    for source in range(1, XS):
+        rows += pieces_ref[source, OUT_ROWS:]
+    updated_ref[...] = ema_decay * own_ref[...] + (1.0 - ema_decay) * rows
+    first = this_device() % SHARDS // (BLOCK // OUT_ROWS) * COLS
     for col in range(COLS):
         direction_ref[:, col * BLOCK : (col + 1) * BLOCK] = pieces_ref[first + col, :OUT_ROWS]
 
@@ -279,7 +290,6 @@
 
 
 def body(activations, cotangents, statistics, owner):
-    device = lax.axis_index(("x", "yl", "z4", "zp", "yh", "core")).astype(jnp.int32).reshape(1)
     array = jax.ShapeDtypeStruct
     own = statistics[0]
     tokens = activations.shape[0]
@@ -288,7 +298,7 @@
         theirs_kernel,
         "grad_theirs",
         array((BLOCKS, QUADS, HALF, LANES), bf16),
-        (device, activations, cotangents),
+        (activations, cotangents),
         scratch=[
             pltpu.VMEM((2, tokens, HALF), bf16),
             pltpu.VMEM((COLS, tokens, BLOCK), bf16),
@@ -298,29 +308,35 @@
         ],
         limit=GRAD_LIMIT,
     )
-    packed = call(
+    mine = call(
         mine_kernel,
         "grad_mine",
+        array((BLOCKS, QUADS, HALF, LANES), f32),
+        (activations, cotangents),
+    )
+    packed = call(
+        pack_kernel,
+        "pack",
         array((XS * QUADS, HALF + STATS, LANES), bf16),
-        (device, activations, cotangents, swap(other, "core"), own),
+        (mine, swap(other, "core"), own),
     )
     reduced = call(
         reduce_kernel,
         "reduce",
         array((FAR, TILE * (1 + GROUPS), LANES), bf16),
-        (device, owner, exchange(packed, NEAR_AXES)),
+        (owner, exchange(packed, NEAR_AXES)),
     )
     parts = exchange(reduced, FAR_AXES)
     gradient = call(total_kernel, "total", array((PARTS, TILE, LANES), bf16), (parts,))
     rows = call(
-        unpack_kernel, "unpack", array((2, BLOCK, BLOCK), f32), (device, parts, swap(parts, "core"))
+        unpack_kernel, "unpack", array((2, BLOCK, BLOCK), f32), (parts, swap(parts, "core"))
     )
     tiles = exchange(gradient, PLANE)
     pieces = call(
         root_kernel,
         "root",
         array((XS, OUT_ROWS + OWN_ROWS, BLOCK), f32),
-        (device, owner, rows, tiles, swap(tiles, "core")),
+        (owner, rows, tiles, swap(tiles, "core")),
         scratch=[
             pltpu.VMEM((BLOCK, BLOCK), bf16),
             pltpu.VMEM((2, BLOCK, BLOCK), f32),
@@ -331,7 +347,7 @@
         join_kernel,
         "join",
         (array((OWN_ROWS, BLOCK), f32), array((OUT_ROWS, COLS * BLOCK), f32)),
-        (device, owner, own, exchange(pieces, "x")),
+        (own, exchange(pieces, "x")),
     )
     return updated[None], direction
 

time: 106 us -> 104 us (0.981)
  waiting for transfers between devices: 12.7 us -> 11.6 us
    ppermute x3, waiting for transfers between devices: 3.19 us -> 2.1 us  [swap(): return lax.ppermute(value, axis, [(0, 1), (1, 0)])]
    pallas_call x7 -> x8, Pallas kernels: 13.1 us -> 12.8 us  [call(): pl.pallas_call(kernel, out_shape=outs, in_specs=[smem if array.ndim == 1...]
  transfers between devices with their start and end apart: 4 -> 4, of which waited for: 3 -> 3; matrix products, arithmetic and copies ran while one was open for 0% -> 0% of each run, Pallas kernels for 0% -> 1%
where the time goes in v9:
time: 104 us
  blocking collectives  53.7 us (52%)
  starting transfers between devices  25.2 us (24%)
  Pallas kernels  12.8 us (12%)
  waiting for transfers between devices  11.6 us (11%)
    all_to_all x3, blocking collectives, exchange(): return lax.all_to_all(value, axes, split_axis=0, concat_axis=0, tiled=True)  53.7 us
    ppermute x3, starting transfers between devices, swap(): return lax.ppermute(value, axis, [(0, 1), (1, 0)])  16.9 us
    pallas_call x8, Pallas kernels, call(): pl.pallas_call(kernel, out_shape=outs, in_specs=[smem if array.ndim == 1...  12.8 us
    all_to_all x1, waiting for transfers between devices, exchange(): return lax.all_to_all(value, axes, split_axis=0, concat_axis=0, tiled=True)  9.55 us
    all_to_all x1, starting transfers between devices, exchange(): return lax.all_to_all(value, axes, split_axis=0, concat_axis=0, tiled=True)  8.21 us
    ppermute x3, waiting for transfers between devices, swap(): return lax.ppermute(value, axis, [(0, 1), (1, 0)])  2.1 us
  transfers between devices with their start and end apart: 4, of which 3 were waited for; matrix products, arithmetic and copies ran while one was open for 0% of the time, Pallas kernels for 1%

profile of v9, /device:TPU:1, one launch (start us, length us, event | category | flops | bytes accessed | tf_op | source)
XLA Modules:
  0.0 104.1 jit_solution(10610123072991010468)
XLA Ops:
  0.6 0.0 copy-start.1
  0.6 0.0 copy-start
  0.6 3.6 %grad_theirs.1 = bf16[4,4,256,128]{3,2,1,0:T(8,128)(2,1)} custom-call(bf16[768,1024]{1,0:T(8,128)(2,1)} %act_hbm.1, bf16[768,1024]{1,0:T(8,128)(2,1)} %cot_hbm.1), custom_call_target="tpu_custom_call" | custom-call | tf_op jit(solution)/shard_map/grad_theirs/pallas_call | solution.py:277
  4.3 0.0 copy-start.2
  4.3 8.8 %collective-permute-start = (bf16[4,4,256,128]{3,2,1,0:T(8,128)(2,1)}, bf16[4,4,256,128]{3,2,1,0:T(8,128)(2,1)S(1)}, u32[]{:S(2)}, u32[]{:S(2)}) collective-permute-start(bf16[4,4,256,128]{3,2,1,0:T(8,128)(2,1)} %grad_theirs.1), channel_id=1, source_target_pairs={{0,1},{1,0},{2,3},{3,2},{4,5},{5,4},{6,7},{7,6},{8,9},{9,8},{10,11... | collective-permute-start | bytes 3145736 | tf_op jit(solution)/shard_map/ppermute | solution.py:289
  13.1 0.0 copy-done.1
  13.1 0.0 copy-done
  13.1 1.0 %grad_mine.1.mine_ref = f32[4,4,256,128]{3,2,1,0:T(8,128)S(1)} custom-call(bf16[768,1024]{1,0:T(8,128)(2,1)S(1)} %copy-done, bf16[768,1024]{1,0:T(8,128)(2,1)S(1)} %copy-done.1), custom_call_target="tpu_custom_call" | custom-call | tf_op jit(solution)/shard_map/grad_mine/pallas_call | solution.py:277
  14.1 1.4 %collective-permute-done.other_ref = bf16[4,4,256,128]{3,2,1,0:T(8,128)(2,1)S(1)} collective-permute-done((bf16[4,4,256,128]{3,2,1,0:T(8,128)(2,1)}, bf16[4,4,256,128]{3,2,1,0:T(8,128)(2,1)S(1)}, u32[]{:S(2)}, u32[]{:S(2)}) %collective-permute-start) | collective-permute-done | bytes 1048608 | tf_op jit(solution)/shard_map/ppermute | solution.py:289
  15.5 0.0 copy-done.2
  15.5 0.2 pack.1
  15.7 0.0 copy-start.3
  15.7 19.8 %all_to_all.20.terms_ref = bf16[16,288,128]{2,1,0:T(8,128)(2,1)S(1)} all-to-all(bf16[16,288,128]{2,1,0:T(8,128)(2,1)S(1)} %pack.1), channel_id=1, replica_groups=mesh['x'=4,'yl'=2,'z4'=4,'zp'=2,'yh'=4,'core'=2] {'x','yl','zp'}, dimensions={0} | all-to-all | bytes 2359296 | tf_op jit(solution)/shard_map/all_to_all | solution.py:270
  35.5 0.0 copy-done.3
  35.5 0.7 reduce.1
  36.2 26.3 %all_to_all.21.parts_here_ref.parts_ref = bf16[16,96,128]{2,1,0:T(8,128)(2,1)S(1)} all-to-all(bf16[16,96,128]{2,1,0:T(8,128)(2,1)S(1)} %reduce.1), channel_id=1, replica_groups=mesh['x'=4,'yl'=2,'z4'=4,'zp'=2,'yh'=4,'core'=2] {'z4','yh'}, dimensions={0} | all-to-all | bytes 786432 | tf_op jit(solution)/shard_map/all_to_all | solution.py:270
  62.5 0.7 total.1
  63.3 8.2 %all-to-all-start.2 = ((bf16[64,16,128]{2,1,0:T(8,128)(2,1)}), bf16[64,16,128]{2,1,0:T(8,128)(2,1)S(1)}, u32[]{:S(2)}, u32[]{:S(2)}) async-start(bf16[64,16,128]{2,1,0:T(8,128)(2,1)} %total.1), calls=%async_computation.2 | async-start | bytes 524288 | tf_op jit(solution)/shard_map/all_to_all | solution.py:270
  71.5 3.0 %collective-permute-start.1 = (bf16[16,96,128]{2,1,0:T(8,128)(2,1)S(1)}, bf16[16,96,128]{2,1,0:T(8,128)(2,1)S(1)}, u32[]{:S(2)}, u32[]{:S(2)}) collective-permute-start(bf16[16,96,128]{2,1,0:T(8,128)(2,1)S(1)} %all_to_all.21.parts_here_ref.parts_ref), channel_id=1, source_target_pairs={{0,1},{1,0},{2,3},{3,2},{4,5},{5,4},{6,7},{7,6},{8,9},{9,8},{10,11... | collective-permute-start | bytes 1179656 | tf_op jit(solution)/shard_map/ppermute | solution.py:289
  74.5 9.5 %all-to-all-done.2.tiles_here_ref = bf16[64,16,128]{2,1,0:T(8,128)(2,1)S(1)} async-done(((bf16[64,16,128]{2,1,0:T(8,128)(2,1)}), bf16[64,16,128]{2,1,0:T(8,128)(2,1)S(1)}, u32[]{:S(2)}, u32[]{:S(2)}) %all-to-all-start.2) | async-done | bytes 262176 | tf_op jit(solution)/shard_map/all_to_all | solution.py:270
  84.0 5.2 %collective-permute-start.2 = (bf16[64,16,128]{2,1,0:T(8,128)(2,1)S(1)}, bf16[64,16,128]{2,1,0:T(8,128)(2,1)S(1)}, u32[]{:S(2)}, u32[]{:S(2)}) collective-permute-start(bf16[64,16,128]{2,1,0:T(8,128)(2,1)S(1)} %all-to-all-done.2.tiles_here_ref), channel_id=1, source_target_pairs={{0,1},{1,0},{2,3},{3,2},{4,5},{5,4},{6,7},{7,6},{8,9},{9,8},{10,11... | collective-permute-start | bytes 786440 | tf_op jit(solution)/shard_map/ppermute | solution.py:289
  89.2 0.0 collective-permute-done.1.parts_there_ref
  89.2 0.4 unpack.1.stats
  89.6 0.7 collective-permute-done.2.tiles_there_ref
  90.3 5.4 %root.1 = f32[4,24,512]{2,1,0:T(8,128)S(1)} custom-call(s32[8]{0:T(128)S(1)} %copy-done.3, f32[2,512,512]{2,1,0:T(8,128)S(1)} %unpack.1.stats, bf16[64,16,128]{2,1,0:T(8,128)(2,1)S(1)} %all-to-all-done.2.tiles_here_ref, bf16[64,16,128]{2,1,0:T(8,128)(2,1)S(1)} %collective-permute-done.2.tiles_there_ref), custom_call_target="tpu_custom_call" | custom-call | tf_op jit(solution)/shard_map/root/pallas_call | solution.py:277
  95.8 7.7 %all_to_all.22.pieces_ref = f32[4,24,512]{2,1,0:T(8,128)S(1)} all-to-all(f32[4,24,512]{2,1,0:T(8,128)S(1)} %root.1), channel_id=1, replica_groups=mesh['x'=4,'yl'=2,'z4'=4,'zp'=2,'yh'=4,'core'=2] {'x'}, dimensions={0} | all-to-all | bytes 393216 | tf_op jit(solution)/shard_map/all_to_all | solution.py:270
  103.4 0.7 join.1
Async XLA Ops:
  0.6 12.4 %copy-start.1 = (bf16[768,1024]{1,0:T(8,128)(2,1)S(1)}, bf16[768,1024]{1,0:T(8,128)(2,1)}, u32[]{:S(2)}) copy-start(bf16[768,1024]{1,0:T(8,128)(2,1)} %cot_hbm.1) | copy-start | bytes 4718596
  0.6 12.4 %copy-start = (bf16[768,1024]{1,0:T(8,128)(2,1)S(1)}, bf16[768,1024]{1,0:T(8,128)(2,1)}, u32[]{:S(2)}) copy-start(bf16[768,1024]{1,0:T(8,128)(2,1)} %act_hbm.1) | copy-start | bytes 4718596
  4.3 11.3 %copy-start.2 = (f32[1,8,512]{2,1,0:T(8,128)S(1)}, f32[1,8,512]{2,1,0:T(8,128)}, u32[]{:S(2)}) copy-start(f32[1,8,512]{2,1,0:T(8,128)} %param.6) | copy-start | bytes 49156
  4.3 11.3 %collective-permute-start = (bf16[4,4,256,128]{3,2,1,0:T(8,128)(2,1)}, bf16[4,4,256,128]{3,2,1,0:T(8,128)(2,1)S(1)}, u32[]{:S(2)}, u32[]{:S(2)}) collective-permute-start(bf16[4,4,256,128]{3,2,1,0:T(8,128)(2,1)} %grad_theirs.1), channel_id=1, source_target_pairs={{0,1},{1,0},{2,3},{3,2},{4,5},{5,4},{6,7},{7,6},{8,9},{9,8},{10,11... | collective-permute-start | bytes 3145736 | tf_op jit(solution)/shard_map/ppermute | solution.py:289
  15.7 19.8 %copy-start.3 = (s32[8]{0:T(128)S(1)}, s32[8]{0:T(128)}, u32[]{:S(2)}) copy-start(s32[8]{0:T(128)} %owner_ref.3) | copy-start | bytes 100
  63.3 20.7 %all-to-all-start.2 = ((bf16[64,16,128]{2,1,0:T(8,128)(2,1)}), bf16[64,16,128]{2,1,0:T(8,128)(2,1)S(1)}, u32[]{:S(2)}, u32[]{:S(2)}) async-start(bf16[64,16,128]{2,1,0:T(8,128)(2,1)} %total.1), calls=%async_computation.2 | async-start | bytes 524288 | tf_op jit(solution)/shard_map/all_to_all | solution.py:270
  71.5 17.7 %collective-permute-start.1 = (bf16[16,96,128]{2,1,0:T(8,128)(2,1)S(1)}, bf16[16,96,128]{2,1,0:T(8,128)(2,1)S(1)}, u32[]{:S(2)}, u32[]{:S(2)}) collective-permute-start(bf16[16,96,128]{2,1,0:T(8,128)(2,1)S(1)} %all_to_all.21.parts_here_ref.parts_ref), channel_id=1, source_target_pairs={{0,1},{1,0},{2,3},{3,2},{4,5},{5,4},{6,7},{7,6},{8,9},{9,8},{10,11... | collective-permute-start | bytes 1179656 | tf_op jit(solution)/shard_map/ppermute | solution.py:289
  84.0 6.3 %collective-permute-start.2 = (bf16[64,16,128]{2,1,0:T(8,128)(2,1)S(1)}, bf16[64,16,128]{2,1,0:T(8,128)(2,1)S(1)}, u32[]{:S(2)}, u32[]{:S(2)}) collective-permute-start(bf16[64,16,128]{2,1,0:T(8,128)(2,1)S(1)} %all-to-all-done.2.tiles_here_ref), channel_id=1, source_target_pairs={{0,1},{1,0},{2,3},{3,2},{4,5},{5,4},{6,7},{7,6},{8,9},{9,8},{10,11... | collective-permute-start | bytes 786440 | tf_op jit(solution)/shard_map/ppermute | solution.py:289

commit v10 on v9

--- a/solution.py
+++ b/solution.py
@@ -35,10 +35,10 @@
 GRAD_LIMIT = 60 * 1024 * 1024
 
 
-def held_by(slot, owner_ref):
-    held = jnp.int32(0)
+def held_by(slot, owners_ref):
+    held = jnp.zeros((1, LANES), jnp.int32)
     for root in range(1, ROOTS):
-        held = jnp.where(owner_ref[root] == slot, root, held)
+        held = jnp.where(owners_ref[root : root + 1] == slot, root, held)
     return held
 
 
@@ -87,7 +87,9 @@
     return lax.dot_general(act, cot, (((0,), (0,)), ((), ())), preferred_element_type=f32)
 
 
-def mine_kernel(act_ref, cot_ref, out_ref):
+def mine_kernel(owner_ref, act_ref, cot_ref, out_ref, owners_ref):
+    for root in range(ROOTS):
+        owners_ref[root : root + 1] = jnp.full((1, LANES), owner_ref[root], jnp.int32)
     half = this_device() % CORES
     for row in range(2):
         start = pl.multiple_of(row * BLOCK + half * HALF, HALF)
@@ -113,13 +115,20 @@
     return near + [(row_block // 2, (row_block + 2) % 4)]
 
 
-def reduce_kernel(owner_ref, terms_ref, out_ref):
+def picked(terms_ref, slot, chip):
+    rows = terms_ref[chip, HALF:].astype(f32)
+    for number in range(1, ROOTS):
+        rows = jnp.where(slot == number, terms_ref[number * PAIR + chip, HALF:].astype(f32), rows)
+    return rows
+
+
+def reduce_kernel(owners_ref, terms_ref, out_ref):
     block = near_place(this_device())[0]
     row_block = this_device() % SHARDS // 16
     lanes = []
     for side in range(2):
-        first = owner_ref[side * BLOCKS + block] * PAIR
-        low, high = (terms_ref[first + chip, HALF:].astype(f32) for chip in range(PAIR))
+        slot = owners_ref[pl.ds(side * BLOCKS + block, 1)]
+        low, high = (picked(terms_ref, slot, chip) for chip in range(PAIR))
         rows = [slice(lane * OWN_ROWS, (lane + 1) * OWN_ROWS) for lane in range(4)]
         lanes.append([jnp.concatenate([low[place], high[place]], axis=0) for place in rows])
     stats = []
@@ -210,7 +219,7 @@
 
 
 def root_kernel(
-    owner_ref,
+    owners_ref,
     stats,
     tiles_here_ref,
     tiles_there_ref,
@@ -230,10 +239,14 @@
     gram[0] = symmetric(grad, grad, ((1,), (1,)))
     gram[1] = symmetric(grad, grad, ((0,), (0,)))
     own = pl.ds(pl.multiple_of(position * OWN_ROWS, OWN_ROWS), OWN_ROWS)
+    sides = [gram[side, own, :] for side in range(2)]
     for receiver in range(XS):
-        held = held_by(receiver * PAIR + near_y, owner_ref)
-        here = held % BLOCKS == block
-        out_ref[receiver, OUT_ROWS:] = jnp.where(here, gram[held // BLOCKS, own, :], 0.0)
+        held = held_by(receiver * PAIR + near_y, owners_ref)
+        for lane in range(BLOCK // LANES):
+            columns = slice(lane * LANES, (lane + 1) * LANES)
+            rows_out = jnp.where(held == block, sides[0][:, columns], 0.0)
+            rows_out = jnp.where(held == block + BLOCKS, sides[1][:, columns], rows_out)
+            out_ref[receiver, OUT_ROWS:, columns] = rows_out
 
     start = pl.multiple_of(position % (BLOCK // OUT_ROWS) * OUT_ROWS, OUT_ROWS)
     states = newton(stats, gram)
@@ -308,11 +321,11 @@
         ],
         limit=GRAD_LIMIT,
     )
-    mine = call(
+    mine, owners = call(
         mine_kernel,
         "grad_mine",
-        array((BLOCKS, QUADS, HALF, LANES), f32),
-        (activations, cotangents),
+        (array((BLOCKS, QUADS, HALF, LANES), f32), array((ROOTS, LANES), jnp.int32)),
+        (owner, activations, cotangents),
     )
     packed = call(
         pack_kernel,
@@ -324,7 +337,7 @@
         reduce_kernel,
         "reduce",
         array((FAR, TILE * (1 + GROUPS), LANES), bf16),
-        (owner, exchange(packed, NEAR_AXES)),
+        (owners, exchange(packed, NEAR_AXES)),
     )
     parts = exchange(reduced, FAR_AXES)
     gradient = call(total_kernel, "total", array((PARTS, TILE, LANES), bf16), (parts,))
@@ -336,7 +349,7 @@
         root_kernel,
         "root",
         array((XS, OUT_ROWS + OWN_ROWS, BLOCK), f32),
-        (owner, rows, tiles, swap(tiles, "core")),
+        (owners, rows, tiles, swap(tiles, "core")),
         scratch=[
             pltpu.VMEM((BLOCK, BLOCK), bf16),
             pltpu.VMEM((2, BLOCK, BLOCK), f32),

time: 104 us -> 103 us (level)
  transfers between devices with their start and end apart: 4 -> 4, of which waited for: 3 -> 3; matrix products, arithmetic and copies ran while one was open for 0% -> 0% of each run, Pallas kernels for 1% -> 2%
where the time goes in v10:
time: 103 us
  blocking collectives  53.7 us (52%)
  starting transfers between devices  25.2 us (24%)
  Pallas kernels  12.3 us (12%)
  waiting for transfers between devices  11.1 us (11%)
    all_to_all x3, blocking collectives, exchange(): return lax.all_to_all(value, axes, split_axis=0, concat_axis=0, tiled=True)  53.7 us
    ppermute x3, starting transfers between devices, swap(): return lax.ppermute(value, axis, [(0, 1), (1, 0)])  17 us
    pallas_call x8, Pallas kernels, call(): pl.pallas_call(kernel, out_shape=outs, in_specs=[smem if array.ndim == 1...  12.3 us
    all_to_all x1, waiting for transfers between devices, exchange(): return lax.all_to_all(value, axes, split_axis=0, concat_axis=0, tiled=True)  9.55 us
    all_to_all x1, starting transfers between devices, exchange(): return lax.all_to_all(value, axes, split_axis=0, concat_axis=0, tiled=True)  8.21 us
  transfers between devices with their start and end apart: 4, of which 3 were waited for; matrix products, arithmetic and copies ran while one was open for 0% of the time, Pallas kernels for 2%

profile of v10, /device:TPU:1, one launch (start us, length us, event | category | flops | bytes accessed | tf_op | source)
XLA Modules:
  0.0 103.0 jit_solution(5954213283912339985)
XLA Ops:
  0.6 0.0 copy-start.1
  0.6 0.0 copy-start
  0.6 0.0 copy-start.3
  0.7 3.6 %grad_theirs.1 = bf16[4,4,256,128]{3,2,1,0:T(8,128)(2,1)} custom-call(bf16[768,1024]{1,0:T(8,128)(2,1)} %act_hbm.1, bf16[768,1024]{1,0:T(8,128)(2,1)} %cot_hbm.1), custom_call_target="tpu_custom_call" | custom-call | tf_op jit(solution)/shard_map/grad_theirs/pallas_call | solution.py:290
  4.3 0.0 copy-start.2
  4.3 8.8 %collective-permute-start = (bf16[4,4,256,128]{3,2,1,0:T(8,128)(2,1)}, bf16[4,4,256,128]{3,2,1,0:T(8,128)(2,1)S(1)}, u32[]{:S(2)}, u32[]{:S(2)}) collective-permute-start(bf16[4,4,256,128]{3,2,1,0:T(8,128)(2,1)} %grad_theirs.1), channel_id=1, source_target_pairs={{0,1},{1,0},{2,3},{3,2},{4,5},{5,4},{6,7},{7,6},{8,9},{9,8},{10,11... | collective-permute-start | bytes 3145736 | tf_op jit(solution)/shard_map/ppermute | solution.py:302
  13.1 0.0 copy-done.1
  13.1 0.0 copy-done
  13.1 0.0 copy-done.3
  13.1 1.6 %grad_mine.1 = (f32[4,4,256,128]{3,2,1,0:T(8,128)S(1)}, s32[8,128]{1,0:T(8,128)S(1)}) custom-call(s32[8]{0:T(128)S(1)} %copy-done.3, bf16[768,1024]{1,0:T(8,128)(2,1)S(1)} %copy-done, bf16[768,1024]{1,0:T(8,128)(2,1)S(1)} %copy-done.1), custom_call_target="tpu_custom_call" | custom-call | tf_op jit(solution)/shard_map/grad_mine/pallas_call | solution.py:290
  14.7 0.8 collective-permute-done.other_ref
  15.5 0.0 copy-done.2
  15.6 0.2 pack.1
  15.7 19.8 %all_to_all.20.terms_ref = bf16[16,288,128]{2,1,0:T(8,128)(2,1)S(1)} all-to-all(bf16[16,288,128]{2,1,0:T(8,128)(2,1)S(1)} %pack.1), channel_id=1, replica_groups=mesh['x'=4,'yl'=2,'z4'=4,'zp'=2,'yh'=4,'core'=2] {'x','yl','zp'}, dimensions={0} | all-to-all | bytes 2359296 | tf_op jit(solution)/shard_map/all_to_all | solution.py:283
  35.5 0.2 reduce.1
  35.7 26.3 %all_to_all.21.parts_here_ref.parts_ref = bf16[16,96,128]{2,1,0:T(8,128)(2,1)S(1)} all-to-all(bf16[16,96,128]{2,1,0:T(8,128)(2,1)S(1)} %reduce.1), channel_id=1, replica_groups=mesh['x'=4,'yl'=2,'z4'=4,'zp'=2,'yh'=4,'core'=2] {'z4','yh'}, dimensions={0} | all-to-all | bytes 786432 | tf_op jit(solution)/shard_map/all_to_all | solution.py:283
  62.0 0.7 total.1
  62.8 8.2 %all-to-all-start.2 = ((bf16[64,16,128]{2,1,0:T(8,128)(2,1)}), bf16[64,16,128]{2,1,0:T(8,128)(2,1)S(1)}, u32[]{:S(2)}, u32[]{:S(2)}) async-start(bf16[64,16,128]{2,1,0:T(8,128)(2,1)} %total.1), calls=%async_computation.2 | async-start | bytes 524288 | tf_op jit(solution)/shard_map/all_to_all | solution.py:283
  71.0 3.0 %collective-permute-start.1 = (bf16[16,96,128]{2,1,0:T(8,128)(2,1)S(1)}, bf16[16,96,128]{2,1,0:T(8,128)(2,1)S(1)}, u32[]{:S(2)}, u32[]{:S(2)}) collective-permute-start(bf16[16,96,128]{2,1,0:T(8,128)(2,1)S(1)} %all_to_all.21.parts_here_ref.parts_ref), channel_id=1, source_target_pairs={{0,1},{1,0},{2,3},{3,2},{4,5},{5,4},{6,7},{7,6},{8,9},{9,8},{10,11... | collective-permute-start | bytes 1179656 | tf_op jit(solution)/shard_map/ppermute | solution.py:302
  74.0 9.5 %all-to-all-done.2.tiles_here_ref = bf16[64,16,128]{2,1,0:T(8,128)(2,1)S(1)} async-done(((bf16[64,16,128]{2,1,0:T(8,128)(2,1)}), bf16[64,16,128]{2,1,0:T(8,128)(2,1)S(1)}, u32[]{:S(2)}, u32[]{:S(2)}) %all-to-all-start.2) | async-done | bytes 262176 | tf_op jit(solution)/shard_map/all_to_all | solution.py:283
  83.5 5.2 %collective-permute-start.2 = (bf16[64,16,128]{2,1,0:T(8,128)(2,1)S(1)}, bf16[64,16,128]{2,1,0:T(8,128)(2,1)S(1)}, u32[]{:S(2)}, u32[]{:S(2)}) collective-permute-start(bf16[64,16,128]{2,1,0:T(8,128)(2,1)S(1)} %all-to-all-done.2.tiles_here_ref), channel_id=1, source_target_pairs={{0,1},{1,0},{2,3},{3,2},{4,5},{5,4},{6,7},{7,6},{8,9},{9,8},{10,11... | collective-permute-start | bytes 786440 | tf_op jit(solution)/shard_map/ppermute | solution.py:302
  88.7 0.0 collective-permute-done.1.parts_there_ref
  88.7 0.4 unpack.1.stats
  89.1 0.7 collective-permute-done.2.tiles_there_ref
  89.8 4.9 %root.1 = f32[4,24,512]{2,1,0:T(8,128)S(1)} custom-call(s32[8,128]{1,0:T(8,128)S(1)} %get-tuple-element.6.owners_ref, f32[2,512,512]{2,1,0:T(8,128)S(1)} %unpack.1.stats, bf16[64,16,128]{2,1,0:T(8,128)(2,1)S(1)} %all-to-all-done.2.tiles_here_ref, bf16[64,16,128]{2,1,0:T(8,128)(2,1)S(1)} %collective-permute-done.2.tiles_there_ref), custom_call_target="tpu_custom_call" | custom-call | tf_op jit(solution)/shard_map/root/pallas_call | solution.py:290
  94.7 7.7 %all_to_all.22.pieces_ref = f32[4,24,512]{2,1,0:T(8,128)S(1)} all-to-all(f32[4,24,512]{2,1,0:T(8,128)S(1)} %root.1), channel_id=1, replica_groups=mesh['x'=4,'yl'=2,'z4'=4,'zp'=2,'yh'=4,'core'=2] {'x'}, dimensions={0} | all-to-all | bytes 393216 | tf_op jit(solution)/shard_map/all_to_all | solution.py:283
  102.4 0.7 join.1
Async XLA Ops:
  0.6 12.4 %copy-start.1 = (bf16[768,1024]{1,0:T(8,128)(2,1)S(1)}, bf16[768,1024]{1,0:T(8,128)(2,1)}, u32[]{:S(2)}) copy-start(bf16[768,1024]{1,0:T(8,128)(2,1)} %cot_hbm.1) | copy-start | bytes 4718596
  0.6 12.4 %copy-start = (bf16[768,1024]{1,0:T(8,128)(2,1)S(1)}, bf16[768,1024]{1,0:T(8,128)(2,1)}, u32[]{:S(2)}) copy-start(bf16[768,1024]{1,0:T(8,128)(2,1)} %act_hbm.1) | copy-start | bytes 4718596
  0.6 12.4 %copy-start.3 = (s32[8]{0:T(128)S(1)}, s32[8]{0:T(128)}, u32[]{:S(2)}) copy-start(s32[8]{0:T(128)} %owner_ref.1) | copy-start | bytes 100
  4.3 11.3 %copy-start.2 = (f32[1,8,512]{2,1,0:T(8,128)S(1)}, f32[1,8,512]{2,1,0:T(8,128)}, u32[]{:S(2)}) copy-start(f32[1,8,512]{2,1,0:T(8,128)} %param.6) | copy-start | bytes 49156
  4.3 11.3 %collective-permute-start = (bf16[4,4,256,128]{3,2,1,0:T(8,128)(2,1)}, bf16[4,4,256,128]{3,2,1,0:T(8,128)(2,1)S(1)}, u32[]{:S(2)}, u32[]{:S(2)}) collective-permute-start(bf16[4,4,256,128]{3,2,1,0:T(8,128)(2,1)} %grad_theirs.1), channel_id=1, source_target_pairs={{0,1},{1,0},{2,3},{3,2},{4,5},{5,4},{6,7},{7,6},{8,9},{9,8},{10,11... | collective-permute-start | bytes 3145736 | tf_op jit(solution)/shard_map/ppermute | solution.py:302
  62.8 20.7 %all-to-all-start.2 = ((bf16[64,16,128]{2,1,0:T(8,128)(2,1)}), bf16[64,16,128]{2,1,0:T(8,128)(2,1)S(1)}, u32[]{:S(2)}, u32[]{:S(2)}) async-start(bf16[64,16,128]{2,1,0:T(8,128)(2,1)} %total.1), calls=%async_computation.2 | async-start | bytes 524288 | tf_op jit(solution)/shard_map/all_to_all | solution.py:283
  71.0 17.7 %collective-permute-start.1 = (bf16[16,96,128]{2,1,0:T(8,128)(2,1)S(1)}, bf16[16,96,128]{2,1,0:T(8,128)(2,1)S(1)}, u32[]{:S(2)}, u32[]{:S(2)}) collective-permute-start(bf16[16,96,128]{2,1,0:T(8,128)(2,1)S(1)} %all_to_all.21.parts_here_ref.parts_ref), channel_id=1, source_target_pairs={{0,1},{1,0},{2,3},{3,2},{4,5},{5,4},{6,7},{7,6},{8,9},{9,8},{10,11... | collective-permute-start | bytes 1179656 | tf_op jit(solution)/shard_map/ppermute | solution.py:302
  83.5 6.3 %collective-permute-start.2 = (bf16[64,16,128]{2,1,0:T(8,128)(2,1)S(1)}, bf16[64,16,128]{2,1,0:T(8,128)(2,1)S(1)}, u32[]{:S(2)}, u32[]{:S(2)}) collective-permute-start(bf16[64,16,128]{2,1,0:T(8,128)(2,1)S(1)} %all-to-all-done.2.tiles_here_ref), channel_id=1, source_target_pairs={{0,1},{1,0},{2,3},{3,2},{4,5},{5,4},{6,7},{7,6},{8,9},{9,8},{10,11... | collective-permute-start | bytes 786440 | tf_op jit(solution)/shard_map/ppermute | solution.py:302

commit v11 on v10

--- a/solution.py
+++ b/solution.py
@@ -149,13 +149,20 @@
             out_ref[part, TILE * (group + 1) : TILE * (group + 2)] = stats[group]
 
 
-def total_kernel(parts_ref, gradient_ref):
+def total_kernel(parts_ref, gradient_hbm, copies_ref, sems):
     total = parts_ref[0, :TILE].astype(f32)
     for part in range(1, FAR):
         total += parts_ref[part, :TILE].astype(f32)
     gradient = total.astype(bf16)
-    for part in range(PARTS):
-        gradient_ref[part] = gradient
+    for part in range(FAR):
+        copies_ref[part] = gradient
+    sent = []
+    for quad in range(QUADS):
+        place = pl.ds(quad * FAR, FAR)
+        sent.append(pltpu.make_async_copy(copies_ref, gradient_hbm.at[place], sems.at[quad]))
+        sent[-1].start()
+    for copy in sent:
+        copy.wait()
 
 
 def unpack_kernel(parts_here_ref, parts_there_ref, stats):
@@ -165,6 +172,7 @@
             row_block, column = divmod(part, 4)
             for group, (side, lane) in enumerate(sent_groups(row_block)):
                 value = parts_ref[part, TILE * (group + 1) : TILE * (group + 2)].astype(f32)
+                value = ema_decay * value
                 for low in range(PAIR):
                     shard = (row_block * PAIR + low) * 8 + column * CORES + at
                     place = pl.ds(pl.multiple_of(shard * OWN_ROWS, OWN_ROWS), OWN_ROWS)
@@ -199,7 +207,7 @@
 
 def newton(stats, gram):
     sides = range(2)
-    updated = [ema_decay * stats[side] + (1.0 - ema_decay) * gram[side] for side in sides]
+    updated = [stats[side] + (1.0 - ema_decay) * gram[side] for side in sides]
     scales = [jnp.sqrt(jnp.sum(value * value, keepdims=True) + 1e-06) for value in updated]
 
     def step(state):
@@ -251,6 +259,11 @@
     start = pl.multiple_of(position % (BLOCK // OUT_ROWS) * OUT_ROWS, OUT_ROWS)
     states = newton(stats, gram)
     left, right = [[state[side] for state in states] for side in range(2)]
+    shape = (BLOCK, BLOCK)
+    diagonal = lax.broadcasted_iota(jnp.int32, shape, 0) == lax.broadcasted_iota(jnp.int32, shape, 1)
+    right_root = root_rows(
+        right, right[1], right[2], jnp.where(diagonal, 1.0, 0.0), symmetric
+    ).astype(bf16)
     for number in range(3):
         rows[number] = left[number]
     own = tuple(rows[number, pl.ds(start, OUT_ROWS), :] for number in range(3))
@@ -259,11 +272,6 @@
     left_rows = root_rows(own, left[1], left[2], jnp.where(diagonal, 1.0, 0.0)).astype(bf16)
     mixed = jnp.dot(left_rows, grad[...], preferred_element_type=f32).astype(bf16)
 
-    shape = (BLOCK, BLOCK)
-    diagonal = lax.broadcasted_iota(jnp.int32, shape, 0) == lax.broadcasted_iota(jnp.int32, shape, 1)
-    right_root = root_rows(
-        right, right[1], right[2], jnp.where(diagonal, 1.0, 0.0), symmetric
-    ).astype(bf16)
     piece = jnp.dot(mixed, right_root, preferred_element_type=f32)
     for receiver in range(XS):
         out_ref[receiver, :OUT_ROWS] = piece
@@ -283,15 +291,17 @@
     return lax.all_to_all(value, axes, split_axis=0, concat_axis=0, tiled=True)
 
 
-def call(kernel, name, outs, arrays, scratch=(), limit=VMEM_LIMIT):
-    vmem = pl.BlockSpec(memory_space=pltpu.VMEM)
-    smem = pl.BlockSpec(memory_space=pltpu.SMEM)
-    rest = pl.BlockSpec(memory_space=pl.ANY) if limit > VMEM_LIMIT else vmem
+vmem = pl.BlockSpec(memory_space=pltpu.VMEM)
+smem = pl.BlockSpec(memory_space=pltpu.SMEM)
+anywhere = pl.BlockSpec(memory_space=pl.ANY)
+
+
+def call(kernel, name, outs, arrays, scratch=(), limit=VMEM_LIMIT, operands=vmem, results=vmem):
     return pl.pallas_call(
         kernel,
         out_shape=outs,
-        in_specs=[smem if array.ndim == 1 else rest for array in arrays],
-        out_specs=tuple(rest for _ in outs) if isinstance(outs, tuple) else rest,
+        in_specs=[smem if array.ndim == 1 else operands for array in arrays],
+        out_specs=tuple(results for _ in outs) if isinstance(outs, tuple) else results,
         scratch_shapes=list(scratch),
         compiler_params=pltpu.CompilerParams(vmem_limit_bytes=limit),
         name=name,
@@ -320,6 +330,8 @@
             pltpu.SemaphoreType.DMA((BLOCKS,)),
         ],
         limit=GRAD_LIMIT,
+        operands=anywhere,
+        results=anywhere,
     )
     mine, owners = call(
         mine_kernel,
@@ -340,7 +352,14 @@
         (owners, exchange(packed, NEAR_AXES)),
     )
     parts = exchange(reduced, FAR_AXES)
-    gradient = call(total_kernel, "total", array((PARTS, TILE, LANES), bf16), (parts,))
+    gradient = call(
+        total_kernel,
+        "total",
+        array((PARTS, TILE, LANES), bf16),
+        (parts,),
+        scratch=[pltpu.VMEM((FAR, TILE, LANES), bf16), pltpu.SemaphoreType.DMA((QUADS,))],
+        results=anywhere,
+    )
     rows = call(
         unpack_kernel, "unpack", array((2, BLOCK, BLOCK), f32), (parts, swap(parts, "core"))
     )

time: 103 us -> 103 us (level)
  no operation moved by 1% of the time
where the time goes in v11:
time: 103 us
  blocking collectives  53.7 us (52%)
  starting transfers between devices  25.2 us (24%)
  Pallas kernels  12.3 us (12%)
  waiting for transfers between devices  11.1 us (11%)
    all_to_all x3, blocking collectives, exchange(): return lax.all_to_all(value, axes, split_axis=0, concat_axis=0, tiled=True)  53.7 us
    ppermute x3, starting transfers between devices, swap(): return lax.ppermute(value, axis, [(0, 1), (1, 0)])  17 us
    pallas_call x8, Pallas kernels, call(): pl.pallas_call(kernel, out_shape=outs, in_specs=[smem if array.ndim == 1...  12.3 us
    all_to_all x1, waiting for transfers between devices, exchange(): return lax.all_to_all(value, axes, split_axis=0, concat_axis=0, tiled=True)  9.55 us
    all_to_all x1, starting transfers between devices, exchange(): return lax.all_to_all(value, axes, split_axis=0, concat_axis=0, tiled=True)  8.22 us
  transfers between devices with their start and end apart: 4, of which 3 were waited for; matrix products, arithmetic and copies ran while one was open for 0% of the time, Pallas kernels for 2%

profile of v11, /device:TPU:1, one launch (start us, length us, event | category | flops | bytes accessed | tf_op | source)
XLA Modules:
  0.0 103.1 jit_solution(7021874585753562547)
XLA Ops:
  0.6 0.0 copy-start.1
  0.6 0.0 copy-start
  0.6 0.0 copy-start.3
  0.7 3.6 %grad_theirs.1 = bf16[4,4,256,128]{3,2,1,0:T(8,128)(2,1)} custom-call(bf16[768,1024]{1,0:T(8,128)(2,1)} %act_hbm.1, bf16[768,1024]{1,0:T(8,128)(2,1)} %cot_hbm.1), custom_call_target="tpu_custom_call" | custom-call | tf_op jit(solution)/shard_map/grad_theirs/pallas_call | solution.py:300
  4.3 0.0 copy-start.2
  4.3 8.8 %collective-permute-start = (bf16[4,4,256,128]{3,2,1,0:T(8,128)(2,1)}, bf16[4,4,256,128]{3,2,1,0:T(8,128)(2,1)S(1)}, u32[]{:S(2)}, u32[]{:S(2)}) collective-permute-start(bf16[4,4,256,128]{3,2,1,0:T(8,128)(2,1)} %grad_theirs.1), channel_id=1, source_target_pairs={{0,1},{1,0},{2,3},{3,2},{4,5},{5,4},{6,7},{7,6},{8,9},{9,8},{10,11... | collective-permute-start | bytes 3145736 | tf_op jit(solution)/shard_map/ppermute | solution.py:312
  13.1 0.0 copy-done.1
  13.1 0.0 copy-done
  13.1 0.0 copy-done.3
  13.1 1.6 %grad_mine.1 = (f32[4,4,256,128]{3,2,1,0:T(8,128)S(1)}, s32[8,128]{1,0:T(8,128)S(1)}) custom-call(s32[8]{0:T(128)S(1)} %copy-done.3, bf16[768,1024]{1,0:T(8,128)(2,1)S(1)} %copy-done, bf16[768,1024]{1,0:T(8,128)(2,1)S(1)} %copy-done.1), custom_call_target="tpu_custom_call" | custom-call | tf_op jit(solution)/shard_map/grad_mine/pallas_call | solution.py:300
  14.7 0.8 collective-permute-done.other_ref
  15.5 0.0 copy-done.2
  15.6 0.2 pack.1
  15.7 19.8 %all_to_all.20.terms_ref = bf16[16,288,128]{2,1,0:T(8,128)(2,1)S(1)} all-to-all(bf16[16,288,128]{2,1,0:T(8,128)(2,1)S(1)} %pack.1), channel_id=1, replica_groups=mesh['x'=4,'yl'=2,'z4'=4,'zp'=2,'yh'=4,'core'=2] {'x','yl','zp'}, dimensions={0} | all-to-all | bytes 2359296 | tf_op jit(solution)/shard_map/all_to_all | solution.py:291
  35.5 0.2 reduce.1
  35.7 26.3 %all_to_all.21.parts_here_ref.parts_ref = bf16[16,96,128]{2,1,0:T(8,128)(2,1)S(1)} all-to-all(bf16[16,96,128]{2,1,0:T(8,128)(2,1)S(1)} %reduce.1), channel_id=1, replica_groups=mesh['x'=4,'yl'=2,'z4'=4,'zp'=2,'yh'=4,'core'=2] {'z4','yh'}, dimensions={0} | all-to-all | bytes 786432 | tf_op jit(solution)/shard_map/all_to_all | solution.py:291
  62.0 0.8 total.1
  62.8 8.2 %all-to-all-start.2 = ((bf16[64,16,128]{2,1,0:T(8,128)(2,1)}), bf16[64,16,128]{2,1,0:T(8,128)(2,1)S(1)}, u32[]{:S(2)}, u32[]{:S(2)}) async-start(bf16[64,16,128]{2,1,0:T(8,128)(2,1)} %total.1), calls=%async_computation.2 | async-start | bytes 524288 | tf_op jit(solution)/shard_map/all_to_all | solution.py:291
  71.0 3.0 %collective-permute-start.1 = (bf16[16,96,128]{2,1,0:T(8,128)(2,1)S(1)}, bf16[16,96,128]{2,1,0:T(8,128)(2,1)S(1)}, u32[]{:S(2)}, u32[]{:S(2)}) collective-permute-start(bf16[16,96,128]{2,1,0:T(8,128)(2,1)S(1)} %all_to_all.21.parts_here_ref.parts_ref), channel_id=1, source_target_pairs={{0,1},{1,0},{2,3},{3,2},{4,5},{5,4},{6,7},{7,6},{8,9},{9,8},{10,11... | collective-permute-start | bytes 1179656 | tf_op jit(solution)/shard_map/ppermute | solution.py:312
  74.0 9.5 %all-to-all-done.2.tiles_here_ref = bf16[64,16,128]{2,1,0:T(8,128)(2,1)S(1)} async-done(((bf16[64,16,128]{2,1,0:T(8,128)(2,1)}), bf16[64,16,128]{2,1,0:T(8,128)(2,1)S(1)}, u32[]{:S(2)}, u32[]{:S(2)}) %all-to-all-start.2) | async-done | bytes 262176 | tf_op jit(solution)/shard_map/all_to_all | solution.py:291
  83.5 5.2 %collective-permute-start.2 = (bf16[64,16,128]{2,1,0:T(8,128)(2,1)S(1)}, bf16[64,16,128]{2,1,0:T(8,128)(2,1)S(1)}, u32[]{:S(2)}, u32[]{:S(2)}) collective-permute-start(bf16[64,16,128]{2,1,0:T(8,128)(2,1)S(1)} %all-to-all-done.2.tiles_here_ref), channel_id=1, source_target_pairs={{0,1},{1,0},{2,3},{3,2},{4,5},{5,4},{6,7},{7,6},{8,9},{9,8},{10,11... | collective-permute-start | bytes 786440 | tf_op jit(solution)/shard_map/ppermute | solution.py:312
  88.7 0.0 collective-permute-done.1.parts_there_ref
  88.8 0.5 unpack.1.stats
  89.2 0.7 collective-permute-done.2.tiles_there_ref
  89.9 4.9 %root.1 = f32[4,24,512]{2,1,0:T(8,128)S(1)} custom-call(s32[8,128]{1,0:T(8,128)S(1)} %get-tuple-element.6.owners_ref, f32[2,512,512]{2,1,0:T(8,128)S(1)} %unpack.1.stats, bf16[64,16,128]{2,1,0:T(8,128)(2,1)S(1)} %all-to-all-done.2.tiles_here_ref, bf16[64,16,128]{2,1,0:T(8,128)(2,1)S(1)} %collective-permute-done.2.tiles_there_ref), custom_call_target="tpu_custom_call" | custom-call | tf_op jit(solution)/shard_map/root/pallas_call | solution.py:300
  94.8 7.7 %all_to_all.22.pieces_ref = f32[4,24,512]{2,1,0:T(8,128)S(1)} all-to-all(f32[4,24,512]{2,1,0:T(8,128)S(1)} %root.1), channel_id=1, replica_groups=mesh['x'=4,'yl'=2,'z4'=4,'zp'=2,'yh'=4,'core'=2] {'x'}, dimensions={0} | all-to-all | bytes 393216 | tf_op jit(solution)/shard_map/all_to_all | solution.py:291
  102.4 0.7 join.1
Async XLA Ops:
  0.6 12.4 %copy-start.1 = (bf16[768,1024]{1,0:T(8,128)(2,1)S(1)}, bf16[768,1024]{1,0:T(8,128)(2,1)}, u32[]{:S(2)}) copy-start(bf16[768,1024]{1,0:T(8,128)(2,1)} %cot_hbm.1) | copy-start | bytes 4718596
  0.6 12.4 %copy-start = (bf16[768,1024]{1,0:T(8,128)(2,1)S(1)}, bf16[768,1024]{1,0:T(8,128)(2,1)}, u32[]{:S(2)}) copy-start(bf16[768,1024]{1,0:T(8,128)(2,1)} %act_hbm.1) | copy-start | bytes 4718596
  0.6 12.4 %copy-start.3 = (s32[8]{0:T(128)S(1)}, s32[8]{0:T(128)}, u32[]{:S(2)}) copy-start(s32[8]{0:T(128)} %owner_ref.1) | copy-start | bytes 100
  4.3 11.3 %copy-start.2 = (f32[1,8,512]{2,1,0:T(8,128)S(1)}, f32[1,8,512]{2,1,0:T(8,128)}, u32[]{:S(2)}) copy-start(f32[1,8,512]{2,1,0:T(8,128)} %param.6) | copy-start | bytes 49156
  4.3 11.3 %collective-permute-start = (bf16[4,4,256,128]{3,2,1,0:T(8,128)(2,1)}, bf16[4,4,256,128]{3,2,1,0:T(8,128)(2,1)S(1)}, u32[]{:S(2)}, u32[]{:S(2)}) collective-permute-start(bf16[4,4,256,128]{3,2,1,0:T(8,128)(2,1)} %grad_theirs.1), channel_id=1, source_target_pairs={{0,1},{1,0},{2,3},{3,2},{4,5},{5,4},{6,7},{7,6},{8,9},{9,8},{10,11... | collective-permute-start | bytes 3145736 | tf_op jit(solution)/shard_map/ppermute | solution.py:312
  62.8 20.8 %all-to-all-start.2 = ((bf16[64,16,128]{2,1,0:T(8,128)(2,1)}), bf16[64,16,128]{2,1,0:T(8,128)(2,1)S(1)}, u32[]{:S(2)}, u32[]{:S(2)}) async-start(bf16[64,16,128]{2,1,0:T(8,128)(2,1)} %total.1), calls=%async_computation.2 | async-start | bytes 524288 | tf_op jit(solution)/shard_map/all_to_all | solution.py:291
  71.0 17.7 %collective-permute-start.1 = (bf16[16,96,128]{2,1,0:T(8,128)(2,1)S(1)}, bf16[16,96,128]{2,1,0:T(8,128)(2,1)S(1)}, u32[]{:S(2)}, u32[]{:S(2)}) collective-permute-start(bf16[16,96,128]{2,1,0:T(8,128)(2,1)S(1)} %all_to_all.21.parts_here_ref.parts_ref), channel_id=1, source_target_pairs={{0,1},{1,0},{2,3},{3,2},{4,5},{5,4},{6,7},{7,6},{8,9},{9,8},{10,11... | collective-permute-start | bytes 1179656 | tf_op jit(solution)/shard_map/ppermute | solution.py:312
  83.5 6.3 %collective-permute-start.2 = (bf16[64,16,128]{2,1,0:T(8,128)(2,1)S(1)}, bf16[64,16,128]{2,1,0:T(8,128)(2,1)S(1)}, u32[]{:S(2)}, u32[]{:S(2)}) collective-permute-start(bf16[64,16,128]{2,1,0:T(8,128)(2,1)S(1)} %all-to-all-done.2.tiles_here_ref), channel_id=1, source_target_pairs={{0,1},{1,0},{2,3},{3,2},{4,5},{5,4},{6,7},{7,6},{8,9},{9,8},{10,11... | collective-permute-start | bytes 786440 | tf_op jit(solution)/shard_map/ppermute | solution.py:312

commit v12 on v10

--- a/solution.py
+++ b/solution.py
@@ -165,6 +165,7 @@
             row_block, column = divmod(part, 4)
             for group, (side, lane) in enumerate(sent_groups(row_block)):
                 value = parts_ref[part, TILE * (group + 1) : TILE * (group + 2)].astype(f32)
+                value = ema_decay * value
                 for low in range(PAIR):
                     shard = (row_block * PAIR + low) * 8 + column * CORES + at
                     place = pl.ds(pl.multiple_of(shard * OWN_ROWS, OWN_ROWS), OWN_ROWS)
@@ -199,7 +200,7 @@
 
 def newton(stats, gram):
     sides = range(2)
-    updated = [ema_decay * stats[side] + (1.0 - ema_decay) * gram[side] for side in sides]
+    updated = [stats[side] + (1.0 - ema_decay) * gram[side] for side in sides]
     scales = [jnp.sqrt(jnp.sum(value * value, keepdims=True) + 1e-06) for value in updated]
 
     def step(state):
@@ -251,6 +252,11 @@
     start = pl.multiple_of(position % (BLOCK // OUT_ROWS) * OUT_ROWS, OUT_ROWS)
     states = newton(stats, gram)
     left, right = [[state[side] for state in states] for side in range(2)]
+    shape = (BLOCK, BLOCK)
+    diagonal = lax.broadcasted_iota(jnp.int32, shape, 0) == lax.broadcasted_iota(jnp.int32, shape, 1)
+    right_root = root_rows(
+        right, right[1], right[2], jnp.where(diagonal, 1.0, 0.0), symmetric
+    ).astype(bf16)
     for number in range(3):
         rows[number] = left[number]
     own = tuple(rows[number, pl.ds(start, OUT_ROWS), :] for number in range(3))
@@ -259,11 +265,6 @@
     left_rows = root_rows(own, left[1], left[2], jnp.where(diagonal, 1.0, 0.0)).astype(bf16)
     mixed = jnp.dot(left_rows, grad[...], preferred_element_type=f32).astype(bf16)
 
-    shape = (BLOCK, BLOCK)
-    diagonal = lax.broadcasted_iota(jnp.int32, shape, 0) == lax.broadcasted_iota(jnp.int32, shape, 1)
-    right_root = root_rows(
-        right, right[1], right[2], jnp.where(diagonal, 1.0, 0.0), symmetric
-    ).astype(bf16)
     piece = jnp.dot(mixed, right_root, preferred_element_type=f32)
     for receiver in range(XS):
         out_ref[receiver, :OUT_ROWS] = piece

time: 103 us -> 103 us (level)
  no operation moved by 1% of the time
where the time goes in v12:
time: 103 us
  blocking collectives  53.7 us (52%)
  starting transfers between devices  25.2 us (24%)
  Pallas kernels  12.3 us (12%)
  waiting for transfers between devices  11.1 us (11%)
    all_to_all x3, blocking collectives, exchange(): return lax.all_to_all(value, axes, split_axis=0, concat_axis=0, tiled=True)  53.7 us
    ppermute x3, starting transfers between devices, swap(): return lax.ppermute(value, axis, [(0, 1), (1, 0)])  17 us
    pallas_call x8, Pallas kernels, call(): pl.pallas_call(kernel, out_shape=outs, in_specs=[smem if array.ndim == 1...  12.3 us
    all_to_all x1, waiting for transfers between devices, exchange(): return lax.all_to_all(value, axes, split_axis=0, concat_axis=0, tiled=True)  9.55 us
    all_to_all x1, starting transfers between devices, exchange(): return lax.all_to_all(value, axes, split_axis=0, concat_axis=0, tiled=True)  8.21 us
  transfers between devices with their start and end apart: 4, of which 3 were waited for; matrix products, arithmetic and copies ran while one was open for 0% of the time, Pallas kernels for 2%

profile of v12, /device:TPU:1, one launch (start us, length us, event | category | flops | bytes accessed | tf_op | source)
XLA Modules:
  0.0 103.1 jit_solution(531442760224214537)
XLA Ops:
  0.6 0.0 copy-start.1
  0.6 0.0 copy-start
  0.6 0.0 copy-start.3
  0.7 3.6 %grad_theirs.1 = bf16[4,4,256,128]{3,2,1,0:T(8,128)(2,1)} custom-call(bf16[768,1024]{1,0:T(8,128)(2,1)} %act_hbm.1, bf16[768,1024]{1,0:T(8,128)(2,1)} %cot_hbm.1), custom_call_target="tpu_custom_call" | custom-call | tf_op jit(solution)/shard_map/grad_theirs/pallas_call | solution.py:291
  4.3 0.0 copy-start.2
  4.3 8.8 %collective-permute-start = (bf16[4,4,256,128]{3,2,1,0:T(8,128)(2,1)}, bf16[4,4,256,128]{3,2,1,0:T(8,128)(2,1)S(1)}, u32[]{:S(2)}, u32[]{:S(2)}) collective-permute-start(bf16[4,4,256,128]{3,2,1,0:T(8,128)(2,1)} %grad_theirs.1), channel_id=1, source_target_pairs={{0,1},{1,0},{2,3},{3,2},{4,5},{5,4},{6,7},{7,6},{8,9},{9,8},{10,11... | collective-permute-start | bytes 3145736 | tf_op jit(solution)/shard_map/ppermute | solution.py:303
  13.1 0.0 copy-done.1
  13.1 0.0 copy-done
  13.1 0.0 copy-done.3
  13.1 1.6 %grad_mine.1 = (f32[4,4,256,128]{3,2,1,0:T(8,128)S(1)}, s32[8,128]{1,0:T(8,128)S(1)}) custom-call(s32[8]{0:T(128)S(1)} %copy-done.3, bf16[768,1024]{1,0:T(8,128)(2,1)S(1)} %copy-done, bf16[768,1024]{1,0:T(8,128)(2,1)S(1)} %copy-done.1), custom_call_target="tpu_custom_call" | custom-call | tf_op jit(solution)/shard_map/grad_mine/pallas_call | solution.py:291
  14.7 0.8 collective-permute-done.other_ref
  15.5 0.0 copy-done.2
  15.6 0.2 pack.1
  15.7 19.8 %all_to_all.20.terms_ref = bf16[16,288,128]{2,1,0:T(8,128)(2,1)S(1)} all-to-all(bf16[16,288,128]{2,1,0:T(8,128)(2,1)S(1)} %pack.1), channel_id=1, replica_groups=mesh['x'=4,'yl'=2,'z4'=4,'zp'=2,'yh'=4,'core'=2] {'x','yl','zp'}, dimensions={0} | all-to-all | bytes 2359296 | tf_op jit(solution)/shard_map/all_to_all | solution.py:284
  35.5 0.2 reduce.1
  35.7 26.3 %all_to_all.21.parts_here_ref.parts_ref = bf16[16,96,128]{2,1,0:T(8,128)(2,1)S(1)} all-to-all(bf16[16,96,128]{2,1,0:T(8,128)(2,1)S(1)} %reduce.1), channel_id=1, replica_groups=mesh['x'=4,'yl'=2,'z4'=4,'zp'=2,'yh'=4,'core'=2] {'z4','yh'}, dimensions={0} | all-to-all | bytes 786432 | tf_op jit(solution)/shard_map/all_to_all | solution.py:284
  62.0 0.7 total.1
  62.8 8.2 %all-to-all-start.2 = ((bf16[64,16,128]{2,1,0:T(8,128)(2,1)}), bf16[64,16,128]{2,1,0:T(8,128)(2,1)S(1)}, u32[]{:S(2)}, u32[]{:S(2)}) async-start(bf16[64,16,128]{2,1,0:T(8,128)(2,1)} %total.1), calls=%async_computation.2 | async-start | bytes 524288 | tf_op jit(solution)/shard_map/all_to_all | solution.py:284
  71.0 3.0 %collective-permute-start.1 = (bf16[16,96,128]{2,1,0:T(8,128)(2,1)S(1)}, bf16[16,96,128]{2,1,0:T(8,128)(2,1)S(1)}, u32[]{:S(2)}, u32[]{:S(2)}) collective-permute-start(bf16[16,96,128]{2,1,0:T(8,128)(2,1)S(1)} %all_to_all.21.parts_here_ref.parts_ref), channel_id=1, source_target_pairs={{0,1},{1,0},{2,3},{3,2},{4,5},{5,4},{6,7},{7,6},{8,9},{9,8},{10,11... | collective-permute-start | bytes 1179656 | tf_op jit(solution)/shard_map/ppermute | solution.py:303
  74.0 9.5 %all-to-all-done.2.tiles_here_ref = bf16[64,16,128]{2,1,0:T(8,128)(2,1)S(1)} async-done(((bf16[64,16,128]{2,1,0:T(8,128)(2,1)}), bf16[64,16,128]{2,1,0:T(8,128)(2,1)S(1)}, u32[]{:S(2)}, u32[]{:S(2)}) %all-to-all-start.2) | async-done | bytes 262176 | tf_op jit(solution)/shard_map/all_to_all | solution.py:284
  83.5 5.2 %collective-permute-start.2 = (bf16[64,16,128]{2,1,0:T(8,128)(2,1)S(1)}, bf16[64,16,128]{2,1,0:T(8,128)(2,1)S(1)}, u32[]{:S(2)}, u32[]{:S(2)}) collective-permute-start(bf16[64,16,128]{2,1,0:T(8,128)(2,1)S(1)} %all-to-all-done.2.tiles_here_ref), channel_id=1, source_target_pairs={{0,1},{1,0},{2,3},{3,2},{4,5},{5,4},{6,7},{7,6},{8,9},{9,8},{10,11... | collective-permute-start | bytes 786440 | tf_op jit(solution)/shard_map/ppermute | solution.py:303
  88.7 0.0 collective-permute-done.1.parts_there_ref
  88.7 0.5 unpack.1.stats
  89.2 0.7 collective-permute-done.2.tiles_there_ref
  89.8 4.9 %root.1 = f32[4,24,512]{2,1,0:T(8,128)S(1)} custom-call(s32[8,128]{1,0:T(8,128)S(1)} %get-tuple-element.6.owners_ref, f32[2,512,512]{2,1,0:T(8,128)S(1)} %unpack.1.stats, bf16[64,16,128]{2,1,0:T(8,128)(2,1)S(1)} %all-to-all-done.2.tiles_here_ref, bf16[64,16,128]{2,1,0:T(8,128)(2,1)S(1)} %collective-permute-done.2.tiles_there_ref), custom_call_target="tpu_custom_call" | custom-call | tf_op jit(solution)/shard_map/root/pallas_call | solution.py:291
  94.7 7.7 %all_to_all.22.pieces_ref = f32[4,24,512]{2,1,0:T(8,128)S(1)} all-to-all(f32[4,24,512]{2,1,0:T(8,128)S(1)} %root.1), channel_id=1, replica_groups=mesh['x'=4,'yl'=2,'z4'=4,'zp'=2,'yh'=4,'core'=2] {'x'}, dimensions={0} | all-to-all | bytes 393216 | tf_op jit(solution)/shard_map/all_to_all | solution.py:284
  102.4 0.7 join.1
Async XLA Ops:
  0.6 12.4 %copy-start.1 = (bf16[768,1024]{1,0:T(8,128)(2,1)S(1)}, bf16[768,1024]{1,0:T(8,128)(2,1)}, u32[]{:S(2)}) copy-start(bf16[768,1024]{1,0:T(8,128)(2,1)} %cot_hbm.1) | copy-start | bytes 4718596
  0.6 12.4 %copy-start = (bf16[768,1024]{1,0:T(8,128)(2,1)S(1)}, bf16[768,1024]{1,0:T(8,128)(2,1)}, u32[]{:S(2)}) copy-start(bf16[768,1024]{1,0:T(8,128)(2,1)} %act_hbm.1) | copy-start | bytes 4718596
  0.6 12.4 %copy-start.3 = (s32[8]{0:T(128)S(1)}, s32[8]{0:T(128)}, u32[]{:S(2)}) copy-start(s32[8]{0:T(128)} %owner_ref.1) | copy-start | bytes 100
  4.3 11.3 %copy-start.2 = (f32[1,8,512]{2,1,0:T(8,128)S(1)}, f32[1,8,512]{2,1,0:T(8,128)}, u32[]{:S(2)}) copy-start(f32[1,8,512]{2,1,0:T(8,128)} %param.6) | copy-start | bytes 49156
  4.3 11.3 %collective-permute-start = (bf16[4,4,256,128]{3,2,1,0:T(8,128)(2,1)}, bf16[4,4,256,128]{3,2,1,0:T(8,128)(2,1)S(1)}, u32[]{:S(2)}, u32[]{:S(2)}) collective-permute-start(bf16[4,4,256,128]{3,2,1,0:T(8,128)(2,1)} %grad_theirs.1), channel_id=1, source_target_pairs={{0,1},{1,0},{2,3},{3,2},{4,5},{5,4},{6,7},{7,6},{8,9},{9,8},{10,11... | collective-permute-start | bytes 3145736 | tf_op jit(solution)/shard_map/ppermute | solution.py:303
  62.8 20.7 %all-to-all-start.2 = ((bf16[64,16,128]{2,1,0:T(8,128)(2,1)}), bf16[64,16,128]{2,1,0:T(8,128)(2,1)S(1)}, u32[]{:S(2)}, u32[]{:S(2)}) async-start(bf16[64,16,128]{2,1,0:T(8,128)(2,1)} %total.1), calls=%async_computation.2 | async-start | bytes 524288 | tf_op jit(solution)/shard_map/all_to_all | solution.py:284
  71.0 17.7 %collective-permute-start.1 = (bf16[16,96,128]{2,1,0:T(8,128)(2,1)S(1)}, bf16[16,96,128]{2,1,0:T(8,128)(2,1)S(1)}, u32[]{:S(2)}, u32[]{:S(2)}) collective-permute-start(bf16[16,96,128]{2,1,0:T(8,128)(2,1)S(1)} %all_to_all.21.parts_here_ref.parts_ref), channel_id=1, source_target_pairs={{0,1},{1,0},{2,3},{3,2},{4,5},{5,4},{6,7},{7,6},{8,9},{9,8},{10,11... | collective-permute-start | bytes 1179656 | tf_op jit(solution)/shard_map/ppermute | solution.py:303
  83.5 6.3 %collective-permute-start.2 = (bf16[64,16,128]{2,1,0:T(8,128)(2,1)S(1)}, bf16[64,16,128]{2,1,0:T(8,128)(2,1)S(1)}, u32[]{:S(2)}, u32[]{:S(2)}) collective-permute-start(bf16[64,16,128]{2,1,0:T(8,128)(2,1)S(1)} %all-to-all-done.2.tiles_here_ref), channel_id=1, source_target_pairs={{0,1},{1,0},{2,3},{3,2},{4,5},{5,4},{6,7},{7,6},{8,9},{9,8},{10,11... | collective-permute-start | bytes 786440 | tf_op jit(solution)/shard_map/ppermute | solution.py:303
